TPU v7x, 32 devices: a whole 2x2x4 slice. The times are simulated.
32 devices in a mesh: runs: 2 (over y), row: 4 (over z), col: 2 (over x), sub: 2 (over core).
Axes of the slice: x: 2, y: 2, z: 4, core: 2. Of those that a mesh axis runs over, the one named last changes fastest.
Arguments:
- packed: bfloat16 [4, 2048, 256], P(('col', 'sub'), ('runs', 'row')), parts along dimension 1, may hold values from -6 to 6
- h_real: bfloat16 [8, 4, 128, 128], P('row'), may hold values from -0.25 to 0.25
- h_imag: bfloat16 [8, 4, 128, 128], P('row'), may hold values from -0.25 to 0.25
- h_cols: int32 [8, 4], P('row'), may hold values from 0 to 7, as said below
Outputs:
- evolved: float32 [4, 2048, 256], P(('col', 'sub'), ('runs', 'row')), parts along dimension 1
There are 2 independent parts, one for each index of `runs`. A program takes and returns all parts, laid end to end along the dimension named above; an argument that names none is the same for every part. Nothing has to cross between parts.
Inputs may be any that keep to these rules, and one draw needn't show every extreme that they name: h_cols[b, 0] = b, and h_cols[b, 1], h_cols[b, 2], h_cols[b, 3] are (b + e) mod 8 for three different e among -2, -1, 1, 2.
All inputs are finite; a program needn't handle non-finite values.
Results may differ from a plain program's by a relative error of at most 0.0027.
Values may be sent and summed in bfloat16 or wider, within the bound.
No kernel may reach another device: no remote copies, remote signals or barrier semaphores. Data moves between devices by JAX's collectives and lax.ppermute only.
A program may use at most 64 MiB of HBM per device.

v0:
```python
import jax
import jax.numpy as jnp
from jax import lax
from jax.sharding import PartitionSpec as P

TERMS = 3


step_size = 0.5


def extended(block, sides, width):
    for axis, dim in sides:
        count = lax.axis_size(axis)
        forward = [(i, i + 1) for i in range(count - 1)]
        forward.append((count - 1, 0))
        backward = [(target, source) for source, target in forward]
        low = lax.ppermute(
            lax.slice_in_dim(block, block.shape[dim] - width, None, axis=dim), axis, forward
        )
        high = lax.ppermute(lax.slice_in_dim(block, 0, width, axis=dim), axis, backward)
        block = jnp.concatenate([low, block, high], axis=dim)
    return block


def mirror(stacked):
    groups, rows_here, col_count = stacked.shape
    piece_count = lax.axis_size(("col", "sub"))
    band_count = lax.axis_size("row")
    piece_len = rows_here // piece_count
    split_rows = stacked.reshape(groups, piece_count, piece_len, col_count)
    arrived = lax.all_to_all(split_rows, ("col", "sub"), split_axis=1, concat_axis=1, tiled=True)
    turned = jnp.swapaxes(arrived.reshape(groups, rows_here, col_count), 1, 2).reshape(
        groups, band_count, piece_len, rows_here
    )
    landed = lax.all_to_all(turned, "row", split_axis=1, concat_axis=1, tiled=True)
    spread = landed.reshape(groups, band_count, piece_len, piece_count, piece_len)
    placed = jnp.transpose(spread, (0, 3, 2, 1, 4))
    return placed.reshape(groups, rows_here, col_count)


def body(packed, h_real, h_imag, h_cols):
    packed_here = packed.reshape(packed.shape[1], packed.shape[2])
    rows_here, col_count = packed_here.shape
    band_index = lax.axis_index("row")
    piece_index = lax.axis_index(("col", "sub"))
    piece_len = rows_here // lax.axis_size(("col", "sub"))
    flipped = mirror(packed_here[None])[0]
    row_ids = band_index * rows_here + jnp.arange(rows_here, dtype=jnp.int32)[:, None]
    col_local = jnp.arange(col_count, dtype=jnp.int32)[None, :]
    col_ids = col_local // piece_len * rows_here + piece_index * piece_len + col_local % piece_len
    upper_mask = row_ids <= col_ids
    real_part = jnp.where(upper_mask, packed_here, flipped)
    imag_part = jnp.where(
        row_ids > col_ids,
        packed_here,
        jnp.where(row_ids < col_ids, -flipped, jnp.zeros_like(flipped)),
    )
    current = jnp.stack([real_part, imag_part])
    summed = current.astype(jnp.float32)
    combined = jnp.stack([jnp.stack([h_imag, h_real], 2), jnp.stack([-h_real, h_imag], 2)])
    local_blocks = h_real.shape[0]
    block_len = h_real.shape[2]
    block_total = lax.axis_size("row") * local_blocks
    block_ids = band_index * local_blocks + jnp.arange(local_blocks, dtype=jnp.int32)[:, None]
    offsets = (h_cols - block_ids + 2) % block_total - 2
    starts = (
        (jnp.arange(local_blocks, dtype=jnp.int32)[:, None] + offsets + 2) * block_len
    ).reshape(-1)
    for term_index in range(1, TERMS + 1):
        padded = extended(current, (("row", 1),), 2 * block_len)
        sliced = jax.vmap(
            lambda row_start: lax.dynamic_slice_in_dim(padded, row_start, block_len, 1)
        )(starts)
        gathered = sliced.reshape(local_blocks, 4, 2, block_len, col_count)
        product = jnp.einsum(
            "obsgij,bsgjc->obic", combined, gathered, preferred_element_type=jnp.float32
        )
        generator = product.reshape(2, rows_here, col_count).astype(jnp.bfloat16)
        mirror_part = mirror(generator).astype(jnp.float32)
        own_part = generator.astype(jnp.float32)
        update = (
            step_size
            / term_index
            * jnp.stack([own_part[0] + mirror_part[0], own_part[1] - mirror_part[1]])
        )
        summed = summed + update
        current = update.astype(jnp.bfloat16)
    result = jnp.where(upper_mask, summed[0], summed[1])
    return result[None]


def solution(mesh):
    in_specs = (
        P(("col", "sub"), ("runs", "row"), None),
        P("row", None, None, None),
        P("row", None, None, None),
        P("row", None),
    )
    out_specs = P(("col", "sub"), ("runs", "row"), None)
    return jax.shard_map(body, mesh=mesh, in_specs=in_specs, out_specs=out_specs, check_vma=False)
```

profile of v0, /device:TPU:0, one launch (start us, length us, event | category | flops | bytes accessed | tf_op | source)
XLA Modules:
  0.0 156.5 jit_solution(1723708452518779441)
XLA Ops:
  0.0 4.3 %all-to-all-start = ((bf16[1,4,64,256]{3,2,0,1:T(8,128)(2,1)}), bf16[1,4,64,256]{3,2,0,1:T(8,128)(2,1)S(1)}, u32[]{:S(2)}, u32[]{:S(2)}) async-start(bf16[1,4,64,256]{3,2,0,1:T(8,128)(2,1)} %bitcast.116), calls=%async_computation | async-start | bytes 262144 | tf_op jit(solution)/shard_map/all_to_all | solution.py:32
  4.3 1.0 negate_bitcast_fusion
  5.4 3.6 %all-to-all-done = bf16[1,4,64,256]{3,2,0,1:T(8,128)(2,1)S(1)} async-done(((bf16[1,4,64,256]{3,2,0,1:T(8,128)(2,1)}), bf16[1,4,64,256]{3,2,0,1:T(8,128)(2,1)S(1)}, u32[]{:S(2)}, u32[]{:S(2)}) %all-to-all-start) | async-done | bytes 131104 | tf_op jit(solution)/shard_map/all_to_all | solution.py:32
  9.0 0.8 copy.115
  9.7 5.4 %all-to-all-start.1 = ((bf16[1,4,64,256]{3,2,0,1:T(8,128)(2,1)}), bf16[1,4,64,256]{3,2,0,1:T(8,128)(2,1)S(1)}, u32[]{:S(2)}, u32[]{:S(2)}) async-start(bf16[1,4,64,256]{3,2,0,1:T(8,128)(2,1)} %bitcast.4), calls=%async_computation.1 | async-start | bytes 262144 | tf_op jit(solution)/shard_map/all_to_all | solution.py:36
  15.2 5.8 %all-to-all-done.1 = bf16[1,4,64,256]{3,2,0,1:T(8,128)(2,1)S(1)} async-done(((bf16[1,4,64,256]{3,2,0,1:T(8,128)(2,1)}), bf16[1,4,64,256]{3,2,0,1:T(8,128)(2,1)S(1)}, u32[]{:S(2)}, u32[]{:S(2)}) %all-to-all-start.1) | async-done | bytes 131104 | tf_op jit(solution)/shard_map/all_to_all | solution.py:36
  21.6 2.4 %compare_select_fusion.1 = (bf16[1,256,256]{2,0,1:T(2,128)(2,1)S(1)}, bf16[1,256,256]{2,0,1:T(2,128)(2,1)S(1)}) fusion(bf16[1,256,256]{2,0,1:T(2,128)(2,1)S(1)} %squeeze_reshape.4, bf16[1,256,256]{2,1,0:T(8,128)(2,1)S(1)} %copy-done.9, s32[256]{0:T(256)S(1)} %get-tuple-element.21, s32[256]{0:T(256)S(1)} %get-tuple-element.22), kind=kLoop, calls=%fused_computation.13 | loop fusion | flops 458752 | bytes 526336 | tf_op jit(solution)/shard_map/jit(_where)/select_n | solution.py:53
  24.1 0.6 pad_maximum_fusion.7
  24.7 1.3 collective-permute-start
  26.0 2.6 %collective-permute-start.1 = (bf16[2,256,256]{2,0,1:T(2,128)(2,1)S(1)}, bf16[2,256,256]{2,0,1:T(2,128)(2,1)S(1)}, u32[]{:S(2)}, u32[]{:S(2)}) collective-permute-start(bf16[2,256,256]{2,0,1:T(2,128)(2,1)S(1)} %pad_maximum_fusion.7), channel_id=1, source_target_pairs={{4,0},{8,4},{12,8},{0,12},{5,1},{9,5},{13,9},{1,13},{6,2},{10,6},{... | collective-permute-start | bytes 786440 | tf_op jit(solution)/shard_map/ppermute | solution.py:21
  28.8 7.0 %collective-permute-done = bf16[2,256,256]{2,0,1:T(2,128)(2,1)S(1)} collective-permute-done((bf16[2,256,256]{2,0,1:T(2,128)(2,1)S(1)}, bf16[2,256,256]{2,0,1:T(2,128)(2,1)S(1)}, u32[]{:S(2)}, u32[]{:S(2)}) %collective-permute-start) | collective-permute-done | bytes 262176 | tf_op jit(solution)/shard_map/ppermute | solution.py:18
  35.8 1.9 %collective-permute-done.1 = bf16[2,256,256]{2,0,1:T(2,128)(2,1)S(1)} collective-permute-done((bf16[2,256,256]{2,0,1:T(2,128)(2,1)S(1)}, bf16[2,256,256]{2,0,1:T(2,128)(2,1)S(1)}, u32[]{:S(2)}, u32[]{:S(2)}) %collective-permute-start.1) | collective-permute-done | bytes 262176 | tf_op jit(solution)/shard_map/ppermute | solution.py:21
  37.6 1.1 pad_maximum_fusion.1
  38.7 2.7 %gather_fusion = bf16[8,2,128,256]{3,1,2,0:T(2,128)(2,1)S(1)} fusion(bf16[2,768,256]{2,0,1:T(2,128)(2,1)S(1)} %pad_maximum_fusion.1, s32[8]{0:T(128)S(1)} %fusion.22), kind=kCustom, calls=%fused_computation | custom fusion | bytes 2097248 | tf_op jit(solution)/shard_map/vmap()/gather | solution.py:73
  41.9 8.4 %all_to_all.40 = bf16[2,4,64,256]{3,2,0,1:T(8,128)(2,1)S(1)} all-to-all(bf16[2,4,64,256]{3,2,0,1:T(8,128)(2,1)S(1)} %copy.125), channel_id=1, replica_groups=mesh['runs'=2,'row'=4,'col'=2,'sub'=2] {'col','sub'}, dimensions={1} | all-to-all | bytes 524288 | tf_op jit(solution)/shard_map/all_to_all | solution.py:32
  50.5 0.7 copy.128
  51.2 3.4 %all-to-all-start.3 = ((bf16[2,4,64,256]{3,2,0,1:T(8,128)(2,1)}), bf16[2,4,64,256]{3,2,0,1:T(8,128)(2,1)S(1)}, u32[]{:S(2)}, u32[]{:S(2)}) async-start(bf16[2,4,64,256]{3,2,0,1:T(8,128)(2,1)} %copy.128), calls=%async_computation.3 | async-start | bytes 524288 | tf_op jit(solution)/shard_map/all_to_all | solution.py:36
  54.7 8.7 %all-to-all-done.3 = bf16[2,4,64,256]{3,2,0,1:T(8,128)(2,1)S(1)} async-done(((bf16[2,4,64,256]{3,2,0,1:T(8,128)(2,1)}), bf16[2,4,64,256]{3,2,0,1:T(8,128)(2,1)S(1)}, u32[]{:S(2)}, u32[]{:S(2)}) %all-to-all-start.3) | async-done | bytes 262176 | tf_op jit(solution)/shard_map/all_to_all | solution.py:36
  64.4 0.5 slice.81
  66.4 0.5 fusion.11
  67.2 3.7 %collective-permute-start.3 = (bf16[2,256,256]{2,0,1:T(2,128)(2,1)S(1)}, bf16[2,256,256]{2,0,1:T(2,128)(2,1)S(1)}, u32[]{:S(2)}, u32[]{:S(2)}) collective-permute-start(bf16[2,256,256]{2,0,1:T(2,128)(2,1)S(1)} %fusion.11), channel_id=1, source_target_pairs={{4,0},{8,4},{12,8},{0,12},{5,1},{9,5},{13,9},{1,13},{6,2},{10,6},{... | collective-permute-start | bytes 786440 | tf_op jit(solution)/shard_map/ppermute | solution.py:21
  70.8 7.2 %collective-permute-done.2 = bf16[2,256,256]{2,0,1:T(2,128)(2,1)S(1)} collective-permute-done((bf16[2,256,256]{2,0,1:T(2,128)(2,1)S(1)}, bf16[2,256,256]{2,0,1:T(2,128)(2,1)S(1)}, u32[]{:S(2)}, u32[]{:S(2)}) %collective-permute-start.2) | collective-permute-done | bytes 262176 | tf_op jit(solution)/shard_map/ppermute | solution.py:18
  78.1 1.2 collective-permute-done.3
  79.3 1.1 pad_maximum_fusion.2
  80.4 2.7 %gather_fusion.1 = bf16[8,2,128,256]{3,1,2,0:T(2,128)(2,1)S(1)} fusion(bf16[2,768,256]{2,0,1:T(2,128)(2,1)S(1)} %pad_maximum_fusion.2, s32[8]{0:T(128)S(1)} %fusion.22), kind=kCustom, calls=%fused_computation.1 | custom fusion | bytes 2097248 | tf_op jit(solution)/shard_map/vmap()/gather | solution.py:73
  83.1 1.5 fusion.4
  84.7 8.4 %all_to_all.41 = bf16[2,4,64,256]{3,2,0,1:T(8,128)(2,1)S(1)} all-to-all(bf16[2,4,64,256]{3,2,0,1:T(8,128)(2,1)S(1)} %copy.136), channel_id=1, replica_groups=mesh['runs'=2,'row'=4,'col'=2,'sub'=2] {'col','sub'}, dimensions={1} | all-to-all | bytes 524288 | tf_op jit(solution)/shard_map/all_to_all | solution.py:32
  93.2 0.7 copy.139
  94.0 3.4 %all-to-all-start.5 = ((bf16[2,4,64,256]{3,2,0,1:T(8,128)(2,1)}), bf16[2,4,64,256]{3,2,0,1:T(8,128)(2,1)S(1)}, u32[]{:S(2)}, u32[]{:S(2)}) async-start(bf16[2,4,64,256]{3,2,0,1:T(8,128)(2,1)} %copy.139), calls=%async_computation.5 | async-start | bytes 524288 | tf_op jit(solution)/shard_map/all_to_all | solution.py:36
  97.4 0.8 fusion.30
  98.2 8.0 %all-to-all-done.5 = bf16[2,4,64,256]{3,2,0,1:T(8,128)(2,1)S(1)} async-done(((bf16[2,4,64,256]{3,2,0,1:T(8,128)(2,1)}), bf16[2,4,64,256]{3,2,0,1:T(8,128)(2,1)S(1)}, u32[]{:S(2)}, u32[]{:S(2)}) %all-to-all-start.5) | async-done | bytes 262176 | tf_op jit(solution)/shard_map/all_to_all | solution.py:36
  107.1 0.5 slice.89
  109.3 0.5 fusion.10
  110.0 3.7 %collective-permute-start.5 = (bf16[2,256,256]{2,0,1:T(2,128)(2,1)S(1)}, bf16[2,256,256]{2,0,1:T(2,128)(2,1)S(1)}, u32[]{:S(2)}, u32[]{:S(2)}) collective-permute-start(bf16[2,256,256]{2,0,1:T(2,128)(2,1)S(1)} %fusion.10), channel_id=1, source_target_pairs={{4,0},{8,4},{12,8},{0,12},{5,1},{9,5},{13,9},{1,13},{6,2},{10,6},{... | collective-permute-start | bytes 786440 | tf_op jit(solution)/shard_map/ppermute | solution.py:21
  113.7 7.2 %collective-permute-done.4 = bf16[2,256,256]{2,0,1:T(2,128)(2,1)S(1)} collective-permute-done((bf16[2,256,256]{2,0,1:T(2,128)(2,1)S(1)}, bf16[2,256,256]{2,0,1:T(2,128)(2,1)S(1)}, u32[]{:S(2)}, u32[]{:S(2)}) %collective-permute-start.4) | collective-permute-done | bytes 262176 | tf_op jit(solution)/shard_map/ppermute | solution.py:18
  120.9 1.1 collective-permute-done.5
  122.0 1.1 pad_maximum_fusion.3
  123.1 2.7 %gather_fusion.2 = bf16[8,2,128,256]{3,1,2,0:T(2,128)(2,1)S(1)} fusion(bf16[2,768,256]{2,0,1:T(2,128)(2,1)S(1)} %pad_maximum_fusion.3, s32[8]{0:T(128)S(1)} %fusion.22), kind=kCustom, calls=%fused_computation.2 | custom fusion | bytes 2097248 | tf_op jit(solution)/shard_map/vmap()/gather | solution.py:73
  125.7 1.6 %fusion.3 = bf16[2,2,128,256]{3,2,0,1:T(8,128)(2,1)S(1)} fusion(bf16[2,4,2,128,256,1]{4,2,3,1,0,5:T(2,128)(2,1)S(1)} %bitcast.97, bf16[1,2,4,2,128,128]{5,4,2,3,0,1:T(8,128)(2,1)} %copy-done.8, bf16[1,2,4,2,128,128]{5,4,2,3,0,1:T(8,128)(2,1)} %copy-done.6), kind=kOutput, calls=%fused_computation.9 | convolution fusion | flops 270663680 | bytes 2359296 | tf_op jit(solution)/shard_map/obsgij,bsgjc->obic/dot_general | solution.py:76
  127.4 8.4 %all_to_all.42 = bf16[2,4,64,256]{3,2,0,1:T(8,128)(2,1)S(1)} all-to-all(bf16[2,4,64,256]{3,2,0,1:T(8,128)(2,1)S(1)} %copy.147), channel_id=1, replica_groups=mesh['runs'=2,'row'=4,'col'=2,'sub'=2] {'col','sub'}, dimensions={1} | all-to-all | bytes 524288 | tf_op jit(solution)/shard_map/all_to_all | solution.py:32
  136.0 0.7 copy.150
  136.8 3.6 %all-to-all-start.7 = ((bf16[2,4,64,256]{3,2,0,1:T(8,128)(2,1)}), bf16[2,4,64,256]{3,2,0,1:T(8,128)(2,1)S(1)}, u32[]{:S(2)}, u32[]{:S(2)}) async-start(bf16[2,4,64,256]{3,2,0,1:T(8,128)(2,1)} %copy.150), calls=%async_computation.7 | async-start | bytes 524288 | tf_op jit(solution)/shard_map/all_to_all | solution.py:36
  140.4 0.9 fusion.29
  141.2 7.7 %all-to-all-done.7 = bf16[2,4,64,256]{3,2,0,1:T(8,128)(2,1)S(1)} async-done(((bf16[2,4,64,256]{3,2,0,1:T(8,128)(2,1)}), bf16[2,4,64,256]{3,2,0,1:T(8,128)(2,1)S(1)}, u32[]{:S(2)}, u32[]{:S(2)}) %all-to-all-start.7) | async-done | bytes 262176 | tf_op jit(solution)/shard_map/all_to_all | solution.py:36
  149.4 0.9 fusion.26
  153.0 1.9 %fusion.9 = f32[2,256,256]{2,0,1:T(2,128)S(1)} fusion(f32[1,256,256]{2,0,1:T(1,128)S(1)} %copy_subtract_fusion, f32[1,256,256]{2,0,1:T(1,128)S(1)} %copy_add_fusion, f32[1,256,256]{2,0,1:T(1,128)S(1)} %copy_subtract_fusion.1, f32[1,256,256]{2,0,1:T(1,128)S(1)} %copy_add_fusion.1, f32[1,256,256]{2,0,1:T(1,128)S(1)} %copy_subtract_fusion.2, ...), kind=kLoop, calls=%fused_computation.28 | loop fusion | flops 1703936 | bytes 2359296 | tf_op jit(solution)/shard_map/add | solution.py:87
  154.9 0.9 compare_select_fusion
  155.8 0.7 copy.156
  (73 shorter events, 10.4 us)
Async XLA Ops:
  0.0 15.1 %copy-start.11 = (s32[2,4]{1,0:T(2,128)S(1)}, s32[2,4]{1,0:T(2,128)}, u32[]{:S(2)}) copy-start(s32[2,4]{1,0:T(2,128)} %param.7) | copy-start | bytes 100
  0.0 9.0 %all-to-all-start = ((bf16[1,4,64,256]{3,2,0,1:T(8,128)(2,1)}), bf16[1,4,64,256]{3,2,0,1:T(8,128)(2,1)S(1)}, u32[]{:S(2)}, u32[]{:S(2)}) async-start(bf16[1,4,64,256]{3,2,0,1:T(8,128)(2,1)} %bitcast.116), calls=%async_computation | async-start | bytes 262144 | tf_op jit(solution)/shard_map/all_to_all | solution.py:32
  5.3 16.3 %copy-start.9 = (bf16[1,256,256]{2,1,0:T(8,128)(2,1)S(1)}, bf16[1,256,256]{2,1,0:T(8,128)(2,1)}, u32[]{:S(2)}) copy-start(bf16[1,256,256]{2,1,0:T(8,128)(2,1)} %param.4) | copy-start | bytes 393220
  9.7 11.3 %all-to-all-start.1 = ((bf16[1,4,64,256]{3,2,0,1:T(8,128)(2,1)}), bf16[1,4,64,256]{3,2,0,1:T(8,128)(2,1)S(1)}, u32[]{:S(2)}, u32[]{:S(2)}) async-start(bf16[1,4,64,256]{3,2,0,1:T(8,128)(2,1)} %bitcast.4), calls=%async_computation.1 | async-start | bytes 262144 | tf_op jit(solution)/shard_map/all_to_all | solution.py:36
  21.4 7.1 %copy-start.1 = (bf16[2,4,128,128]{3,2,1,0:T(8,128)(2,1)S(1)}, bf16[2,4,128,128]{3,2,1,0:T(8,128)(2,1)}, u32[]{:S(2)}) copy-start(bf16[2,4,128,128]{3,2,1,0:T(8,128)(2,1)} %param.5) | copy-start | bytes 786436
  21.5 7.1 %copy-start.10 = (bf16[2,4,128,128]{3,2,1,0:T(8,128)(2,1)S(1)}, bf16[2,4,128,128]{3,2,1,0:T(8,128)(2,1)}, u32[]{:S(2)}) copy-start(bf16[2,4,128,128]{3,2,1,0:T(8,128)(2,1)} %param.6) | copy-start | bytes 786436
  24.7 11.1 %collective-permute-start = (bf16[2,256,256]{2,0,1:T(2,128)(2,1)S(1)}, bf16[2,256,256]{2,0,1:T(2,128)(2,1)S(1)}, u32[]{:S(2)}, u32[]{:S(2)}) collective-permute-start(bf16[2,256,256]{2,0,1:T(2,128)(2,1)S(1)} %pad_maximum_fusion.7), channel_id=1, source_target_pairs={{0,4},{4,8},{8,12},{12,0},{1,5},{5,9},{9,13},{13,1},{2,6},{6,10},{... | collective-permute-start | bytes 786440 | tf_op jit(solution)/shard_map/ppermute | solution.py:18
  26.0 11.6 %collective-permute-start.1 = (bf16[2,256,256]{2,0,1:T(2,128)(2,1)S(1)}, bf16[2,256,256]{2,0,1:T(2,128)(2,1)S(1)}, u32[]{:S(2)}, u32[]{:S(2)}) collective-permute-start(bf16[2,256,256]{2,0,1:T(2,128)(2,1)S(1)} %pad_maximum_fusion.7), channel_id=1, source_target_pairs={{4,0},{8,4},{12,8},{0,12},{5,1},{9,5},{13,9},{1,13},{6,2},{10,6},{... | collective-permute-start | bytes 786440 | tf_op jit(solution)/shard_map/ppermute | solution.py:21
  28.7 13.2 %copy-start.6 = (bf16[1,2,4,2,128,128]{5,4,2,3,0,1:T(8,128)(2,1)}, bf16[1,2,4,2,128,128]{5,4,2,3,0,1:T(8,128)(2,1)S(1)}, u32[]{:S(2)}) copy-start(bf16[1,2,4,2,128,128]{5,4,2,3,0,1:T(8,128)(2,1)S(1)} %get-tuple-element.19) | copy-start | bytes 1572868
  28.7 13.2 %copy-start.8 = (bf16[1,2,4,2,128,128]{5,4,2,3,0,1:T(8,128)(2,1)}, bf16[1,2,4,2,128,128]{5,4,2,3,0,1:T(8,128)(2,1)S(1)}, u32[]{:S(2)}) copy-start(bf16[1,2,4,2,128,128]{5,4,2,3,0,1:T(8,128)(2,1)S(1)} %get-tuple-element.20) | copy-start | bytes 1572868
  51.2 12.2 %all-to-all-start.3 = ((bf16[2,4,64,256]{3,2,0,1:T(8,128)(2,1)}), bf16[2,4,64,256]{3,2,0,1:T(8,128)(2,1)S(1)}, u32[]{:S(2)}, u32[]{:S(2)}) async-start(bf16[2,4,64,256]{3,2,0,1:T(8,128)(2,1)} %copy.128), calls=%async_computation.3 | async-start | bytes 524288 | tf_op jit(solution)/shard_map/all_to_all | solution.py:36
  67.0 11.1 %collective-permute-start.2 = (bf16[2,256,256]{2,0,1:T(2,128)(2,1)S(1)}, bf16[2,256,256]{2,0,1:T(2,128)(2,1)S(1)}, u32[]{:S(2)}, u32[]{:S(2)}) collective-permute-start(bf16[2,256,256]{2,0,1:T(2,128)(2,1)S(1)} %fusion.11), channel_id=1, source_target_pairs={{0,4},{4,8},{8,12},{12,0},{1,5},{5,9},{9,13},{13,1},{2,6},{6,10},{... | collective-permute-start | bytes 786440 | tf_op jit(solution)/shard_map/ppermute | solution.py:18
  67.2 12.1 %collective-permute-start.3 = (bf16[2,256,256]{2,0,1:T(2,128)(2,1)S(1)}, bf16[2,256,256]{2,0,1:T(2,128)(2,1)S(1)}, u32[]{:S(2)}, u32[]{:S(2)}) collective-permute-start(bf16[2,256,256]{2,0,1:T(2,128)(2,1)S(1)} %fusion.11), channel_id=1, source_target_pairs={{4,0},{8,4},{12,8},{0,12},{5,1},{9,5},{13,9},{1,13},{6,2},{10,6},{... | collective-permute-start | bytes 786440 | tf_op jit(solution)/shard_map/ppermute | solution.py:21
  80.4 2.7 %copy-start.7 = (bf16[1,2,4,2,128,128]{5,4,2,3,0,1:T(8,128)(2,1)S(1)}, bf16[1,2,4,2,128,128]{5,4,2,3,0,1:T(8,128)(2,1)}, u32[]{:S(2)}) copy-start(bf16[1,2,4,2,128,128]{5,4,2,3,0,1:T(8,128)(2,1)} %copy-done.6) | copy-start | bytes 1572868
  94.0 12.2 %all-to-all-start.5 = ((bf16[2,4,64,256]{3,2,0,1:T(8,128)(2,1)}), bf16[2,4,64,256]{3,2,0,1:T(8,128)(2,1)S(1)}, u32[]{:S(2)}, u32[]{:S(2)}) async-start(bf16[2,4,64,256]{3,2,0,1:T(8,128)(2,1)} %copy.139), calls=%async_computation.5 | async-start | bytes 524288 | tf_op jit(solution)/shard_map/all_to_all | solution.py:36
  107.6 1.0 copy-start.4
  107.9 1.0 copy-start.2
  109.8 11.1 %collective-permute-start.4 = (bf16[2,256,256]{2,0,1:T(2,128)(2,1)S(1)}, bf16[2,256,256]{2,0,1:T(2,128)(2,1)S(1)}, u32[]{:S(2)}, u32[]{:S(2)}) collective-permute-start(bf16[2,256,256]{2,0,1:T(2,128)(2,1)S(1)} %fusion.10), channel_id=1, source_target_pairs={{0,4},{4,8},{8,12},{12,0},{1,5},{5,9},{9,13},{13,1},{2,6},{6,10},{... | collective-permute-start | bytes 786440 | tf_op jit(solution)/shard_map/ppermute | solution.py:18
  110.0 11.9 %collective-permute-start.5 = (bf16[2,256,256]{2,0,1:T(2,128)(2,1)S(1)}, bf16[2,256,256]{2,0,1:T(2,128)(2,1)S(1)}, u32[]{:S(2)}, u32[]{:S(2)}) collective-permute-start(bf16[2,256,256]{2,0,1:T(2,128)(2,1)S(1)} %fusion.10), channel_id=1, source_target_pairs={{4,0},{8,4},{12,8},{0,12},{5,1},{9,5},{13,9},{1,13},{6,2},{10,6},{... | collective-permute-start | bytes 786440 | tf_op jit(solution)/shard_map/ppermute | solution.py:21
  136.8 12.2 %all-to-all-start.7 = ((bf16[2,4,64,256]{3,2,0,1:T(8,128)(2,1)}), bf16[2,4,64,256]{3,2,0,1:T(8,128)(2,1)S(1)}, u32[]{:S(2)}, u32[]{:S(2)}) async-start(bf16[2,4,64,256]{3,2,0,1:T(8,128)(2,1)} %copy.150), calls=%async_computation.7 | async-start | bytes 524288 | tf_op jit(solution)/shard_map/all_to_all | solution.py:36
  150.3 1.0 copy-start
  151.1 1.1 copy-start.5
  151.7 1.0 copy-start.3
where the time goes:
time: 157 us
  waiting for transfers between devices  59.4 us (38%)
  starting transfers between devices  31.8 us (20%)
  blocking collectives  25.3 us (16%)
  local copies, waits for them, and re-layouts  22.4 us (14%)
  other arithmetic  13.5 us (9%)
  matrix products  3.57 us (2%)
    all_to_all x4, waiting for transfers between devices, mirror(): lax.all_to_all(turned, 'row', split_axis=1, concat_axis=1, tiled=True)  30.2 us
    all_to_all x3, blocking collectives, mirror(): lax.all_to_all(split_rows, ('col', 'sub'), split_axis=1, concat_axis=1, t...  25.3 us
    ppermute x3, waiting for transfers between devices, extended(): lax.ppermute(lax.slice_in_dim(block, block.shape[dim] - width, None, axis...  21.4 us
    all_to_all x4, starting transfers between devices, mirror(): lax.all_to_all(turned, 'row', split_axis=1, concat_axis=1, tiled=True)  15.9 us
    ppermute x3, starting transfers between devices, extended(): lax.ppermute(lax.slice_in_dim(block, 0, width, axis=dim), axis, backward)  9.88 us
    gather x3, local copies, waits for them, and re-layouts, body(): lax.dynamic_slice_in_dim(padded, row_start, block_len, 1)  7.98 us
    all_to_all x1, starting transfers between devices, mirror(): lax.all_to_all(split_rows, ('col', 'sub'), split_axis=1, concat_axis=1, t...  4.34 us
    ppermute x3, waiting for transfers between devices, extended(): lax.ppermute(lax.slice_in_dim(block, 0, width, axis=dim), axis, backward)  4.15 us
  transfers between devices with their start and end apart: 11, of which 11 were waited for; matrix products, arithmetic and copies ran while one was open for 2% of the time, Pallas kernels for 0%

commit v1 on v0

--- a/solution.py
+++ b/solution.py
@@ -69,9 +69,12 @@
     ).reshape(-1)
     for term_index in range(1, TERMS + 1):
         padded = extended(current, (("row", 1),), 2 * block_len)
-        sliced = jax.vmap(
-            lambda row_start: lax.dynamic_slice_in_dim(padded, row_start, block_len, 1)
-        )(starts)
+        sliced = jnp.stack(
+            [
+                lax.dynamic_slice_in_dim(padded, starts[k], block_len, 1)
+                for k in range(starts.shape[0])
+            ]
+        )
         gathered = sliced.reshape(local_blocks, 4, 2, block_len, col_count)
         product = jnp.einsum(
             "obsgij,bsgjc->obic", combined, gathered, preferred_element_type=jnp.float32

time: 157 us -> 148 us (0.943)
  between operations: 0.56 us -> 15.6 us
  other arithmetic: 13.5 us -> 2.49 us
  local copies, waits for them, and re-layouts: 22.4 us -> 13.1 us
  starting transfers between devices: 31.8 us -> 27.9 us
  matrix products: 3.57 us -> 1.32 us
  waiting for transfers between devices: 59.4 us -> 61.6 us
    ppermute x3, waiting for transfers between devices: 4.15 us -> 15.7 us  [extended(): lax.ppermute(lax.slice_in_dim(block, 0, width, axis=dim), axis, backward)]
    gather x3 -> x0, local copies, waits for them, and re-layouts: 7.98 us -> none  [body(): lax.dynamic_slice_in_dim(padded, row_start, block_len, 1)]
    ppermute x3, waiting for transfers between devices: 21.4 us -> 15.9 us  [extended(): lax.ppermute(lax.slice_in_dim(block, block.shape[dim] - width, None, axis...]
    ppermute x3, starting transfers between devices: 9.88 us -> 4.85 us  [extended(): lax.ppermute(lax.slice_in_dim(block, 0, width, axis=dim), axis, backward)]
    all_to_all x4, waiting for transfers between devices: 30.2 us -> 26.3 us  [mirror(): lax.all_to_all(turned, 'row', split_axis=1, concat_axis=1, tiled=True)]
    concatenate x3, other arithmetic: 3.33 us -> 0.15 us  [extended(): block = jnp.concatenate([low, block, high], axis=dim)]
    select_n x1, other arithmetic: 2.45 us -> 0.16 us  [body(): real_part = jnp.where(upper_mask, packed_here, flipped)]
    dot_general x3, matrix products: 3.57 us -> 1.32 us  [body(): jnp.einsum('obsgij,bsgjc->obic', combined, gathered, preferred_element_ty...]
  transfers between devices with their start and end apart: 11 -> 11, of which waited for: 11 -> 10; matrix products, arithmetic and copies ran while one was open for 2% -> 1% of each run, Pallas kernels for 0% -> 0%
where the time goes in v1:
time: 148 us; the launch traced here: 147 us
  waiting for transfers between devices  61.6 us (42%)
  starting transfers between devices  27.9 us (19%)
  blocking collectives  25.3 us (17%)
  between operations  15.6 us (11%)
  local copies, waits for them, and re-layouts  13.1 us (9%)
  other arithmetic  2.49 us (2%)
    all_to_all x4, waiting for transfers between devices, mirror(): lax.all_to_all(turned, 'row', split_axis=1, concat_axis=1, tiled=True)  26.3 us
    all_to_all x3, blocking collectives, mirror(): lax.all_to_all(split_rows, ('col', 'sub'), split_axis=1, concat_axis=1, t...  25.3 us
    ppermute x3, waiting for transfers between devices, extended(): lax.ppermute(lax.slice_in_dim(block, block.shape[dim] - width, None, axis...  15.9 us
    ppermute x3, waiting for transfers between devices, extended(): lax.ppermute(lax.slice_in_dim(block, 0, width, axis=dim), axis, backward)  15.7 us
    all_to_all x4, starting transfers between devices, mirror(): lax.all_to_all(turned, 'row', split_axis=1, concat_axis=1, tiled=True)  15.6 us
    ppermute x3, starting transfers between devices, extended(): lax.ppermute(lax.slice_in_dim(block, 0, width, axis=dim), axis, backward)  4.85 us
    all_to_all x1, starting transfers between devices, mirror(): lax.all_to_all(split_rows, ('col', 'sub'), split_axis=1, concat_axis=1, t...  4.21 us
    all_to_all x1, waiting for transfers between devices, mirror(): lax.all_to_all(split_rows, ('col', 'sub'), split_axis=1, concat_axis=1, t...  3.75 us
  transfers between devices with their start and end apart: 11, of which 10 were waited for; matrix products, arithmetic and copies ran while one was open for 1% of the time, Pallas kernels for 0%

profile of v1, /device:TPU:0, one launch (start us, length us, event | category | flops | bytes accessed | tf_op | source)
XLA Modules:
  0.0 147.3 jit_solution(12437414779562573687)
XLA Ops:
  0.0 4.2 %all-to-all-start = ((bf16[1,4,64,256]{3,2,0,1:T(8,128)(2,1)}), bf16[1,4,64,256]{3,2,0,1:T(8,128)(2,1)S(1)}, u32[]{:S(2)}, u32[]{:S(2)}) async-start(bf16[1,4,64,256]{3,2,0,1:T(8,128)(2,1)} %bitcast.168), calls=%async_computation | async-start | bytes 262144 | tf_op jit(solution)/shard_map/all_to_all | solution.py:32
  4.2 0.8 add_multiply_fusion
  5.1 3.7 %all-to-all-done = bf16[1,4,64,256]{3,2,0,1:T(8,128)(2,1)S(1)} async-done(((bf16[1,4,64,256]{3,2,0,1:T(8,128)(2,1)}), bf16[1,4,64,256]{3,2,0,1:T(8,128)(2,1)S(1)}, u32[]{:S(2)}, u32[]{:S(2)}) %all-to-all-start) | async-done | bytes 131104 | tf_op jit(solution)/shard_map/all_to_all | solution.py:32
  8.8 0.8 copy.63
  9.6 5.4 %all-to-all-start.1 = ((bf16[1,4,64,256]{3,2,0,1:T(8,128)(2,1)}), bf16[1,4,64,256]{3,2,0,1:T(8,128)(2,1)S(1)}, u32[]{:S(2)}, u32[]{:S(2)}) async-start(bf16[1,4,64,256]{3,2,0,1:T(8,128)(2,1)} %bitcast.4), calls=%async_computation.1 | async-start | bytes 262144 | tf_op jit(solution)/shard_map/all_to_all | solution.py:36
  15.0 0.7 fusion.29
  31.4 2.1 %collective-permute-start = (bf16[2,256,256]{2,1,0:T(8,128)(2,1)S(1)}, bf16[2,256,256]{2,1,0:T(8,128)(2,1)S(1)}, u32[]{:S(2)}, u32[]{:S(2)}) collective-permute-start(bf16[2,256,256]{2,1,0:T(8,128)(2,1)S(1)} %pad_maximum_fusion.7), channel_id=1, source_target_pairs={{0,4},{4,8},{8,12},{12,0},{1,5},{5,9},{9,13},{13,1},{2,6},{6,10},{... | collective-permute-start | bytes 786440 | tf_op jit(solution)/shard_map/ppermute | solution.py:18
  33.5 1.9 %collective-permute-start.1 = (bf16[2,256,256]{2,1,0:T(8,128)(2,1)S(1)}, bf16[2,256,256]{2,1,0:T(8,128)(2,1)S(1)}, u32[]{:S(2)}, u32[]{:S(2)}) collective-permute-start(bf16[2,256,256]{2,1,0:T(8,128)(2,1)S(1)} %pad_maximum_fusion.7), channel_id=1, source_target_pairs={{4,0},{8,4},{12,8},{0,12},{5,1},{9,5},{13,9},{1,13},{6,2},{10,6},{... | collective-permute-start | bytes 786440 | tf_op jit(solution)/shard_map/ppermute | solution.py:21
  35.5 7.0 %collective-permute-done = bf16[2,256,256]{2,1,0:T(8,128)(2,1)S(1)} collective-permute-done((bf16[2,256,256]{2,1,0:T(8,128)(2,1)S(1)}, bf16[2,256,256]{2,1,0:T(8,128)(2,1)S(1)}, u32[]{:S(2)}, u32[]{:S(2)}) %collective-permute-start) | collective-permute-done | bytes 262176 | tf_op jit(solution)/shard_map/ppermute | solution.py:18
  42.6 3.4 %collective-permute-done.1 = bf16[2,256,256]{2,1,0:T(8,128)(2,1)S(1)} collective-permute-done((bf16[2,256,256]{2,1,0:T(8,128)(2,1)S(1)}, bf16[2,256,256]{2,1,0:T(8,128)(2,1)S(1)}, u32[]{:S(2)}, u32[]{:S(2)}) %collective-permute-start.1) | collective-permute-done | bytes 262176 | tf_op jit(solution)/shard_map/ppermute | solution.py:21
  46.4 0.4 fusion.5
  46.9 8.4 %all_to_all.40 = bf16[2,4,64,256]{3,2,0,1:T(8,128)(2,1)S(1)} all-to-all(bf16[2,4,64,256]{3,2,0,1:T(8,128)(2,1)S(1)} %copy.69), channel_id=1, replica_groups=mesh['runs'=2,'row'=4,'col'=2,'sub'=2] {'col','sub'}, dimensions={1} | all-to-all | bytes 524288 | tf_op jit(solution)/shard_map/all_to_all | solution.py:32
  55.5 0.7 copy.72
  56.2 3.4 %all-to-all-start.3 = ((bf16[2,4,64,256]{3,2,0,1:T(8,128)(2,1)}), bf16[2,4,64,256]{3,2,0,1:T(8,128)(2,1)S(1)}, u32[]{:S(2)}, u32[]{:S(2)}) async-start(bf16[2,4,64,256]{3,2,0,1:T(8,128)(2,1)} %copy.72), calls=%async_computation.3 | async-start | bytes 524288 | tf_op jit(solution)/shard_map/all_to_all | solution.py:36
  59.7 8.7 %all-to-all-done.3 = bf16[2,4,64,256]{3,2,0,1:T(8,128)(2,1)S(1)} async-done(((bf16[2,4,64,256]{3,2,0,1:T(8,128)(2,1)}), bf16[2,4,64,256]{3,2,0,1:T(8,128)(2,1)S(1)}, u32[]{:S(2)}, u32[]{:S(2)}) %all-to-all-start.3) | async-done | bytes 262176 | tf_op jit(solution)/shard_map/all_to_all | solution.py:36
  68.5 0.5 reshape.321
  69.0 0.3 copy.74
  69.4 0.3 slice.129
  69.7 0.3 copy.75
  70.1 0.3 slice.133
  70.5 1.5 collective-permute-start.3
  72.0 0.6 collective-permute-start.2
  72.6 6.2 %collective-permute-done.3 = bf16[2,256,256]{2,1,0:T(8,128)(2,1)S(1)} collective-permute-done((bf16[2,256,256]{2,1,0:T(8,128)(2,1)S(1)}, bf16[2,256,256]{2,1,0:T(8,128)(2,1)S(1)}, u32[]{:S(2)}, u32[]{:S(2)}) %collective-permute-start.3) | collective-permute-done | bytes 262176 | tf_op jit(solution)/shard_map/ppermute | solution.py:21
  78.8 4.4 %collective-permute-done.2 = bf16[2,256,256]{2,1,0:T(8,128)(2,1)S(1)} collective-permute-done((bf16[2,256,256]{2,1,0:T(8,128)(2,1)S(1)}, bf16[2,256,256]{2,1,0:T(8,128)(2,1)S(1)}, u32[]{:S(2)}, u32[]{:S(2)}) %collective-permute-start.2) | collective-permute-done | bytes 262176 | tf_op jit(solution)/shard_map/ppermute | solution.py:18
  83.6 0.6 copy-done.4
  84.2 0.4 fusion.4
  84.7 8.4 %all_to_all.41 = bf16[2,4,64,256]{3,2,0,1:T(8,128)(2,1)S(1)} all-to-all(bf16[2,4,64,256]{3,2,0,1:T(8,128)(2,1)S(1)} %copy.78), channel_id=1, replica_groups=mesh['runs'=2,'row'=4,'col'=2,'sub'=2] {'col','sub'}, dimensions={1} | all-to-all | bytes 524288 | tf_op jit(solution)/shard_map/all_to_all | solution.py:32
  93.3 0.7 copy.81
  94.0 3.4 %all-to-all-start.5 = ((bf16[2,4,64,256]{3,2,0,1:T(8,128)(2,1)}), bf16[2,4,64,256]{3,2,0,1:T(8,128)(2,1)S(1)}, u32[]{:S(2)}, u32[]{:S(2)}) async-start(bf16[2,4,64,256]{3,2,0,1:T(8,128)(2,1)} %copy.81), calls=%async_computation.5 | async-start | bytes 524288 | tf_op jit(solution)/shard_map/all_to_all | solution.py:36
  97.5 8.7 %all-to-all-done.5 = bf16[2,4,64,256]{3,2,0,1:T(8,128)(2,1)S(1)} async-done(((bf16[2,4,64,256]{3,2,0,1:T(8,128)(2,1)}), bf16[2,4,64,256]{3,2,0,1:T(8,128)(2,1)S(1)}, u32[]{:S(2)}, u32[]{:S(2)}) %all-to-all-start.5) | async-done | bytes 262176 | tf_op jit(solution)/shard_map/all_to_all | solution.py:36
  106.3 0.5 reshape.322
  106.8 0.3 copy.83
  107.5 0.3 copy.84
  108.3 1.5 %collective-permute-start.5 = (bf16[2,256,256]{2,1,0:T(8,128)(2,1)S(1)}, bf16[2,256,256]{2,1,0:T(8,128)(2,1)S(1)}, u32[]{:S(2)}, u32[]{:S(2)}) collective-permute-start(bf16[2,256,256]{2,1,0:T(8,128)(2,1)S(1)} %fusion.10), channel_id=1, source_target_pairs={{4,0},{8,4},{12,8},{0,12},{5,1},{9,5},{13,9},{1,13},{6,2},{10,6},{... | collective-permute-start | bytes 786440 | tf_op jit(solution)/shard_map/ppermute | solution.py:21
  109.9 0.6 collective-permute-start.4
  110.4 6.2 %collective-permute-done.5 = bf16[2,256,256]{2,1,0:T(8,128)(2,1)S(1)} collective-permute-done((bf16[2,256,256]{2,1,0:T(8,128)(2,1)S(1)}, bf16[2,256,256]{2,1,0:T(8,128)(2,1)S(1)}, u32[]{:S(2)}, u32[]{:S(2)}) %collective-permute-start.5) | collective-permute-done | bytes 262176 | tf_op jit(solution)/shard_map/ppermute | solution.py:21
  116.6 4.4 %collective-permute-done.4 = bf16[2,256,256]{2,1,0:T(8,128)(2,1)S(1)} collective-permute-done((bf16[2,256,256]{2,1,0:T(8,128)(2,1)S(1)}, bf16[2,256,256]{2,1,0:T(8,128)(2,1)S(1)}, u32[]{:S(2)}, u32[]{:S(2)}) %collective-permute-start.4) | collective-permute-done | bytes 262176 | tf_op jit(solution)/shard_map/ppermute | solution.py:18
  121.6 0.6 copy-done.2
  122.3 0.4 fusion.3
  122.8 8.4 %all_to_all.42 = bf16[2,4,64,256]{3,2,0,1:T(8,128)(2,1)S(1)} all-to-all(bf16[2,4,64,256]{3,2,0,1:T(8,128)(2,1)S(1)} %copy.87), channel_id=1, replica_groups=mesh['runs'=2,'row'=4,'col'=2,'sub'=2] {'col','sub'}, dimensions={1} | all-to-all | bytes 524288 | tf_op jit(solution)/shard_map/all_to_all | solution.py:32
  131.4 0.7 copy.90
  132.2 3.4 %all-to-all-start.7 = ((bf16[2,4,64,256]{3,2,0,1:T(8,128)(2,1)}), bf16[2,4,64,256]{3,2,0,1:T(8,128)(2,1)S(1)}, u32[]{:S(2)}, u32[]{:S(2)}) async-start(bf16[2,4,64,256]{3,2,0,1:T(8,128)(2,1)} %copy.90), calls=%async_computation.7 | async-start | bytes 524288 | tf_op jit(solution)/shard_map/all_to_all | solution.py:36
  135.6 8.7 %all-to-all-done.7 = bf16[2,4,64,256]{3,2,0,1:T(8,128)(2,1)S(1)} async-done(((bf16[2,4,64,256]{3,2,0,1:T(8,128)(2,1)}), bf16[2,4,64,256]{3,2,0,1:T(8,128)(2,1)S(1)}, u32[]{:S(2)}, u32[]{:S(2)}) %all-to-all-start.7) | async-done | bytes 262176 | tf_op jit(solution)/shard_map/all_to_all | solution.py:36
  144.4 0.5 reshape.323
  144.9 0.3 copy.92
  145.3 0.3 slice.145
  145.6 0.3 copy.93
  146.5 0.8 compare_select_fusion
  (85 shorter events, 4.8 us)
Async XLA Ops:
  0.0 8.8 %all-to-all-start = ((bf16[1,4,64,256]{3,2,0,1:T(8,128)(2,1)}), bf16[1,4,64,256]{3,2,0,1:T(8,128)(2,1)S(1)}, u32[]{:S(2)}, u32[]{:S(2)}) async-start(bf16[1,4,64,256]{3,2,0,1:T(8,128)(2,1)} %bitcast.168), calls=%async_computation | async-start | bytes 262144 | tf_op jit(solution)/shard_map/all_to_all | solution.py:32
  4.2 27.0 %copy-start.6 = (bf16[1,256,256]{2,1,0:T(8,128)(2,1)S(1)}, bf16[1,256,256]{2,1,0:T(8,128)(2,1)}, u32[]{:S(2)}) copy-start(bf16[1,256,256]{2,1,0:T(8,128)(2,1)} %param.4) | copy-start | bytes 393220
  9.6 21.0 %all-to-all-start.1 = ((bf16[1,4,64,256]{3,2,0,1:T(8,128)(2,1)}), bf16[1,4,64,256]{3,2,0,1:T(8,128)(2,1)S(1)}, u32[]{:S(2)}, u32[]{:S(2)}) async-start(bf16[1,4,64,256]{3,2,0,1:T(8,128)(2,1)} %bitcast.4), calls=%async_computation.1 | async-start | bytes 262144 | tf_op jit(solution)/shard_map/all_to_all | solution.py:36
  30.8 4.6 %copy-start = (bf16[2,4,128,128]{3,2,1,0:T(8,128)(2,1)S(1)}, bf16[2,4,128,128]{3,2,1,0:T(8,128)(2,1)}, u32[]{:S(2)}) copy-start(bf16[2,4,128,128]{3,2,1,0:T(8,128)(2,1)} %param.5) | copy-start | bytes 786436
  31.0 4.4 %copy-start.7 = (bf16[2,4,128,128]{3,2,1,0:T(8,128)(2,1)S(1)}, bf16[2,4,128,128]{3,2,1,0:T(8,128)(2,1)}, u32[]{:S(2)}) copy-start(bf16[2,4,128,128]{3,2,1,0:T(8,128)(2,1)} %param.6) | copy-start | bytes 786436
  31.4 11.1 %collective-permute-start = (bf16[2,256,256]{2,1,0:T(8,128)(2,1)S(1)}, bf16[2,256,256]{2,1,0:T(8,128)(2,1)S(1)}, u32[]{:S(2)}, u32[]{:S(2)}) collective-permute-start(bf16[2,256,256]{2,1,0:T(8,128)(2,1)S(1)} %pad_maximum_fusion.7), channel_id=1, source_target_pairs={{0,4},{4,8},{8,12},{12,0},{1,5},{5,9},{9,13},{13,1},{2,6},{6,10},{... | collective-permute-start | bytes 786440 | tf_op jit(solution)/shard_map/ppermute | solution.py:18
  33.5 12.5 %collective-permute-start.1 = (bf16[2,256,256]{2,1,0:T(8,128)(2,1)S(1)}, bf16[2,256,256]{2,1,0:T(8,128)(2,1)S(1)}, u32[]{:S(2)}, u32[]{:S(2)}) collective-permute-start(bf16[2,256,256]{2,1,0:T(8,128)(2,1)S(1)} %pad_maximum_fusion.7), channel_id=1, source_target_pairs={{4,0},{8,4},{12,8},{0,12},{5,1},{9,5},{13,9},{1,13},{6,2},{10,6},{... | collective-permute-start | bytes 786440 | tf_op jit(solution)/shard_map/ppermute | solution.py:21
  35.5 10.9 %copy-start.3 = (bf16[1,2,4,2,128,128]{5,4,2,3,0,1:T(8,128)(2,1)}, bf16[1,2,4,2,128,128]{5,4,2,3,0,1:T(8,128)(2,1)S(1)}, u32[]{:S(2)}) copy-start(bf16[1,2,4,2,128,128]{5,4,2,3,0,1:T(8,128)(2,1)S(1)} %get-tuple-element.20) | copy-start | bytes 1572868
  35.5 48.1 %copy-start.1 = (bf16[1,2,4,2,128,128]{5,4,2,3,0,1:T(8,128)(2,1)}, bf16[1,2,4,2,128,128]{5,4,2,3,0,1:T(8,128)(2,1)S(1)}, u32[]{:S(2)}) copy-start(bf16[1,2,4,2,128,128]{5,4,2,3,0,1:T(8,128)(2,1)S(1)} %get-tuple-element.19) | copy-start | bytes 1572868
  56.2 12.2 %all-to-all-start.3 = ((bf16[2,4,64,256]{3,2,0,1:T(8,128)(2,1)}), bf16[2,4,64,256]{3,2,0,1:T(8,128)(2,1)S(1)}, u32[]{:S(2)}, u32[]{:S(2)}) async-start(bf16[2,4,64,256]{3,2,0,1:T(8,128)(2,1)} %copy.72), calls=%async_computation.3 | async-start | bytes 524288 | tf_op jit(solution)/shard_map/all_to_all | solution.py:36
  70.5 8.2 %collective-permute-start.3 = (bf16[2,256,256]{2,1,0:T(8,128)(2,1)S(1)}, bf16[2,256,256]{2,1,0:T(8,128)(2,1)S(1)}, u32[]{:S(2)}, u32[]{:S(2)}) collective-permute-start(bf16[2,256,256]{2,1,0:T(8,128)(2,1)S(1)} %fusion.11), channel_id=1, source_target_pairs={{4,0},{8,4},{12,8},{0,12},{5,1},{9,5},{13,9},{1,13},{6,2},{10,6},{... | collective-permute-start | bytes 786440 | tf_op jit(solution)/shard_map/ppermute | solution.py:21
  72.0 11.1 %collective-permute-start.2 = (bf16[2,256,256]{2,1,0:T(8,128)(2,1)S(1)}, bf16[2,256,256]{2,1,0:T(8,128)(2,1)S(1)}, u32[]{:S(2)}, u32[]{:S(2)}) collective-permute-start(bf16[2,256,256]{2,1,0:T(8,128)(2,1)S(1)} %fusion.11), channel_id=1, source_target_pairs={{0,4},{4,8},{8,12},{12,0},{1,5},{5,9},{9,13},{13,1},{2,6},{6,10},{... | collective-permute-start | bytes 786440 | tf_op jit(solution)/shard_map/ppermute | solution.py:18
  83.2 1.0 copy-start.4
  94.0 12.2 %all-to-all-start.5 = ((bf16[2,4,64,256]{3,2,0,1:T(8,128)(2,1)}), bf16[2,4,64,256]{3,2,0,1:T(8,128)(2,1)S(1)}, u32[]{:S(2)}, u32[]{:S(2)}) async-start(bf16[2,4,64,256]{3,2,0,1:T(8,128)(2,1)} %copy.81), calls=%async_computation.5 | async-start | bytes 524288 | tf_op jit(solution)/shard_map/all_to_all | solution.py:36
  108.3 8.3 %collective-permute-start.5 = (bf16[2,256,256]{2,1,0:T(8,128)(2,1)S(1)}, bf16[2,256,256]{2,1,0:T(8,128)(2,1)S(1)}, u32[]{:S(2)}, u32[]{:S(2)}) collective-permute-start(bf16[2,256,256]{2,1,0:T(8,128)(2,1)S(1)} %fusion.10), channel_id=1, source_target_pairs={{4,0},{8,4},{12,8},{0,12},{5,1},{9,5},{13,9},{1,13},{6,2},{10,6},{... | collective-permute-start | bytes 786440 | tf_op jit(solution)/shard_map/ppermute | solution.py:21
  109.9 11.2 %collective-permute-start.4 = (bf16[2,256,256]{2,1,0:T(8,128)(2,1)S(1)}, bf16[2,256,256]{2,1,0:T(8,128)(2,1)S(1)}, u32[]{:S(2)}, u32[]{:S(2)}) collective-permute-start(bf16[2,256,256]{2,1,0:T(8,128)(2,1)S(1)} %fusion.10), channel_id=1, source_target_pairs={{0,4},{4,8},{8,12},{12,0},{1,5},{5,9},{9,13},{13,1},{2,6},{6,10},{... | collective-permute-start | bytes 786440 | tf_op jit(solution)/shard_map/ppermute | solution.py:18
  121.1 1.0 copy-start.2
  121.1 1.2 copy-start.5
  132.2 12.2 %all-to-all-start.7 = ((bf16[2,4,64,256]{3,2,0,1:T(8,128)(2,1)}), bf16[2,4,64,256]{3,2,0,1:T(8,128)(2,1)S(1)}, u32[]{:S(2)}, u32[]{:S(2)}) async-start(bf16[2,4,64,256]{3,2,0,1:T(8,128)(2,1)} %copy.90), calls=%async_computation.7 | async-start | bytes 524288 | tf_op jit(solution)/shard_map/all_to_all | solution.py:36

commit v2 on v1

--- a/solution.py
+++ b/solution.py
@@ -1,6 +1,10 @@
+import functools
+
 import jax
 import jax.numpy as jnp
 from jax import lax
+from jax.experimental import pallas as pl
+from jax.experimental.pallas import tpu as pltpu
 from jax.sharding import PartitionSpec as P
 
 TERMS = 3
@@ -39,7 +43,7 @@
     return placed.reshape(groups, rows_here, col_count)
 
 
-def body(packed, h_real, h_imag, h_cols):
+def banded_body(packed, h_real, h_imag, h_cols):
     packed_here = packed.reshape(packed.shape[1], packed.shape[2])
     rows_here, col_count = packed_here.shape
     band_index = lax.axis_index("row")
@@ -93,6 +97,275 @@
     return result[None]
 
 
+VMEM_BYTES = 56 * 2**20
+F32 = jnp.float32
+BF16 = jnp.bfloat16
+
+
+def exchange(block, axes, offset):
+    count = lax.axis_size(axes)
+    return lax.ppermute(block, axes, [(i, i ^ offset) for i in range(count)])
+
+
+def apply_a(a_ref, v_ref, k, bands, rows, skip):
+    order = bands * rows
+    slots = [m for m in range(bands) if not (skip and m == k ^ 2)]
+    row = slice(k * rows, (k + 1) * rows)
+    left = jnp.concatenate(
+        [a_ref[row, part * order + m * rows : part * order + (m + 1) * rows] for part in (0, 1) for m in slots],
+        axis=1,
+    )
+    right = jnp.concatenate(
+        [v_ref[part * order + m * rows : part * order + (m + 1) * rows, :] for part in (0, 1) for m in slots],
+        axis=0,
+    )
+    return jnp.dot(left, right, preferred_element_type=F32)
+
+
+def put_v(v_ref, k, value, bands, rows, cols):
+    order = bands * rows
+    low = value.astype(BF16)
+    v_ref[k * rows : (k + 1) * rows, :] = low
+    v_ref[order + k * rows : order + (k + 1) * rows, :] = jnp.concatenate(
+        [-low[:, cols:], low[:, :cols]], axis=1
+    )
+
+
+def powers_kernel(dims, ids, cols_ref, hr_ref, hi_ref, hg_ref, a_ref, d_ref, va, vb, csum):
+    bands, rows, cols, piece, local, count, block, per, skip = dims
+    order = bands * rows
+    r, q, me_plane, me_core = ids[0], ids[1], ids[2], ids[3]
+    a_ref[...] = jnp.zeros_like(a_ref)
+    for k in range(bands):
+        for b in range(local):
+            top = k * rows + b * block
+            for s in range(count):
+                column = cols_ref[k, b * count + s]
+                slot = lax.bitwise_xor(column // local, r)
+                place = pl.multiple_of((slot * local + column % local) * block, block)
+                for part in (0, 1):
+                    if k == 0:
+                        got = (hr_ref if part == 0 else hi_ref)[b, s]
+                    else:
+                        flat = (part * local + b) * count + s
+                        share, at = flat // per, flat % per
+                        got = hg_ref[
+                            lax.bitwise_xor(share % 2, me_core),
+                            lax.bitwise_xor(share // 2, me_plane),
+                            k - 1,
+                            at,
+                        ]
+                    if part == 0:
+                        a_ref[top : top + block, pl.ds(pl.multiple_of(place + order, block), block)] = got * -0.5
+                    else:
+                        a_ref[top : top + block, pl.ds(place, block)] = got * 0.5
+    row_iota = lax.broadcasted_iota(jnp.int32, (rows, cols), 0)
+    col_iota = lax.broadcasted_iota(jnp.int32, (rows, cols), 1)
+    for k in range(bands):
+        hit = (col_iota // piece == lax.bitwise_xor(r, k)) & (row_iota == q * piece + col_iota % piece)
+        sel = jnp.where(hit, 1.0, 0.0)
+        put_v(va, k, jnp.concatenate([sel, jnp.zeros_like(sel)], axis=1), bands, rows, cols)
+    wide = 2 * cols
+    for k in range(bands):
+        c1 = apply_a(a_ref, va, k, bands, rows, skip)
+        put_v(vb, k, c1, bands, rows, cols)
+        csum[k * rows : (k + 1) * rows, :] = c1
+        d_ref[k * rows : (k + 1) * rows, 2 * wide : 3 * wide] = (0.5 * c1).astype(BF16)
+    for k in range(bands):
+        c2 = apply_a(a_ref, vb, k, bands, rows, skip)
+        put_v(va, k, c2, bands, rows, cols)
+        both = csum[k * rows : (k + 1) * rows, :] + 0.5 * c2
+        csum[k * rows : (k + 1) * rows, :] = both
+        d_ref[k * rows : (k + 1) * rows, wide : 2 * wide] = both.astype(BF16)
+    for k in range(bands):
+        c3 = apply_a(a_ref, va, k, bands, rows, skip)
+        both = csum[k * rows : (k + 1) * rows, :] + c3 * (1.0 / 6.0)
+        d_ref[k * rows : (k + 1) * rows, 0:wide] = both.astype(BF16)
+
+
+def main_kernel(dims, ids, f0_ref, fg_ref, a_ref, d_ref, own_ref, keep_ref, send_ref, va, vb, vsum, right, left, outs):
+    bands, rows, cols, piece, local, count, block, per, skip = dims
+    pieces = rows // piece
+    r, q = ids[0], ids[1]
+    wide = 2 * cols
+    row_iota = lax.broadcasted_iota(jnp.int32, (rows, cols), 0)
+    col_iota = lax.broadcasted_iota(jnp.int32, (rows, cols), 1)
+    col_abs = col_iota // piece * rows + q * piece + col_iota % piece
+    depth = 4 * cols
+    t_re, t_im = 2 * depth, 3 * depth
+
+    def put_t(k, at, value):
+        low = value.astype(BF16)
+        right[k * rows : (k + 1) * rows, t_re + at * cols : t_re + (at + 1) * cols] = low[:, :cols]
+        right[k * rows : (k + 1) * rows, t_im + at * cols : t_im + (at + 1) * cols] = low[:, cols:]
+
+    for k in range(bands):
+        here = (f0_ref[...] if k == 0 else fg_ref[k - 1]).astype(F32)
+        row_abs = lax.bitwise_xor(r, k) * rows + row_iota
+        real = jnp.where(row_abs < col_abs, here, jnp.where(row_abs == col_abs, 0.5 * here, 0.0))
+        imag = jnp.where(row_abs > col_abs, here, 0.0)
+        value = jnp.concatenate([real, imag], axis=1)
+        put_v(va, k, value, bands, rows, cols)
+        put_t(k, 1, value)
+        hit = (col_iota // piece == lax.bitwise_xor(r, k)) & (row_iota == q * piece + col_iota % piece)
+        span = slice(k * rows, (k + 1) * rows)
+        right[span, 0:cols] = jnp.where(hit, 1.0, 0.0).astype(BF16)
+        right[span, depth : depth + cols] = jnp.zeros((rows, cols), BF16)
+        for m in range(3):
+            right[span, (m + 1) * cols : (m + 2) * cols] = d_ref[span, m * wide : m * wide + cols]
+            right[span, depth + (m + 1) * cols : depth + (m + 2) * cols] = d_ref[span, m * wide + cols : (m + 1) * wide]
+    for k in range(bands):
+        v1 = apply_a(a_ref, va, k, bands, rows, skip)
+        put_v(vb, k, v1, bands, rows, cols)
+        put_t(k, 2, v1)
+        vsum[k * rows : (k + 1) * rows, :] = v1
+    for k in range(bands):
+        v2 = apply_a(a_ref, vb, k, bands, rows, skip)
+        put_v(va, k, v2, bands, rows, cols)
+        put_t(k, 3, v2)
+        vsum[k * rows : (k + 1) * rows, :] += 0.5 * v2
+    for k in range(bands):
+        v3 = apply_a(a_ref, va, k, bands, rows, skip)
+        put_t(k, 0, vsum[k * rows : (k + 1) * rows, :] + v3 * (1.0 / 6.0))
+    own = slice(0, rows)
+    cr, ci = right[own, 0:depth], right[own, depth : 2 * depth]
+    tr, ti = right[own, 2 * depth : 3 * depth], right[own, 3 * depth : 4 * depth]
+    for n, value in enumerate((tr, ti, cr, ci)):
+        left[0, :, n * depth : (n + 1) * depth] = value
+    for n, value in enumerate((ti, -tr, ci, -cr)):
+        left[1, :, n * depth : (n + 1) * depth] = value
+    nt = (((1,), (1,)), ((), ()))
+
+    def against(which, k):
+        return lax.dot_general(left[which], right[k * rows : (k + 1) * rows, :], nt, preferred_element_type=F32)
+
+    outs[0] = jnp.where(row_iota <= col_iota[:, :rows], against(0, 0), against(1, 0))
+    for k in range(1, bands):
+        lower = (lax.bitwise_xor(r, k) < r).astype(jnp.int32)
+        outs[k] = against(lower, k)
+
+    def target(piece_index):
+        return jnp.concatenate(
+            [outs[lax.bitwise_xor(r, b)][:, piece_index * piece : (piece_index + 1) * piece] for b in range(bands)],
+            axis=1,
+        )
+
+    for p in range(pieces):
+        offset = lax.bitwise_xor(q, p)
+        value = target(p)
+
+        @pl.when(offset == 0)
+        def _():
+            own_ref[...] = value
+
+        @pl.when(offset == 2)
+        def _():
+            keep_ref[...] = value
+
+        @pl.when(offset % 2 == 1)
+        def _():
+            send_ref[offset // 2] = value.astype(BF16)
+
+
+def gathered_body(packed, h_real, h_imag, h_cols):
+    here = packed.reshape(packed.shape[1], packed.shape[2])
+    rows, cols = here.shape
+    bands = lax.axis_size("row")
+    piece = rows // lax.axis_size(("col", "sub"))
+    local, count, block = h_real.shape[0], h_real.shape[1], h_real.shape[2]
+    order = bands * rows
+    r = lax.axis_index("row")
+    q = lax.axis_index(("col", "sub"))
+    me_plane = lax.axis_index(("runs", "col"))
+    me_core = lax.axis_index("sub")
+    shares = lax.axis_size(("runs", "col", "sub"))
+    per = 2 * local * count // shares
+    skip = bands == 4 and local == 2
+    dims = (bands, rows, cols, piece, local, count, block, per, skip)
+    ids = jnp.stack([r, q, me_plane, me_core]).astype(jnp.int32)
+
+    all_h = jnp.stack([h_real, h_imag]).reshape(shares, per * block, block)
+    share = lax.dynamic_index_in_dim(all_h, me_plane * 2 + me_core, 0, keepdims=False)
+    col_row = jnp.pad(h_cols.reshape(1, -1).astype(BF16), ((0, 15), (0, block - local * count)))
+    message = jnp.concatenate([share, col_row], axis=0)
+    arrived = jnp.stack([exchange(message, "row", k) for k in range(1, bands)])
+    their_cols = arrived[:, per * block, : local * count].astype(jnp.int32)
+    all_cols = jnp.concatenate([h_cols.reshape(1, -1), their_cols], axis=0)
+    mine = arrived[:, : per * block, :]
+    plane = jnp.stack([mine] + [exchange(mine, ("runs", "col"), k) for k in range(1, shares // 2)])
+    both = jnp.stack([plane, exchange(plane, "sub", 1)])
+    both = both.reshape(2, shares // 2, bands - 1, per, block, block)
+    rest = jnp.stack([exchange(here, "row", k) for k in range(1, bands)])
+
+    smem = pl.BlockSpec(memory_space=pltpu.SMEM)
+    vmem = pl.BlockSpec(memory_space=pltpu.VMEM)
+    params = pltpu.CompilerParams(vmem_limit_bytes=VMEM_BYTES)
+    step = 2 * order * 2 * order * 2 * cols
+    a_big, d_all = pl.pallas_call(
+        functools.partial(powers_kernel, dims),
+        out_shape=(
+            jax.ShapeDtypeStruct((order, 2 * order), BF16),
+            jax.ShapeDtypeStruct((order, 6 * cols), BF16),
+        ),
+        in_specs=[smem, smem, vmem, vmem, vmem],
+        out_specs=(vmem, vmem),
+        scratch_shapes=[
+            pltpu.VMEM((2 * order, 2 * cols), BF16),
+            pltpu.VMEM((2 * order, 2 * cols), BF16),
+            pltpu.VMEM((order, 2 * cols), F32),
+        ],
+        compiler_params=params,
+        cost_estimate=pl.CostEstimate(flops=3 * step, bytes_accessed=10 * 2**20, transcendentals=0),
+        name="powers",
+    )(ids, all_cols, h_real, h_imag, both)
+    own, keep, send = pl.pallas_call(
+        functools.partial(main_kernel, dims),
+        out_shape=(
+            jax.ShapeDtypeStruct((rows, cols), F32),
+            jax.ShapeDtypeStruct((rows, cols), F32),
+            jax.ShapeDtypeStruct((2, rows, cols), BF16),
+        ),
+        in_specs=[smem, vmem, vmem, vmem, vmem],
+        out_specs=(vmem, vmem, vmem),
+        scratch_shapes=[
+            pltpu.VMEM((2 * order, 2 * cols), BF16),
+            pltpu.VMEM((2 * order, 2 * cols), BF16),
+            pltpu.VMEM((order, 2 * cols), F32),
+            pltpu.VMEM((order, 16 * cols), BF16),
+            pltpu.VMEM((2, rows, 16 * cols), BF16),
+            pltpu.VMEM((bands, rows, rows), F32),
+        ],
+        compiler_params=params,
+        cost_estimate=pl.CostEstimate(flops=6 * step, bytes_accessed=10 * 2**20, transcendentals=0),
+        name="main",
+    )(ids, here, rest, a_big, d_all)
+    swapped = exchange(send, "sub", 1)
+    across = exchange((keep + swapped[1].astype(F32)).astype(BF16), "col", 1)
+    total = here.astype(F32) + own + swapped[0].astype(F32) + across.astype(F32)
+    return total[None]
+
+
+def can_gather(mesh, local_packed, local_h):
+    bands = mesh.shape["row"]
+    rows, cols = local_packed[1], local_packed[2]
+    local, count, block = local_h[0], local_h[1], local_h[2]
+    shares = mesh.shape["runs"] * mesh.shape["col"] * mesh.shape["sub"]
+    return (
+        bands & (bands - 1) == 0
+        and mesh.shape["runs"] == mesh.shape["col"] == mesh.shape["sub"] == 2
+        and rows == cols == local * block
+        and (2 * local * count) % shares == 0
+        and local * count <= block
+        and 80 * bands * rows * bands * rows // 2 <= VMEM_BYTES
+    )
+
+
+def body(mesh, packed, h_real, h_imag, h_cols):
+    if can_gather(mesh, packed.shape, h_real.shape):
+        return gathered_body(packed, h_real, h_imag, h_cols)
+    return banded_body(packed, h_real, h_imag, h_cols)
+
+
 def solution(mesh):
     in_specs = (
         P(("col", "sub"), ("runs", "row"), None),
@@ -101,4 +374,6 @@
         P("row", None),
     )
     out_specs = P(("col", "sub"), ("runs", "row"), None)
-    return jax.shard_map(body, mesh=mesh, in_specs=in_specs, out_specs=out_specs, check_vma=False)
+    return jax.shard_map(
+        functools.partial(body, mesh), mesh=mesh, in_specs=in_specs, out_specs=out_specs, check_vma=False
+    )

time: 148 us -> 74.3 us (0.50)
  waiting for transfers between devices: 61.6 us -> 27.9 us
  blocking collectives: 25.3 us -> 0 us
  Pallas kernels: 0 us -> 23.2 us
  between operations: 15.6 us -> 0.07 us
  starting transfers between devices: 27.9 us -> 14.7 us
  local copies, waits for them, and re-layouts: 13.1 us -> 0.79 us
  other arithmetic: 2.49 us -> 7.45 us
    all_to_all x5 -> x0, waiting for transfers between devices: 30 us -> none  [the longest x4 26.3 us: mirror(): lax.all_to_all(turned, 'row', split_axis=1, concat_axis=1, tiled=True)]
    all_to_all x3 -> x0, blocking collectives: 25.3 us -> none  [mirror(): lax.all_to_all(split_rows, ('col', 'sub'), split_axis=1, concat_axis=1, t...]
    pallas_call x0 -> x2, Pallas kernels: none -> 23.2 us  [the longest x1 13.8 us: gathered_body(): pl.pallas_call(functools.partial(main_kernel, dims), out_shape=(jax.Shape...]
    all_to_all x5 -> x0, starting transfers between devices: 19.8 us -> none  [the longest x4 15.6 us: mirror(): lax.all_to_all(turned, 'row', split_axis=1, concat_axis=1, tiled=True)]
    ppermute x6 -> x12, starting transfers between devices: 8.1 us -> 14.7 us  [exchange(): return lax.ppermute(block, axes, [(i, i ^ offset) for i in range(count)])]
    slice x19 -> x0, local copies, waits for them, and re-layouts: 5.07 us -> none  [the longest x9 2.25 us: body(): mirror_part[0]]
    another operation x3 -> x7, other arithmetic: 0.14 us -> 4.14 us  [the longest x1 1.43 us: gathered_body(): both = jnp.stack([plane, exchange(plane, 'sub', 1)])]
    ppermute x6 -> x12, waiting for transfers between devices: 31.6 us -> 27.9 us  [exchange(): return lax.ppermute(block, axes, [(i, i ^ offset) for i in range(count)])]
  transfers between devices with their start and end apart: 11 -> 12, of which waited for: 10 -> 8; matrix products, arithmetic and copies ran while one was open for 1% -> 3% of each run, Pallas kernels for 0% -> 0%
where the time goes in v2:
time: 74.3 us; the launch traced here: 74.1 us
  waiting for transfers between devices  27.9 us (38%)
  Pallas kernels  23.2 us (31%)
  starting transfers between devices  14.7 us (20%)
  other arithmetic  7.45 us (10%)
  local copies, waits for them, and re-layouts  0.79 us (1%)
    ppermute x12, waiting for transfers between devices, exchange(): return lax.ppermute(block, axes, [(i, i ^ offset) for i in range(count)])  27.9 us
    ppermute x12, starting transfers between devices, exchange(): return lax.ppermute(block, axes, [(i, i ^ offset) for i in range(count)])  14.7 us
    pallas_call x1, Pallas kernels, gathered_body(): pl.pallas_call(functools.partial(main_kernel, dims), out_shape=(jax.Shape...  13.8 us
    pallas_call x1, Pallas kernels, gathered_body(): pl.pallas_call(functools.partial(powers_kernel, dims), out_shape=(jax.Sha...  9.4 us
    broadcast_in_dim x1, other arithmetic, gathered_body(): return total[None]  1.72 us
  transfers between devices with their start and end apart: 12, of which 8 were waited for; matrix products, arithmetic and copies ran while one was open for 3% of the time, Pallas kernels for 0%

profile of v2, /device:TPU:0, one launch (start us, length us, event | category | flops | bytes accessed | tf_op | source)
XLA Modules:
  0.0 74.1 jit_solution(6122432230511688286)
XLA Ops:
  0.0 0.8 %reshape.42 = s32[1,8]{1,0:T(1,128)S(1)} reshape(s32[2,4]{1,0:T(2,128)} %param.7) | data formatting | bytes 64 | tf_op jit(solution)/shard_map/reshape | solution.py:293
  0.8 1.1 %pad_maximum_fusion.2 = bf16[2,2,4,128,128]{4,3,2,1,0:T(8,128)(2,1)S(1)} fusion(bf16[1,2,4,128,128]{4,3,2,1,0:T(8,128)(2,1)} %bitcast.60, bf16[1,2,4,128,128]{4,3,2,1,0:T(8,128)(2,1)} %bitcast.61), kind=kLoop, calls=%fused_computation.2 | loop fusion | flops 262144 | bytes 1048576 | tf_op jit(solution)/shard_map/stack | solution.py:287
  1.8 0.0 copy-start
  1.9 3.1 %collective-permute-start.3 = (bf16[272,128]{1,0:T(8,128)(2,1)S(1)}, bf16[272,128]{1,0:T(8,128)(2,1)S(1)}, u32[]{:S(2)}, u32[]{:S(2)}) collective-permute-start(bf16[272,128]{1,0:T(8,128)(2,1)S(1)} %fusion.4), channel_id=1, source_target_pairs={{0,4},{4,0},{8,12},{12,8},{1,5},{5,1},{9,13},{13,9},{2,6},{6,2},{1... | collective-permute-start | bytes 208904 | tf_op jit(solution)/shard_map/ppermute | solution.py:107
  5.0 2.6 %collective-permute-start.4 = (bf16[272,128]{1,0:T(8,128)(2,1)S(1)}, bf16[272,128]{1,0:T(8,128)(2,1)S(1)}, u32[]{:S(2)}, u32[]{:S(2)}) collective-permute-start(bf16[272,128]{1,0:T(8,128)(2,1)S(1)} %fusion.4), channel_id=1, source_target_pairs={{0,8},{4,12},{8,0},{12,4},{1,9},{5,13},{9,1},{13,5},{2,10},{6,14},... | collective-permute-start | bytes 208904 | tf_op jit(solution)/shard_map/ppermute | solution.py:107
  7.6 0.0 collective-permute-start.5
  7.6 0.0 collective-permute-done.3
  7.6 4.9 %collective-permute-done.4 = bf16[272,128]{1,0:T(8,128)(2,1)S(1)} collective-permute-done((bf16[272,128]{1,0:T(8,128)(2,1)S(1)}, bf16[272,128]{1,0:T(8,128)(2,1)S(1)}, u32[]{:S(2)}, u32[]{:S(2)}) %collective-permute-start.4) | collective-permute-done | bytes 69664 | tf_op jit(solution)/shard_map/ppermute | solution.py:107
  12.5 1.3 %collective-permute-done.5 = bf16[272,128]{1,0:T(8,128)(2,1)S(1)} collective-permute-done((bf16[272,128]{1,0:T(8,128)(2,1)S(1)}, bf16[272,128]{1,0:T(8,128)(2,1)S(1)}, u32[]{:S(2)}, u32[]{:S(2)}) %collective-permute-start.5) | collective-permute-done | bytes 69664 | tf_op jit(solution)/shard_map/ppermute | solution.py:107
  13.8 1.6 %collective-permute-start.6 = (bf16[3,256,128]{2,1,0:T(8,128)(2,1)S(1)}, bf16[3,256,128]{2,1,0:T(8,128)(2,1)S(1)}, u32[]{:S(2)}, u32[]{:S(2)}) collective-permute-start(bf16[3,256,128]{2,1,0:T(8,128)(2,1)S(1)} %pad_maximum_fusion.4), channel_id=1, source_target_pairs={{0,2},{2,0},{16,18},{18,16},{1,3},{3,1},{17,19},{19,17},{4,6},{6,4... | collective-permute-start | bytes 589832 | tf_op jit(solution)/shard_map/ppermute | solution.py:107
  15.4 1.5 %collective-permute-start.7 = (bf16[3,256,128]{2,1,0:T(8,128)(2,1)S(1)}, bf16[3,256,128]{2,1,0:T(8,128)(2,1)S(1)}, u32[]{:S(2)}, u32[]{:S(2)}) collective-permute-start(bf16[3,256,128]{2,1,0:T(8,128)(2,1)S(1)} %pad_maximum_fusion.4), channel_id=1, source_target_pairs={{0,16},{2,18},{16,0},{18,2},{1,17},{3,19},{17,1},{19,3},{4,20},{6,... | collective-permute-start | bytes 589832 | tf_op jit(solution)/shard_map/ppermute | solution.py:107
  16.9 0.5 collective-permute-start.8
  17.4 3.7 %collective-permute-done.6 = bf16[3,256,128]{2,1,0:T(8,128)(2,1)S(1)} collective-permute-done((bf16[3,256,128]{2,1,0:T(8,128)(2,1)S(1)}, bf16[3,256,128]{2,1,0:T(8,128)(2,1)S(1)}, u32[]{:S(2)}, u32[]{:S(2)}) %collective-permute-start.6) | collective-permute-done | bytes 196640 | tf_op jit(solution)/shard_map/ppermute | solution.py:107
  21.1 3.4 %collective-permute-done.7 = bf16[3,256,128]{2,1,0:T(8,128)(2,1)S(1)} collective-permute-done((bf16[3,256,128]{2,1,0:T(8,128)(2,1)S(1)}, bf16[3,256,128]{2,1,0:T(8,128)(2,1)S(1)}, u32[]{:S(2)}, u32[]{:S(2)}) %collective-permute-start.7) | collective-permute-done | bytes 196640 | tf_op jit(solution)/shard_map/ppermute | solution.py:107
  24.5 0.0 collective-permute-done.8
  24.5 0.1 pad_maximum_fusion.1
  24.6 0.1 collective-permute-start.9
  24.6 0.0 copy-done
  24.7 1.1 %collective-permute-start = (bf16[256,256]{1,0:T(8,128)(2,1)S(1)}, bf16[256,256]{1,0:T(8,128)(2,1)S(1)}, u32[]{:S(2)}, u32[]{:S(2)}) collective-permute-start(bf16[256,256]{1,0:T(8,128)(2,1)S(1)} %bitcast.63), channel_id=1, source_target_pairs={{0,4},{4,0},{8,12},{12,8},{1,5},{5,1},{9,13},{13,9},{2,6},{6,2},{1... | collective-permute-start | bytes 393224 | tf_op jit(solution)/shard_map/ppermute | solution.py:107
  25.7 1.4 %collective-permute-start.1 = (bf16[256,256]{1,0:T(8,128)(2,1)S(1)}, bf16[256,256]{1,0:T(8,128)(2,1)S(1)}, u32[]{:S(2)}, u32[]{:S(2)}) collective-permute-start(bf16[256,256]{1,0:T(8,128)(2,1)S(1)} %bitcast.64), channel_id=1, source_target_pairs={{0,8},{4,12},{8,0},{12,4},{1,9},{5,13},{9,1},{13,5},{2,10},{6,14},... | collective-permute-start | bytes 393224 | tf_op jit(solution)/shard_map/ppermute | solution.py:107
  27.2 2.0 %collective-permute-start.2 = (bf16[256,256]{1,0:T(8,128)(2,1)S(1)}, bf16[256,256]{1,0:T(8,128)(2,1)S(1)}, u32[]{:S(2)}, u32[]{:S(2)}) collective-permute-start(bf16[256,256]{1,0:T(8,128)(2,1)S(1)} %bitcast.65), channel_id=1, source_target_pairs={{0,12},{4,8},{8,4},{12,0},{1,13},{5,9},{9,5},{13,1},{2,14},{6,10},... | collective-permute-start | bytes 393224 | tf_op jit(solution)/shard_map/ppermute | solution.py:107
  29.1 0.7 pad_add_fusion.1.ids
  29.8 0.6 pad_add_fusion.cols_ref
  30.4 2.7 %collective-permute-done = bf16[256,256]{1,0:T(8,128)(2,1)S(1)} collective-permute-done((bf16[256,256]{1,0:T(8,128)(2,1)S(1)}, bf16[256,256]{1,0:T(8,128)(2,1)S(1)}, u32[]{:S(2)}, u32[]{:S(2)}) %collective-permute-start) | collective-permute-done | bytes 131104 | tf_op jit(solution)/shard_map/ppermute | solution.py:107
  33.1 5.5 %collective-permute-done.1 = bf16[256,256]{1,0:T(8,128)(2,1)S(1)} collective-permute-done((bf16[256,256]{1,0:T(8,128)(2,1)S(1)}, bf16[256,256]{1,0:T(8,128)(2,1)S(1)}, u32[]{:S(2)}, u32[]{:S(2)}) %collective-permute-start.1) | collective-permute-done | bytes 131104 | tf_op jit(solution)/shard_map/ppermute | solution.py:107
  38.6 0.0 collective-permute-done.2
  38.6 0.8 %pad_maximum_fusion.3.fg_ref = bf16[3,256,256]{2,1,0:T(8,128)(2,1)} fusion(bf16[1,256,256]{2,1,0:T(8,128)(2,1)S(1)} %bitcast.68, bf16[1,256,256]{2,1,0:T(8,128)(2,1)S(1)} %bitcast.67, bf16[1,256,256]{2,1,0:T(8,128)(2,1)S(1)} %bitcast.66), kind=kLoop, calls=%fused_computation.3 | loop fusion | flops 393216 | bytes 786432 | tf_op jit(solution)/shard_map/stack | solution.py:298
  39.4 0.0 collective-permute-done.9
  39.5 1.4 %pad_maximum_fusion.hg_ref = bf16[2,4,3,2,128,128]{5,4,3,2,1,0:T(8,128)(2,1)} fusion(bf16[1,4,3,2,128,128]{5,4,3,2,1,0:T(8,128)(2,1)S(1)} %bitcast.49, bf16[1,1,3,2,128,128]{5,4,3,2,1,0:T(8,128)(2,1)S(1)} %bitcast.47, bf16[1,1,3,2,128,128]{5,4,3,2,1,0:T(8,128)(2,1)S(1)} %bitcast.45, bf16[1,1,3,2,128,128]{5,4,3,2,1,0:T(8,128)(2,1)S(1)} %bitcast.43, ...), kind=kLoop, calls=%fused_computation | loop fusion | flops 3145728 | bytes 3145728 | tf_op jit(solution)/shard_map/stack | solution.py:296
  40.9 9.4 %powers.1 = (bf16[1024,2048]{1,0:T(8,128)(2,1)}, bf16[1024,1536]{1,0:T(8,128)(2,1)}) custom-call(s32[4]{0:T(128)} %pad_add_fusion.1.ids, s32[4,8]{1,0:T(4,128)} %pad_add_fusion.cols_ref, bf16[2,4,128,128]{3,2,1,0:T(8,128)(2,1)} %hr_ref.1, bf16[2,4,128,128]{3,2,1,0:T(8,128)(2,1)} %hi_ref.1, bf16[2,4,3,2,128,128]{5,4,3,2,1,0:T(8,128)(2,1)} %pad_maximum_fusion.hg_ref), custom_call_target="tpu_custom_call" | custom-call | flops 6442450944 | bytes 10485760 | tf_op jit(solution)/shard_map/powers/pallas_call | solution.py:304
  50.3 0.0 copy-start.1
  50.3 13.8 %main.1 = (f32[256,256]{1,0:T(8,128)}, f32[256,256]{1,0:T(8,128)}, bf16[2,256,256]{2,1,0:T(8,128)(2,1)}) custom-call(s32[4]{0:T(128)} %pad_add_fusion.1.ids, bf16[256,256]{1,0:T(8,128)(2,1)} %bitcast.62, bf16[3,256,256]{2,1,0:T(8,128)(2,1)} %pad_maximum_fusion.3.fg_ref, bf16[1024,2048]{1,0:T(8,128)(2,1)} %get-tuple-element.10.a_ref, ...), custom_call_target="tpu_custom_call" | custom-call | flops 12884901888 | bytes 10485760 | tf_op jit(solution)/shard_map/main/pallas_call | solution.py:321
  64.0 0.0 collective-permute-start.10
  64.0 1.7 %collective-permute-done.10 = bf16[2,256,256]{2,1,0:T(8,128)(2,1)S(1)} collective-permute-done((bf16[2,256,256]{2,1,0:T(8,128)(2,1)}, bf16[2,256,256]{2,1,0:T(8,128)(2,1)S(1)}, u32[]{:S(2)}, u32[]{:S(2)}) %collective-permute-start.10) | collective-permute-done | bytes 262176 | tf_op jit(solution)/shard_map/ppermute | solution.py:107
  65.8 1.0 %fusion = bf16[256,256]{1,0:T(8,128)(2,1)S(1)} fusion(f32[256,256]{1,0:T(8,128)} %get-tuple-element.14, bf16[2,256,256]{2,1,0:T(8,128)(2,1)S(1)} %collective-permute-done.10), kind=kLoop, calls=%fused_computation.5 | loop fusion | flops 196608 | bytes 524288 | tf_op jit(solution)/shard_map/convert_element_type | solution.py:343
  66.8 0.9 %collective-permute-start.11 = (bf16[256,256]{1,0:T(8,128)(2,1)S(1)}, bf16[256,256]{1,0:T(8,128)(2,1)S(1)}, u32[]{:S(2)}, u32[]{:S(2)}) collective-permute-start(bf16[256,256]{1,0:T(8,128)(2,1)S(1)} %fusion), channel_id=1, source_target_pairs={{0,2},{2,0},{1,3},{3,1},{4,6},{6,4},{5,7},{7,5},{8,10},{10,8},{9,1... | collective-permute-start | bytes 393224 | tf_op jit(solution)/shard_map/ppermute | solution.py:107
  67.7 4.7 %collective-permute-done.11 = bf16[256,256]{1,0:T(8,128)(2,1)S(1)} collective-permute-done((bf16[256,256]{1,0:T(8,128)(2,1)S(1)}, bf16[256,256]{1,0:T(8,128)(2,1)S(1)}, u32[]{:S(2)}, u32[]{:S(2)}) %collective-permute-start.11) | collective-permute-done | bytes 131104 | tf_op jit(solution)/shard_map/ppermute | solution.py:107
  72.4 0.0 copy-done.1
  72.4 1.7 %fusion.2 = f32[1,256,256]{2,1,0:T(8,128)} fusion(bf16[256,256]{1,0:T(8,128)(2,1)S(1)} %collective-permute-done.11, f32[256,256]{1,0:T(8,128)} %get-tuple-element.12, bf16[2,256,256]{2,1,0:T(8,128)(2,1)S(1)} %collective-permute-done.10, bf16[1,256,256]{2,1,0:T(8,128)(2,1)S(1)} %copy-done.1), kind=kLoop, calls=%fused_computation.8 | loop fusion | flops 393216 | bytes 917504 | tf_op jit(solution)/shard_map/broadcast_in_dim | solution.py:345
  (7 shorter events, 0.1 us)
Async XLA Ops:
  1.8 22.8 %copy-start = (bf16[1,256,256]{2,1,0:T(8,128)(2,1)S(1)}, bf16[1,256,256]{2,1,0:T(8,128)(2,1)}, u32[]{:S(2)}) copy-start(bf16[1,256,256]{2,1,0:T(8,128)(2,1)} %param.4) | copy-start | bytes 393220
  1.9 5.7 %collective-permute-start.3 = (bf16[272,128]{1,0:T(8,128)(2,1)S(1)}, bf16[272,128]{1,0:T(8,128)(2,1)S(1)}, u32[]{:S(2)}, u32[]{:S(2)}) collective-permute-start(bf16[272,128]{1,0:T(8,128)(2,1)S(1)} %fusion.4), channel_id=1, source_target_pairs={{0,4},{4,0},{8,12},{12,8},{1,5},{5,1},{9,13},{13,9},{2,6},{6,2},{1... | collective-permute-start | bytes 208904 | tf_op jit(solution)/shard_map/ppermute | solution.py:107
  5.0 7.5 %collective-permute-start.4 = (bf16[272,128]{1,0:T(8,128)(2,1)S(1)}, bf16[272,128]{1,0:T(8,128)(2,1)S(1)}, u32[]{:S(2)}, u32[]{:S(2)}) collective-permute-start(bf16[272,128]{1,0:T(8,128)(2,1)S(1)} %fusion.4), channel_id=1, source_target_pairs={{0,8},{4,12},{8,0},{12,4},{1,9},{5,13},{9,1},{13,5},{2,10},{6,14},... | collective-permute-start | bytes 208904 | tf_op jit(solution)/shard_map/ppermute | solution.py:107
  7.6 6.2 %collective-permute-start.5 = (bf16[272,128]{1,0:T(8,128)(2,1)S(1)}, bf16[272,128]{1,0:T(8,128)(2,1)S(1)}, u32[]{:S(2)}, u32[]{:S(2)}) collective-permute-start(bf16[272,128]{1,0:T(8,128)(2,1)S(1)} %fusion.4), channel_id=1, source_target_pairs={{0,12},{4,8},{8,4},{12,0},{1,13},{5,9},{9,5},{13,1},{2,14},{6,10},... | collective-permute-start | bytes 208904 | tf_op jit(solution)/shard_map/ppermute | solution.py:107
  13.8 7.3 %collective-permute-start.6 = (bf16[3,256,128]{2,1,0:T(8,128)(2,1)S(1)}, bf16[3,256,128]{2,1,0:T(8,128)(2,1)S(1)}, u32[]{:S(2)}, u32[]{:S(2)}) collective-permute-start(bf16[3,256,128]{2,1,0:T(8,128)(2,1)S(1)} %pad_maximum_fusion.4), channel_id=1, source_target_pairs={{0,2},{2,0},{16,18},{18,16},{1,3},{3,1},{17,19},{19,17},{4,6},{6,4... | collective-permute-start | bytes 589832 | tf_op jit(solution)/shard_map/ppermute | solution.py:107
  15.4 9.1 %collective-permute-start.7 = (bf16[3,256,128]{2,1,0:T(8,128)(2,1)S(1)}, bf16[3,256,128]{2,1,0:T(8,128)(2,1)S(1)}, u32[]{:S(2)}, u32[]{:S(2)}) collective-permute-start(bf16[3,256,128]{2,1,0:T(8,128)(2,1)S(1)} %pad_maximum_fusion.4), channel_id=1, source_target_pairs={{0,16},{2,18},{16,0},{18,2},{1,17},{3,19},{17,1},{19,3},{4,20},{6,... | collective-permute-start | bytes 589832 | tf_op jit(solution)/shard_map/ppermute | solution.py:107
  16.9 7.6 %collective-permute-start.8 = (bf16[3,256,128]{2,1,0:T(8,128)(2,1)S(1)}, bf16[3,256,128]{2,1,0:T(8,128)(2,1)S(1)}, u32[]{:S(2)}, u32[]{:S(2)}) collective-permute-start(bf16[3,256,128]{2,1,0:T(8,128)(2,1)S(1)} %pad_maximum_fusion.4), channel_id=1, source_target_pairs={{0,18},{2,16},{16,2},{18,0},{1,19},{3,17},{17,3},{19,1},{4,22},{6,... | collective-permute-start | bytes 589832 | tf_op jit(solution)/shard_map/ppermute | solution.py:107
  24.6 14.9 %collective-permute-start.9 = (bf16[4,3,256,128]{3,2,1,0:T(8,128)(2,1)S(1)}, bf16[4,3,256,128]{3,2,1,0:T(8,128)(2,1)S(1)}, u32[]{:S(2)}, u32[]{:S(2)}) collective-permute-start(bf16[4,3,256,128]{3,2,1,0:T(8,128)(2,1)S(1)} %pad_maximum_fusion.1), channel_id=1, source_target_pairs={{0,1},{1,0},{2,3},{3,2},{4,5},{5,4},{6,7},{7,6},{8,9},{9,8},{10,11... | collective-permute-start | bytes 2359304 | tf_op jit(solution)/shard_map/ppermute | solution.py:107
  24.7 8.4 %collective-permute-start = (bf16[256,256]{1,0:T(8,128)(2,1)S(1)}, bf16[256,256]{1,0:T(8,128)(2,1)S(1)}, u32[]{:S(2)}, u32[]{:S(2)}) collective-permute-start(bf16[256,256]{1,0:T(8,128)(2,1)S(1)} %bitcast.63), channel_id=1, source_target_pairs={{0,4},{4,0},{8,12},{12,8},{1,5},{5,1},{9,13},{13,9},{2,6},{6,2},{1... | collective-permute-start | bytes 393224 | tf_op jit(solution)/shard_map/ppermute | solution.py:107
  25.7 12.9 %collective-permute-start.1 = (bf16[256,256]{1,0:T(8,128)(2,1)S(1)}, bf16[256,256]{1,0:T(8,128)(2,1)S(1)}, u32[]{:S(2)}, u32[]{:S(2)}) collective-permute-start(bf16[256,256]{1,0:T(8,128)(2,1)S(1)} %bitcast.64), channel_id=1, source_target_pairs={{0,8},{4,12},{8,0},{12,4},{1,9},{5,13},{9,1},{13,5},{2,10},{6,14},... | collective-permute-start | bytes 393224 | tf_op jit(solution)/shard_map/ppermute | solution.py:107
  27.2 11.5 %collective-permute-start.2 = (bf16[256,256]{1,0:T(8,128)(2,1)S(1)}, bf16[256,256]{1,0:T(8,128)(2,1)S(1)}, u32[]{:S(2)}, u32[]{:S(2)}) collective-permute-start(bf16[256,256]{1,0:T(8,128)(2,1)S(1)} %bitcast.65), channel_id=1, source_target_pairs={{0,12},{4,8},{8,4},{12,0},{1,13},{5,9},{9,5},{13,1},{2,14},{6,10},... | collective-permute-start | bytes 393224 | tf_op jit(solution)/shard_map/ppermute | solution.py:107
  50.3 22.1 %copy-start.1 = (bf16[1,256,256]{2,1,0:T(8,128)(2,1)S(1)}, bf16[1,256,256]{2,1,0:T(8,128)(2,1)}, u32[]{:S(2)}) copy-start(bf16[1,256,256]{2,1,0:T(8,128)(2,1)} %param.4) | copy-start | bytes 393220
  64.0 1.7 %collective-permute-start.10 = (bf16[2,256,256]{2,1,0:T(8,128)(2,1)}, bf16[2,256,256]{2,1,0:T(8,128)(2,1)S(1)}, u32[]{:S(2)}, u32[]{:S(2)}) collective-permute-start(bf16[2,256,256]{2,1,0:T(8,128)(2,1)} %get-tuple-element.13), channel_id=1, source_target_pairs={{0,1},{1,0},{2,3},{3,2},{4,5},{5,4},{6,7},{7,6},{8,9},{9,8},{10,11... | collective-permute-start | bytes 786440 | tf_op jit(solution)/shard_map/ppermute | solution.py:107
  66.8 5.6 %collective-permute-start.11 = (bf16[256,256]{1,0:T(8,128)(2,1)S(1)}, bf16[256,256]{1,0:T(8,128)(2,1)S(1)}, u32[]{:S(2)}, u32[]{:S(2)}) collective-permute-start(bf16[256,256]{1,0:T(8,128)(2,1)S(1)} %fusion), channel_id=1, source_target_pairs={{0,2},{2,0},{1,3},{3,1},{4,6},{6,4},{5,7},{7,5},{8,10},{10,8},{9,1... | collective-permute-start | bytes 393224 | tf_op jit(solution)/shard_map/ppermute | solution.py:107

commit v3 on v2

--- a/solution.py
+++ b/solution.py
@@ -98,6 +98,8 @@
 
 
 VMEM_BYTES = 56 * 2**20
+POWERS_VMEM = 22 * 2**20
+MAIN_VMEM = 30 * 2**20
 F32 = jnp.float32
 BF16 = jnp.bfloat16
 
@@ -131,89 +133,109 @@
     )
 
 
-def powers_kernel(dims, ids, cols_ref, hr_ref, hi_ref, hg_ref, a_ref, d_ref, va, vb, csum):
+def place_blocks(dims, r, me_plane, facts, slots, find, a_ref):
     bands, rows, cols, piece, local, count, block, per, skip = dims
     order = bands * rows
-    r, q, me_plane, me_core = ids[0], ids[1], ids[2], ids[3]
-    a_ref[...] = jnp.zeros_like(a_ref)
-    for k in range(bands):
+    for k in slots:
         for b in range(local):
             top = k * rows + b * block
             for s in range(count):
-                column = cols_ref[k, b * count + s]
+                column = facts[4 + k * local * count + b * count + s]
                 slot = lax.bitwise_xor(column // local, r)
                 place = pl.multiple_of((slot * local + column % local) * block, block)
-                for part in (0, 1):
-                    if k == 0:
-                        got = (hr_ref if part == 0 else hi_ref)[b, s]
-                    else:
-                        flat = (part * local + b) * count + s
-                        share, at = flat // per, flat % per
-                        got = hg_ref[
-                            lax.bitwise_xor(share % 2, me_core),
-                            lax.bitwise_xor(share // 2, me_plane),
-                            k - 1,
-                            at,
-                        ]
-                    if part == 0:
-                        a_ref[top : top + block, pl.ds(pl.multiple_of(place + order, block), block)] = got * -0.5
-                    else:
-                        a_ref[top : top + block, pl.ds(place, block)] = got * 0.5
+                imag = pl.multiple_of(place + order, block)
+                a_ref[top : top + block, pl.ds(place, block)] = find(k, 1, b, s) * 0.5
+                a_ref[top : top + block, pl.ds(imag, block)] = find(k, 0, b, s) * -0.5
+
+
+def powers_kernel(dims, facts, hr_ref, hi_ref, near_ref, far_ref, a_ref, c_ref, va, vb, csum):
+    bands, rows, cols, piece, local, count, block, per, skip = dims
+    r, q, me_plane, me_core = facts[0], facts[1], facts[2], facts[3]
+    a_ref[...] = jnp.zeros_like(a_ref)
+    place_blocks(
+        dims, r, me_plane, facts, [0], lambda k, part, b, s: (hi_ref if part else hr_ref)[b, s], a_ref
+    )
+
+    def from_core(refs):
+        def find(k, part, b, s):
+            flat = (part * local + b) * count + s
+            share, at = flat // per, flat % per
+            return refs[share % 2][lax.bitwise_xor(share // 2, me_plane), k - 1, at]
+
+        place_blocks(dims, r, me_plane, facts, list(range(1, bands)), find, a_ref)
+
+    @pl.when(me_core == 0)
+    def _():
+        from_core((near_ref, far_ref))
+
+    @pl.when(me_core == 1)
+    def _():
+        from_core((far_ref, near_ref))
+
     row_iota = lax.broadcasted_iota(jnp.int32, (rows, cols), 0)
     col_iota = lax.broadcasted_iota(jnp.int32, (rows, cols), 1)
     for k in range(bands):
         hit = (col_iota // piece == lax.bitwise_xor(r, k)) & (row_iota == q * piece + col_iota % piece)
-        sel = jnp.where(hit, 1.0, 0.0)
-        put_v(va, k, jnp.concatenate([sel, jnp.zeros_like(sel)], axis=1), bands, rows, cols)
-    wide = 2 * cols
-    for k in range(bands):
-        c1 = apply_a(a_ref, va, k, bands, rows, skip)
+        c_ref[k * rows : (k + 1) * rows, 0:cols] = jnp.where(hit, 1.0, 0.0).astype(BF16)
+
+    def put_d(k, m, value):
+        low = value.astype(BF16)
+        c_ref[k * rows : (k + 1) * rows, m * cols : (m + 1) * cols] = low[:, :cols]
+        c_ref[k * rows : (k + 1) * rows, (m + 3) * cols : (m + 4) * cols] = low[:, cols:]
+
+    order = bands * rows
+    for k in range(bands):
+        slots = [m for m in range(bands) if not (skip and m == k ^ 2)]
+        row = slice(k * rows, (k + 1) * rows)
+        sel = jnp.concatenate([c_ref[m * rows : (m + 1) * rows, 0:cols] for m in slots], axis=0)
+        both = [
+            jnp.dot(
+                jnp.concatenate(
+                    [a_ref[row, part * order + m * rows : part * order + (m + 1) * rows] for m in slots], axis=1
+                ),
+                sel,
+                preferred_element_type=F32,
+            )
+            for part in (0, 1)
+        ]
+        c1 = jnp.concatenate(both, axis=1)
         put_v(vb, k, c1, bands, rows, cols)
-        csum[k * rows : (k + 1) * rows, :] = c1
-        d_ref[k * rows : (k + 1) * rows, 2 * wide : 3 * wide] = (0.5 * c1).astype(BF16)
+        csum[row, :] = c1
+        put_d(k, 3, 0.5 * c1)
     for k in range(bands):
         c2 = apply_a(a_ref, vb, k, bands, rows, skip)
         put_v(va, k, c2, bands, rows, cols)
         both = csum[k * rows : (k + 1) * rows, :] + 0.5 * c2
         csum[k * rows : (k + 1) * rows, :] = both
-        d_ref[k * rows : (k + 1) * rows, wide : 2 * wide] = both.astype(BF16)
+        put_d(k, 2, both)
     for k in range(bands):
         c3 = apply_a(a_ref, va, k, bands, rows, skip)
-        both = csum[k * rows : (k + 1) * rows, :] + c3 * (1.0 / 6.0)
-        d_ref[k * rows : (k + 1) * rows, 0:wide] = both.astype(BF16)
-
-
-def main_kernel(dims, ids, f0_ref, fg_ref, a_ref, d_ref, own_ref, keep_ref, send_ref, va, vb, vsum, right, left, outs):
+        put_d(k, 1, csum[k * rows : (k + 1) * rows, :] + c3 * (1.0 / 6.0))
+
+
+def main_kernel(dims, facts, *refs):
     bands, rows, cols, piece, local, count, block, per, skip = dims
+    f_refs = refs[:bands]
+    a_ref, c_ref, own_ref, keep_ref, send_ref, va, vb, vsum, t_ref, left, outs = refs[bands:]
     pieces = rows // piece
-    r, q = ids[0], ids[1]
-    wide = 2 * cols
+    r, q = facts[0], facts[1]
     row_iota = lax.broadcasted_iota(jnp.int32, (rows, cols), 0)
     col_iota = lax.broadcasted_iota(jnp.int32, (rows, cols), 1)
     col_abs = col_iota // piece * rows + q * piece + col_iota % piece
-    depth = 4 * cols
-    t_re, t_im = 2 * depth, 3 * depth
 
     def put_t(k, at, value):
         low = value.astype(BF16)
-        right[k * rows : (k + 1) * rows, t_re + at * cols : t_re + (at + 1) * cols] = low[:, :cols]
-        right[k * rows : (k + 1) * rows, t_im + at * cols : t_im + (at + 1) * cols] = low[:, cols:]
-
-    for k in range(bands):
-        here = (f0_ref[...] if k == 0 else fg_ref[k - 1]).astype(F32)
+        t_ref[k * rows : (k + 1) * rows, at * cols : (at + 1) * cols] = low[:, :cols]
+        t_ref[k * rows : (k + 1) * rows, (at + 4) * cols : (at + 5) * cols] = low[:, cols:]
+
+    for k in range(bands):
+        here = f_refs[k][...].astype(F32)
         row_abs = lax.bitwise_xor(r, k) * rows + row_iota
         real = jnp.where(row_abs < col_abs, here, jnp.where(row_abs == col_abs, 0.5 * here, 0.0))
         imag = jnp.where(row_abs > col_abs, here, 0.0)
         value = jnp.concatenate([real, imag], axis=1)
         put_v(va, k, value, bands, rows, cols)
         put_t(k, 1, value)
-        hit = (col_iota // piece == lax.bitwise_xor(r, k)) & (row_iota == q * piece + col_iota % piece)
-        span = slice(k * rows, (k + 1) * rows)
-        right[span, 0:cols] = jnp.where(hit, 1.0, 0.0).astype(BF16)
-        right[span, depth : depth + cols] = jnp.zeros((rows, cols), BF16)
-        for m in range(3):
-            right[span, (m + 1) * cols : (m + 2) * cols] = d_ref[span, m * wide : m * wide + cols]
-            right[span, depth + (m + 1) * cols : depth + (m + 2) * cols] = d_ref[span, m * wide + cols : (m + 1) * wide]
     for k in range(bands):
         v1 = apply_a(a_ref, va, k, bands, rows, skip)
         put_v(vb, k, v1, bands, rows, cols)
@@ -228,16 +250,30 @@
         v3 = apply_a(a_ref, va, k, bands, rows, skip)
         put_t(k, 0, vsum[k * rows : (k + 1) * rows, :] + v3 * (1.0 / 6.0))
     own = slice(0, rows)
-    cr, ci = right[own, 0:depth], right[own, depth : 2 * depth]
-    tr, ti = right[own, 2 * depth : 3 * depth], right[own, 3 * depth : 4 * depth]
-    for n, value in enumerate((tr, ti, cr, ci)):
-        left[0, :, n * depth : (n + 1) * depth] = value
-    for n, value in enumerate((ti, -tr, ci, -cr)):
-        left[1, :, n * depth : (n + 1) * depth] = value
+    half = 7 * cols
+    for which, values in enumerate(
+        (
+            (t_ref[own, 0 : 4 * cols], t_ref[own, 5 * cols : 8 * cols]),
+            (t_ref[own, 4 * cols : 8 * cols], -t_ref[own, cols : 4 * cols]),
+        )
+    ):
+        left[which, :, 0 : 4 * cols] = values[0]
+        left[which, :, 4 * cols : half] = values[1]
+    cr, ci = c_ref[own, 0 : 4 * cols], c_ref[own, 4 * cols : half]
+    none = jnp.zeros((rows, cols), BF16)
+    left[0, :, half : half + 4 * cols] = cr
+    left[0, :, half + 4 * cols : half + 5 * cols] = none
+    left[0, :, half + 5 * cols : half + 8 * cols] = ci
+    left[1, :, half : half + cols] = none
+    left[1, :, half + cols : half + 4 * cols] = ci
+    left[1, :, half + 4 * cols : half + 8 * cols] = -cr
     nt = (((1,), (1,)), ((), ()))
 
     def against(which, k):
-        return lax.dot_general(left[which], right[k * rows : (k + 1) * rows, :], nt, preferred_element_type=F32)
+        right = jnp.concatenate(
+            [c_ref[k * rows : (k + 1) * rows, :], t_ref[k * rows : (k + 1) * rows, :]], axis=1
+        )
+        return lax.dot_general(left[which], right, nt, preferred_element_type=F32)
 
     outs[0] = jnp.where(row_iota <= col_iota[:, :rows], against(0, 0), against(1, 0))
     for k in range(1, bands):
@@ -282,42 +318,46 @@
     per = 2 * local * count // shares
     skip = bands == 4 and local == 2
     dims = (bands, rows, cols, piece, local, count, block, per, skip)
-    ids = jnp.stack([r, q, me_plane, me_core]).astype(jnp.int32)
-
-    all_h = jnp.stack([h_real, h_imag]).reshape(shares, per * block, block)
-    share = lax.dynamic_index_in_dim(all_h, me_plane * 2 + me_core, 0, keepdims=False)
+
+    start = q * per
+    share = jnp.where(
+        lax.axis_index("runs") == 0,
+        lax.dynamic_slice_in_dim(h_real.reshape(local * count, block, block), start, per, 0),
+        lax.dynamic_slice_in_dim(h_imag.reshape(local * count, block, block), start, per, 0),
+    ).reshape(per * block, block)
     col_row = jnp.pad(h_cols.reshape(1, -1).astype(BF16), ((0, 15), (0, block - local * count)))
     message = jnp.concatenate([share, col_row], axis=0)
-    arrived = jnp.stack([exchange(message, "row", k) for k in range(1, bands)])
-    their_cols = arrived[:, per * block, : local * count].astype(jnp.int32)
-    all_cols = jnp.concatenate([h_cols.reshape(1, -1), their_cols], axis=0)
-    mine = arrived[:, : per * block, :]
+    arrived = [exchange(message, "row", k) for k in range(1, bands)]
+    their_cols = [a[per * block, : local * count].astype(jnp.int32) for a in arrived]
+    facts = jnp.concatenate(
+        [jnp.stack([r, q, me_plane, me_core]).astype(jnp.int32), h_cols.reshape(-1)] + their_cols
+    )
+    mine = jnp.stack([a[: per * block] for a in arrived])
     plane = jnp.stack([mine] + [exchange(mine, ("runs", "col"), k) for k in range(1, shares // 2)])
-    both = jnp.stack([plane, exchange(plane, "sub", 1)])
-    both = both.reshape(2, shares // 2, bands - 1, per, block, block)
-    rest = jnp.stack([exchange(here, "row", k) for k in range(1, bands)])
+    far = exchange(plane, "sub", 1)
+    near, far = [x.reshape(shares // 2, bands - 1, per, block, block) for x in (plane, far)]
+    rest = [exchange(here, "row", k) for k in range(1, bands)]
 
     smem = pl.BlockSpec(memory_space=pltpu.SMEM)
     vmem = pl.BlockSpec(memory_space=pltpu.VMEM)
-    params = pltpu.CompilerParams(vmem_limit_bytes=VMEM_BYTES)
     step = 2 * order * 2 * order * 2 * cols
-    a_big, d_all = pl.pallas_call(
+    a_big, c_side = pl.pallas_call(
         functools.partial(powers_kernel, dims),
         out_shape=(
             jax.ShapeDtypeStruct((order, 2 * order), BF16),
-            jax.ShapeDtypeStruct((order, 6 * cols), BF16),
+            jax.ShapeDtypeStruct((order, 7 * cols), BF16),
         ),
-        in_specs=[smem, smem, vmem, vmem, vmem],
+        in_specs=[smem] + [vmem] * 4,
         out_specs=(vmem, vmem),
         scratch_shapes=[
             pltpu.VMEM((2 * order, 2 * cols), BF16),
             pltpu.VMEM((2 * order, 2 * cols), BF16),
             pltpu.VMEM((order, 2 * cols), F32),
         ],
-        compiler_params=params,
-        cost_estimate=pl.CostEstimate(flops=3 * step, bytes_accessed=10 * 2**20, transcendentals=0),
+        compiler_params=pltpu.CompilerParams(vmem_limit_bytes=POWERS_VMEM),
+        cost_estimate=pl.CostEstimate(flops=4 * step, bytes_accessed=10 * 2**20, transcendentals=0),
         name="powers",
-    )(ids, all_cols, h_real, h_imag, both)
+    )(facts, h_real, h_imag, near, far)
     own, keep, send = pl.pallas_call(
         functools.partial(main_kernel, dims),
         out_shape=(
@@ -325,20 +365,20 @@
             jax.ShapeDtypeStruct((rows, cols), F32),
             jax.ShapeDtypeStruct((2, rows, cols), BF16),
         ),
-        in_specs=[smem, vmem, vmem, vmem, vmem],
+        in_specs=[smem] + [vmem] * (bands + 2),
         out_specs=(vmem, vmem, vmem),
         scratch_shapes=[
             pltpu.VMEM((2 * order, 2 * cols), BF16),
             pltpu.VMEM((2 * order, 2 * cols), BF16),
             pltpu.VMEM((order, 2 * cols), F32),
-            pltpu.VMEM((order, 16 * cols), BF16),
-            pltpu.VMEM((2, rows, 16 * cols), BF16),
+            pltpu.VMEM((order, 8 * cols), BF16),
+            pltpu.VMEM((2, rows, 15 * cols), BF16),
             pltpu.VMEM((bands, rows, rows), F32),
         ],
-        compiler_params=params,
+        compiler_params=pltpu.CompilerParams(vmem_limit_bytes=MAIN_VMEM),
         cost_estimate=pl.CostEstimate(flops=6 * step, bytes_accessed=10 * 2**20, transcendentals=0),
         name="main",
-    )(ids, here, rest, a_big, d_all)
+    )(facts, here, *rest, a_big, c_side)
     swapped = exchange(send, "sub", 1)
     across = exchange((keep + swapped[1].astype(F32)).astype(BF16), "col", 1)
     total = here.astype(F32) + own + swapped[0].astype(F32) + across.astype(F32)

time: 74.3 us -> 51 us (0.69)
  waiting for transfers between devices: 27.9 us -> 16.6 us
  Pallas kernels: 23.2 us -> 16 us
  other arithmetic: 7.45 us -> 2.68 us
    ppermute x12, waiting for transfers between devices: 27.9 us -> 16.6 us  [exchange(): return lax.ppermute(block, axes, [(i, i ^ offset) for i in range(count)])]
    another operation x5 -> x0, other arithmetic: 4.02 us -> none  [the longest x1 1.43 us: gathered_body(): both = jnp.stack([plane, exchange(plane, 'sub', 1)])]
    pallas_call x1, Pallas kernels: 13.8 us -> 9.86 us  [gathered_body(): pl.pallas_call(functools.partial(main_kernel, dims), out_shape=(jax.Shape...]
    pallas_call x1, Pallas kernels: 9.4 us -> 6.09 us  [gathered_body(): pl.pallas_call(functools.partial(powers_kernel, dims), out_shape=(jax.Sha...]
    broadcast_in_dim x1, other arithmetic: 1.72 us -> 0.76 us  [gathered_body(): return total[None]]
    convert_element_type x1, other arithmetic: 0.98 us -> 0.03 us  [gathered_body(): across = exchange((keep + swapped[1].astype(F32)).astype(BF16), 'col', 1)]
    select_n x0 -> x1, other arithmetic: none -> 0.88 us  [gathered_body(): jnp.where(lax.axis_index('runs') == 0, lax.dynamic_slice_in_dim(h_real.re...]
  transfers between devices with their start and end apart: 12 -> 12, of which waited for: 8 -> 7; matrix products, arithmetic and copies ran while one was open for 3% -> 2% of each run, Pallas kernels for 0% -> 12%
where the time goes in v3:
time: 51 us; the launch traced here: 50.8 us
  waiting for transfers between devices  16.6 us (33%)
  Pallas kernels  16 us (31%)
  starting transfers between devices  14.4 us (28%)
  other arithmetic  2.68 us (5%)
  local copies, waits for them, and re-layouts  0.96 us (2%)
    ppermute x12, waiting for transfers between devices, exchange(): return lax.ppermute(block, axes, [(i, i ^ offset) for i in range(count)])  16.6 us
    ppermute x12, starting transfers between devices, exchange(): return lax.ppermute(block, axes, [(i, i ^ offset) for i in range(count)])  14.4 us
    pallas_call x1, Pallas kernels, gathered_body(): pl.pallas_call(functools.partial(main_kernel, dims), out_shape=(jax.Shape...  9.86 us
    pallas_call x1, Pallas kernels, gathered_body(): pl.pallas_call(functools.partial(powers_kernel, dims), out_shape=(jax.Sha...  6.09 us
  transfers between devices with their start and end apart: 12, of which 7 were waited for; matrix products, arithmetic and copies ran while one was open for 2% of the time, Pallas kernels for 12%

profile of v3, /device:TPU:0, one launch (start us, length us, event | category | flops | bytes accessed | tf_op | source)
XLA Modules:
  0.0 50.8 jit_solution(6942519207600279841)
XLA Ops:
  0.0 0.0 copy-start.2
  0.0 0.0 copy-start.1
  0.0 0.7 %convert_element_type.56 = bf16[2,4]{1,0:T(2,128)(2,1)S(1)} convert(s32[2,4]{1,0:T(2,128)} %param.7) | non-fusion elementwise | flops 8 | bytes 48 | tf_op jit(solution)/shard_map/convert_element_type | solution.py:328
  0.7 0.1 convert_element_type.57
  0.8 0.9 %dynamic-slice_select_fusion = bf16[2,128,128]{2,1,0:T(8,128)(2,1)S(1)} fusion(bf16[8,128,128]{2,1,0:T(8,128)(2,1)} %bitcast.58, s32[]{:T(128)S(6)} %select_n.13, bf16[8,128,128]{2,1,0:T(8,128)(2,1)} %bitcast.59, pred[]{:T(512)S(6)} %eq.3), kind=kLoop, calls=%fused_computation.13 | loop fusion | flops 32768 | bytes 196613 | tf_op jit(solution)/shard_map/jit(_where)/select_n | solution.py:323
  1.7 3.1 %collective-permute-start = (bf16[272,128]{1,0:T(8,128)(2,1)S(1)}, bf16[272,128]{1,0:T(8,128)(2,1)S(1)}, u32[]{:S(2)}, u32[]{:S(2)}) collective-permute-start(bf16[272,128]{1,0:T(8,128)(2,1)S(1)} %fusion.4), channel_id=1, source_target_pairs={{0,4},{4,0},{8,12},{12,8},{1,5},{5,1},{9,13},{13,9},{2,6},{6,2},{1... | collective-permute-start | bytes 208904 | tf_op jit(solution)/shard_map/ppermute | solution.py:109
  4.8 2.6 %collective-permute-start.1 = (bf16[272,128]{1,0:T(8,128)(2,1)S(1)}, bf16[272,128]{1,0:T(8,128)(2,1)S(1)}, u32[]{:S(2)}, u32[]{:S(2)}) collective-permute-start(bf16[272,128]{1,0:T(8,128)(2,1)S(1)} %fusion.4), channel_id=1, source_target_pairs={{0,8},{4,12},{8,0},{12,4},{1,9},{5,13},{9,1},{13,5},{2,10},{6,14},... | collective-permute-start | bytes 208904 | tf_op jit(solution)/shard_map/ppermute | solution.py:109
  7.4 0.0 collective-permute-start.2
  7.4 0.0 collective-permute-done
  7.4 4.9 %collective-permute-done.1 = bf16[272,128]{1,0:T(8,128)(2,1)S(1)} collective-permute-done((bf16[272,128]{1,0:T(8,128)(2,1)S(1)}, bf16[272,128]{1,0:T(8,128)(2,1)S(1)}, u32[]{:S(2)}, u32[]{:S(2)}) %collective-permute-start.1) | collective-permute-done | bytes 69664 | tf_op jit(solution)/shard_map/ppermute | solution.py:109
  12.4 1.3 %collective-permute-done.2 = bf16[272,128]{1,0:T(8,128)(2,1)S(1)} collective-permute-done((bf16[272,128]{1,0:T(8,128)(2,1)S(1)}, bf16[272,128]{1,0:T(8,128)(2,1)S(1)}, u32[]{:S(2)}, u32[]{:S(2)}) %collective-permute-start.2) | collective-permute-done | bytes 69664 | tf_op jit(solution)/shard_map/ppermute | solution.py:109
  13.7 1.6 %collective-permute-start.6 = (bf16[3,256,128]{2,1,0:T(8,128)(2,1)S(1)}, bf16[3,256,128]{2,1,0:T(8,128)(2,1)S(1)}, u32[]{:S(2)}, u32[]{:S(2)}) collective-permute-start(bf16[3,256,128]{2,1,0:T(8,128)(2,1)S(1)} %get-tuple-element.16), channel_id=1, source_target_pairs={{0,2},{2,0},{16,18},{18,16},{1,3},{3,1},{17,19},{19,17},{4,6},{6,4... | collective-permute-start | bytes 589832 | tf_op jit(solution)/shard_map/ppermute | solution.py:109
  15.2 1.5 %collective-permute-start.7 = (bf16[3,256,128]{2,1,0:T(8,128)(2,1)S(1)}, bf16[3,256,128]{2,1,0:T(8,128)(2,1)S(1)}, u32[]{:S(2)}, u32[]{:S(2)}) collective-permute-start(bf16[3,256,128]{2,1,0:T(8,128)(2,1)S(1)} %get-tuple-element.16), channel_id=1, source_target_pairs={{0,16},{2,18},{16,0},{18,2},{1,17},{3,19},{17,1},{19,3},{4,20},{6,... | collective-permute-start | bytes 589832 | tf_op jit(solution)/shard_map/ppermute | solution.py:109
  16.8 0.5 collective-permute-start.8
  17.2 0.8 %collective-permute-start.3 = (bf16[256,256]{1,0:T(8,128)(2,1)}, bf16[256,256]{1,0:T(8,128)(2,1)S(1)}, u32[]{:S(2)}, u32[]{:S(2)}) collective-permute-start(bf16[256,256]{1,0:T(8,128)(2,1)} %bitcast.54), channel_id=1, source_target_pairs={{0,4},{4,0},{8,12},{12,8},{1,5},{5,1},{9,13},{13,9},{2,6},{6,2},{1... | collective-permute-start | bytes 393224 | tf_op jit(solution)/shard_map/ppermute | solution.py:109
  18.0 1.8 %collective-permute-start.4 = (bf16[256,256]{1,0:T(8,128)(2,1)}, bf16[256,256]{1,0:T(8,128)(2,1)S(1)}, u32[]{:S(2)}, u32[]{:S(2)}) collective-permute-start(bf16[256,256]{1,0:T(8,128)(2,1)} %bitcast.55), channel_id=1, source_target_pairs={{0,8},{4,12},{8,0},{12,4},{1,9},{5,13},{9,1},{13,5},{2,10},{6,14},... | collective-permute-start | bytes 393224 | tf_op jit(solution)/shard_map/ppermute | solution.py:109
  19.8 0.8 %reshape.58 = s32[8]{0:T(128)S(1)} reshape(s32[2,4]{1,0:T(2,128)} %param.7) | data formatting | bytes 64 | tf_op jit(solution)/shard_map/reshape | solution.py:333
  20.5 0.4 collective-permute-done.6
  21.0 1.4 %collective-permute-start.5 = (bf16[256,256]{1,0:T(8,128)(2,1)}, bf16[256,256]{1,0:T(8,128)(2,1)S(1)}, u32[]{:S(2)}, u32[]{:S(2)}) collective-permute-start(bf16[256,256]{1,0:T(8,128)(2,1)} %bitcast.56), channel_id=1, source_target_pairs={{0,12},{4,8},{8,4},{12,0},{1,13},{5,9},{9,5},{13,1},{2,14},{6,10},... | collective-permute-start | bytes 393224 | tf_op jit(solution)/shard_map/ppermute | solution.py:109
  22.4 1.9 %collective-permute-done.7 = bf16[3,256,128]{2,1,0:T(8,128)(2,1)S(1)} collective-permute-done((bf16[3,256,128]{2,1,0:T(8,128)(2,1)S(1)}, bf16[3,256,128]{2,1,0:T(8,128)(2,1)S(1)}, u32[]{:S(2)}, u32[]{:S(2)}) %collective-permute-start.7) | collective-permute-done | bytes 196640 | tf_op jit(solution)/shard_map/ppermute | solution.py:109
  24.3 0.0 collective-permute-done.8
  24.3 0.1 pad_maximum_fusion.1
  24.4 0.1 collective-permute-start.9
  24.6 0.1 concatenate.9.facts
  24.6 0.1 pad_maximum_fusion.near_ref
  24.8 2.0 %collective-permute-done.9 = bf16[4,3,256,128]{3,2,1,0:T(8,128)(2,1)S(1)} collective-permute-done((bf16[4,3,256,128]{3,2,1,0:T(8,128)(2,1)S(1)}, bf16[4,3,256,128]{3,2,1,0:T(8,128)(2,1)S(1)}, u32[]{:S(2)}, u32[]{:S(2)}) %collective-permute-start.9) | collective-permute-done | bytes 786464 | tf_op jit(solution)/shard_map/ppermute | solution.py:109
  26.8 0.0 copy-done.2
  26.8 0.0 copy-done.1
  26.8 0.0 copy-start
  26.8 6.1 %powers.1 = (bf16[1024,2048]{1,0:T(8,128)(2,1)S(1)}, bf16[1024,1792]{1,0:T(8,128)(2,1)S(1)}) custom-call(s32[36]{0:T(128)S(1)} %concatenate.9.facts, bf16[2,4,128,128]{3,2,1,0:T(8,128)(2,1)S(1)} %copy-done.2, bf16[2,4,128,128]{3,2,1,0:T(8,128)(2,1)S(1)} %copy-done.1, bf16[4,3,2,128,128]{4,3,2,1,0:T(8,128)(2,1)S(1)} %pad_maximum_fusion.near_ref, ...), custom_call_target="tpu_custom_call" | custom-call | flops 8589934592 | bytes 10485760 | tf_op jit(solution)/shard_map/powers/pallas_call | solution.py:344
  32.9 0.0 collective-permute-done.3.refs_1_
  32.9 0.0 collective-permute-done.4.refs_2_
  32.9 0.0 collective-permute-done.5.refs_3_
  32.9 0.0 copy-done
  32.9 9.9 %main.1 = (f32[256,256]{1,0:T(8,128)S(1)}, f32[256,256]{1,0:T(8,128)S(1)}, bf16[2,256,256]{2,1,0:T(8,128)(2,1)S(1)}) custom-call(s32[36]{0:T(128)S(1)} %concatenate.9.facts, bf16[256,256]{1,0:T(8,128)(2,1)S(1)} %bitcast.57, bf16[256,256]{1,0:T(8,128)(2,1)S(1)} %collective-permute-done.3.refs_1_, bf16[256,256]{1,0:T(8,128)(2,1)S(1)} %collective-permute-done.4.refs_2_, ...), custom_call_target="tpu_custom_call" | custom-call | flops 12884901888 | bytes 10485760 | tf_op jit(solution)/shard_map/main/pallas_call | solution.py:361
  42.8 0.2 collective-permute-start.10
  43.0 1.4 %collective-permute-done.10 = bf16[2,256,256]{2,1,0:T(8,128)(2,1)S(1)} collective-permute-done((bf16[2,256,256]{2,1,0:T(8,128)(2,1)S(1)}, bf16[2,256,256]{2,1,0:T(8,128)(2,1)S(1)}, u32[]{:S(2)}, u32[]{:S(2)}) %collective-permute-start.10) | collective-permute-done | bytes 262176 | tf_op jit(solution)/shard_map/ppermute | solution.py:109
  44.4 1.0 %collective-permute-start.11 = (bf16[256,256]{1,0:T(8,128)(2,1)S(1)}, bf16[256,256]{1,0:T(8,128)(2,1)S(1)}, u32[]{:S(2)}, u32[]{:S(2)}) collective-permute-start(bf16[256,256]{1,0:T(8,128)(2,1)S(1)} %fusion), channel_id=1, source_target_pairs={{0,2},{2,0},{1,3},{3,1},{4,6},{6,4},{5,7},{7,5},{8,10},{10,8},{9,1... | collective-permute-start | bytes 393224 | tf_op jit(solution)/shard_map/ppermute | solution.py:109
  45.4 4.6 %collective-permute-done.11 = bf16[256,256]{1,0:T(8,128)(2,1)S(1)} collective-permute-done((bf16[256,256]{1,0:T(8,128)(2,1)S(1)}, bf16[256,256]{1,0:T(8,128)(2,1)S(1)}, u32[]{:S(2)}, u32[]{:S(2)}) %collective-permute-start.11) | collective-permute-done | bytes 131104 | tf_op jit(solution)/shard_map/ppermute | solution.py:109
  50.0 0.8 %fusion.2 = f32[1,256,256]{2,1,0:T(8,128)} fusion(bf16[256,256]{1,0:T(8,128)(2,1)S(1)} %collective-permute-done.11, f32[256,256]{1,0:T(8,128)S(1)} %get-tuple-element.12, bf16[2,256,256]{2,1,0:T(8,128)(2,1)S(1)} %collective-permute-done.10, bf16[1,256,256]{2,1,0:T(8,128)(2,1)S(1)} %copy-done), kind=kLoop, calls=%fused_computation.6 | loop fusion | flops 393216 | bytes 917504 | tf_op jit(solution)/shard_map/broadcast_in_dim | solution.py:385
  (9 shorter events, 0.1 us)
Async XLA Ops:
  0.0 26.8 %copy-start.2 = (bf16[2,4,128,128]{3,2,1,0:T(8,128)(2,1)S(1)}, bf16[2,4,128,128]{3,2,1,0:T(8,128)(2,1)}, u32[]{:S(2)}) copy-start(bf16[2,4,128,128]{3,2,1,0:T(8,128)(2,1)} %hr_ref.1) | copy-start | bytes 786436
  0.0 26.8 %copy-start.1 = (bf16[2,4,128,128]{3,2,1,0:T(8,128)(2,1)S(1)}, bf16[2,4,128,128]{3,2,1,0:T(8,128)(2,1)}, u32[]{:S(2)}) copy-start(bf16[2,4,128,128]{3,2,1,0:T(8,128)(2,1)} %hi_ref.1) | copy-start | bytes 786436
  1.7 5.7 %collective-permute-start = (bf16[272,128]{1,0:T(8,128)(2,1)S(1)}, bf16[272,128]{1,0:T(8,128)(2,1)S(1)}, u32[]{:S(2)}, u32[]{:S(2)}) collective-permute-start(bf16[272,128]{1,0:T(8,128)(2,1)S(1)} %fusion.4), channel_id=1, source_target_pairs={{0,4},{4,0},{8,12},{12,8},{1,5},{5,1},{9,13},{13,9},{2,6},{6,2},{1... | collective-permute-start | bytes 208904 | tf_op jit(solution)/shard_map/ppermute | solution.py:109
  4.8 7.5 %collective-permute-start.1 = (bf16[272,128]{1,0:T(8,128)(2,1)S(1)}, bf16[272,128]{1,0:T(8,128)(2,1)S(1)}, u32[]{:S(2)}, u32[]{:S(2)}) collective-permute-start(bf16[272,128]{1,0:T(8,128)(2,1)S(1)} %fusion.4), channel_id=1, source_target_pairs={{0,8},{4,12},{8,0},{12,4},{1,9},{5,13},{9,1},{13,5},{2,10},{6,14},... | collective-permute-start | bytes 208904 | tf_op jit(solution)/shard_map/ppermute | solution.py:109
  7.4 6.2 %collective-permute-start.2 = (bf16[272,128]{1,0:T(8,128)(2,1)S(1)}, bf16[272,128]{1,0:T(8,128)(2,1)S(1)}, u32[]{:S(2)}, u32[]{:S(2)}) collective-permute-start(bf16[272,128]{1,0:T(8,128)(2,1)S(1)} %fusion.4), channel_id=1, source_target_pairs={{0,12},{4,8},{8,4},{12,0},{1,13},{5,9},{9,5},{13,1},{2,14},{6,10},... | collective-permute-start | bytes 208904 | tf_op jit(solution)/shard_map/ppermute | solution.py:109
  13.7 7.3 %collective-permute-start.6 = (bf16[3,256,128]{2,1,0:T(8,128)(2,1)S(1)}, bf16[3,256,128]{2,1,0:T(8,128)(2,1)S(1)}, u32[]{:S(2)}, u32[]{:S(2)}) collective-permute-start(bf16[3,256,128]{2,1,0:T(8,128)(2,1)S(1)} %get-tuple-element.16), channel_id=1, source_target_pairs={{0,2},{2,0},{16,18},{18,16},{1,3},{3,1},{17,19},{19,17},{4,6},{6,4... | collective-permute-start | bytes 589832 | tf_op jit(solution)/shard_map/ppermute | solution.py:109
  15.2 9.1 %collective-permute-start.7 = (bf16[3,256,128]{2,1,0:T(8,128)(2,1)S(1)}, bf16[3,256,128]{2,1,0:T(8,128)(2,1)S(1)}, u32[]{:S(2)}, u32[]{:S(2)}) collective-permute-start(bf16[3,256,128]{2,1,0:T(8,128)(2,1)S(1)} %get-tuple-element.16), channel_id=1, source_target_pairs={{0,16},{2,18},{16,0},{18,2},{1,17},{3,19},{17,1},{19,3},{4,20},{6,... | collective-permute-start | bytes 589832 | tf_op jit(solution)/shard_map/ppermute | solution.py:109
  16.8 7.6 %collective-permute-start.8 = (bf16[3,256,128]{2,1,0:T(8,128)(2,1)S(1)}, bf16[3,256,128]{2,1,0:T(8,128)(2,1)S(1)}, u32[]{:S(2)}, u32[]{:S(2)}) collective-permute-start(bf16[3,256,128]{2,1,0:T(8,128)(2,1)S(1)} %get-tuple-element.16), channel_id=1, source_target_pairs={{0,18},{2,16},{16,2},{18,0},{1,19},{3,17},{17,3},{19,1},{4,22},{6,... | collective-permute-start | bytes 589832 | tf_op jit(solution)/shard_map/ppermute | solution.py:109
  17.2 15.7 %collective-permute-start.3 = (bf16[256,256]{1,0:T(8,128)(2,1)}, bf16[256,256]{1,0:T(8,128)(2,1)S(1)}, u32[]{:S(2)}, u32[]{:S(2)}) collective-permute-start(bf16[256,256]{1,0:T(8,128)(2,1)} %bitcast.54), channel_id=1, source_target_pairs={{0,4},{4,0},{8,12},{12,8},{1,5},{5,1},{9,13},{13,9},{2,6},{6,2},{1... | collective-permute-start | bytes 393224 | tf_op jit(solution)/shard_map/ppermute | solution.py:109
  18.0 14.9 %collective-permute-start.4 = (bf16[256,256]{1,0:T(8,128)(2,1)}, bf16[256,256]{1,0:T(8,128)(2,1)S(1)}, u32[]{:S(2)}, u32[]{:S(2)}) collective-permute-start(bf16[256,256]{1,0:T(8,128)(2,1)} %bitcast.55), channel_id=1, source_target_pairs={{0,8},{4,12},{8,0},{12,4},{1,9},{5,13},{9,1},{13,5},{2,10},{6,14},... | collective-permute-start | bytes 393224 | tf_op jit(solution)/shard_map/ppermute | solution.py:109
  21.0 11.9 %collective-permute-start.5 = (bf16[256,256]{1,0:T(8,128)(2,1)}, bf16[256,256]{1,0:T(8,128)(2,1)S(1)}, u32[]{:S(2)}, u32[]{:S(2)}) collective-permute-start(bf16[256,256]{1,0:T(8,128)(2,1)} %bitcast.56), channel_id=1, source_target_pairs={{0,12},{4,8},{8,4},{12,0},{1,13},{5,9},{9,5},{13,1},{2,14},{6,10},... | collective-permute-start | bytes 393224 | tf_op jit(solution)/shard_map/ppermute | solution.py:109
  24.4 2.4 %collective-permute-start.9 = (bf16[4,3,256,128]{3,2,1,0:T(8,128)(2,1)S(1)}, bf16[4,3,256,128]{3,2,1,0:T(8,128)(2,1)S(1)}, u32[]{:S(2)}, u32[]{:S(2)}) collective-permute-start(bf16[4,3,256,128]{3,2,1,0:T(8,128)(2,1)S(1)} %pad_maximum_fusion.1), channel_id=1, source_target_pairs={{0,1},{1,0},{2,3},{3,2},{4,5},{5,4},{6,7},{7,6},{8,9},{9,8},{10,11... | collective-permute-start | bytes 2359304 | tf_op jit(solution)/shard_map/ppermute | solution.py:109
  26.8 6.1 %copy-start = (bf16[1,256,256]{2,1,0:T(8,128)(2,1)S(1)}, bf16[1,256,256]{2,1,0:T(8,128)(2,1)}, u32[]{:S(2)}) copy-start(bf16[1,256,256]{2,1,0:T(8,128)(2,1)} %param.4) | copy-start | bytes 393220
  42.8 1.6 %collective-permute-start.10 = (bf16[2,256,256]{2,1,0:T(8,128)(2,1)S(1)}, bf16[2,256,256]{2,1,0:T(8,128)(2,1)S(1)}, u32[]{:S(2)}, u32[]{:S(2)}) collective-permute-start(bf16[2,256,256]{2,1,0:T(8,128)(2,1)S(1)} %get-tuple-element.13), channel_id=1, source_target_pairs={{0,1},{1,0},{2,3},{3,2},{4,5},{5,4},{6,7},{7,6},{8,9},{9,8},{10,11... | collective-permute-start | bytes 786440 | tf_op jit(solution)/shard_map/ppermute | solution.py:109
  44.4 5.6 %collective-permute-start.11 = (bf16[256,256]{1,0:T(8,128)(2,1)S(1)}, bf16[256,256]{1,0:T(8,128)(2,1)S(1)}, u32[]{:S(2)}, u32[]{:S(2)}) collective-permute-start(bf16[256,256]{1,0:T(8,128)(2,1)S(1)} %fusion), channel_id=1, source_target_pairs={{0,2},{2,0},{1,3},{3,1},{4,6},{6,4},{5,7},{7,5},{8,10},{10,8},{9,1... | collective-permute-start | bytes 393224 | tf_op jit(solution)/shard_map/ppermute | solution.py:109

commit v4 on v1

--- a/solution.py
+++ b/solution.py
@@ -1,6 +1,10 @@
+import functools
+
 import jax
 import jax.numpy as jnp
 from jax import lax
+from jax.experimental import pallas as pl
+from jax.experimental.pallas import tpu as pltpu
 from jax.sharding import PartitionSpec as P
 
 TERMS = 3
@@ -39,7 +43,7 @@
     return placed.reshape(groups, rows_here, col_count)
 
 
-def body(packed, h_real, h_imag, h_cols):
+def banded_body(packed, h_real, h_imag, h_cols):
     packed_here = packed.reshape(packed.shape[1], packed.shape[2])
     rows_here, col_count = packed_here.shape
     band_index = lax.axis_index("row")
@@ -93,6 +97,319 @@
     return result[None]
 
 
+VMEM_BYTES = 56 * 2**20
+POWERS_VMEM = 20 * 2**20
+MAIN_VMEM = 24 * 2**20
+F32 = jnp.float32
+BF16 = jnp.bfloat16
+
+
+def exchange(block, axes, offset):
+    count = lax.axis_size(axes)
+    return lax.ppermute(block, axes, [(i, i ^ offset) for i in range(count)])
+
+
+def block_product(dims, facts, h_ref, at, take):
+    bands, rows, cols, piece, local, count, block, per = dims
+    starts = []
+    for s in range(count):
+        column = facts[4 + at * count + s]
+        slot = lax.bitwise_xor(column // local, facts[0])
+        starts.append(pl.multiple_of((slot * local + column % local) * block, block))
+    right = jnp.concatenate([take(pl.ds(start, block)) for start in starts], axis=0)
+    return jnp.dot(h_ref[at], right, preferred_element_type=F32)
+
+
+def apply_a(dims, facts, h_ref, at, take, width):
+    block = dims[6]
+    got = block_product(dims, facts, h_ref, at, take)
+    real = got[:block, :width] + got[block:, width:]
+    imag = got[:block, width:] - got[block:, :width]
+    return 0.5 * jnp.concatenate([real, imag], axis=1)
+
+
+def powers_kernel(dims, facts, mine_ref, near_ref, far_ref, h_ref, c_ref, sel, c1_ref, c2_ref, csum):
+    bands, rows, cols, piece, local, count, block, per = dims
+    r, q, me_plane, me_core = facts[0], facts[1], facts[2], facts[3]
+    h_ref[0:local] = mine_ref[...]
+    for n in range(2 * near_ref.shape[0]):
+        part = (near_ref, far_ref)[n % 2]
+        share = lax.bitwise_xor(me_plane, n // 2) * 2 + lax.bitwise_xor(me_core, n % 2)
+        for at in range(per):
+            flat = share * per + at
+            below = pl.multiple_of((1 - flat // (local * count)) * block, block)
+            b = flat // count % local
+            beside = pl.multiple_of(flat % count * block, block)
+            for k in range(1, bands):
+                h_ref[k * local + b, pl.ds(below, block), pl.ds(beside, block)] = part[
+                    n // 2, k - 1, at * block : (at + 1) * block, :
+                ]
+    row_iota = lax.broadcasted_iota(jnp.int32, (rows, cols), 0)
+    col_iota = lax.broadcasted_iota(jnp.int32, (rows, cols), 1)
+    for k in range(bands):
+        hit = (col_iota // piece == k) & (row_iota == q * piece + col_iota % piece)
+        sel[k * rows : (k + 1) * rows, :] = jnp.where(hit, 1.0, 0.0).astype(BF16)
+
+    def put_d(span, m, value):
+        low = value.astype(BF16)
+        c_ref[span, m * cols : (m + 1) * cols] = low[:, :cols]
+        c_ref[span, (m + 3) * cols : (m + 4) * cols] = low[:, cols:]
+
+    for at in range(bands * local):
+        span = slice(at * block, (at + 1) * block)
+        got = block_product(dims, facts, h_ref, at, lambda where: sel[where, :])
+        c1 = 0.5 * jnp.concatenate([got[:block], -got[block:]], axis=1)
+        c1_ref[span, :] = c1.astype(BF16)
+        csum[span, :] = c1
+        put_d(span, 2, 0.5 * c1)
+    for at in range(bands * local):
+        span = slice(at * block, (at + 1) * block)
+        c2 = apply_a(dims, facts, h_ref, at, lambda where: c1_ref[where, :], cols)
+        c2_ref[span, :] = c2.astype(BF16)
+        both = csum[span, :] + 0.5 * c2
+        csum[span, :] = both
+        put_d(span, 1, both)
+    for at in range(bands * local):
+        span = slice(at * block, (at + 1) * block)
+        c3 = apply_a(dims, facts, h_ref, at, lambda where: c2_ref[where, :], cols)
+        put_d(span, 0, csum[span, :] + c3 * (1.0 / 6.0))
+
+
+def swap_groups(value, r, piece):
+    size = value.shape[1]
+    groups = size // piece
+    bit = 1
+    while bit < groups:
+        moved = jnp.concatenate(
+            [value[:, (g ^ bit) * piece : (g ^ bit) * piece + piece] for g in range(groups)], axis=1
+        )
+        value = jnp.where(lax.bitwise_and(r, bit) != 0, moved, value)
+        bit *= 2
+    return value
+
+
+def main_kernel(dims, facts, *refs):
+    bands, rows, cols, piece, local, count, block, per = dims
+    f_refs = refs[:bands]
+    h_ref, c_ref, own_ref, keep_ref, send_ref, n_ref, v1_ref, v2_ref, slab, tops, left, outs = refs[bands:]
+    pieces = rows // piece
+    r, q = facts[0], facts[1]
+    row_iota = lax.broadcasted_iota(jnp.int32, (rows, cols), 0)
+    col_iota = lax.broadcasted_iota(jnp.int32, (rows, cols), 1)
+    col_abs = col_iota // piece * rows + q * piece + col_iota % piece
+    for k in range(bands):
+        here = f_refs[k][...].astype(F32)
+        row_abs = lax.bitwise_xor(r, k) * rows + row_iota
+        real = jnp.where(row_abs < col_abs, here, jnp.where(row_abs == col_abs, 0.5 * here, 0.0))
+        imag = jnp.where(row_abs > col_abs, here, 0.0)
+        for half, value in enumerate((real, imag)):
+            n_ref[k * rows : (k + 1) * rows, half * cols : (half + 1) * cols] = swap_groups(
+                value, r, piece
+            ).astype(BF16)
+
+    def thin(value):
+        return jnp.concatenate([value[:, :piece], value[:, cols : cols + piece]], axis=1)
+
+    for at in range(bands * local):
+        span = slice(at * block, (at + 1) * block)
+        v1 = apply_a(dims, facts, h_ref, at, lambda where: n_ref[where, :], cols)
+        v1_ref[span, :] = v1.astype(BF16)
+        slab[span, :] = thin(v1)
+        if at < local:
+            tops[span, :] = v1
+    for at in range(bands * local):
+        span = slice(at * block, (at + 1) * block)
+        v2 = apply_a(dims, facts, h_ref, at, lambda where: v1_ref[where, :], cols)
+        v2_ref[span, :] = v2.astype(BF16)
+        slab[span, :] += 0.5 * thin(v2)
+        if at < local:
+            tops[span, :] += 0.5 * v2
+    for at in range(bands * local):
+        span = slice(at * block, (at + 1) * block)
+        if at < local:
+            v3 = apply_a(dims, facts, h_ref, at, lambda where: v2_ref[where, :], cols)
+            tops[span, :] += v3 * (1.0 / 6.0)
+            slab[span, :] += thin(v3) * (1.0 / 6.0)
+        else:
+            v3 = apply_a(
+                dims,
+                facts,
+                h_ref,
+                at,
+                lambda where: jnp.concatenate(
+                    [v2_ref[where, 0:piece], v2_ref[where, cols : cols + piece]],
+                    axis=1,
+                ),
+                piece,
+            )
+            slab[span, :] += v3 * (1.0 / 6.0)
+    own = slice(0, rows)
+    three = 3 * cols
+    for m, t_ref in enumerate((n_ref, v1_ref, v2_ref)):
+        tr, ti = t_ref[own, :cols], t_ref[own, cols:]
+        cr = c_ref[own, m * cols : (m + 1) * cols]
+        ci = c_ref[own, three + m * cols : three + (m + 1) * cols]
+        for which, (first, second, third, fourth) in enumerate(((tr, ti, cr, ci), (ti, -tr, ci, -cr))):
+            left[which, :, m * cols : (m + 1) * cols] = first
+            left[which, :, three + m * cols : three + (m + 1) * cols] = second
+            left[which, :, 2 * three + 2 * m * cols : 2 * three + (2 * m + 1) * cols] = third
+            left[which, :, 2 * three + (2 * m + 1) * cols : 2 * three + (2 * m + 2) * cols] = fourth
+    nt = (((1,), (1,)), ((), ()))
+
+    def against(which, k):
+        span = slice(k * rows, (k + 1) * rows)
+        right = jnp.concatenate([ref[span, :] for ref in (c_ref, n_ref, v1_ref, v2_ref)], axis=1)
+        return lax.dot_general(left[which], right, nt, preferred_element_type=F32)
+
+    upper = row_iota[:, :rows] <= lax.broadcasted_iota(jnp.int32, (rows, rows), 1)
+    mine = pl.ds(pl.multiple_of(q * piece, piece), piece)
+    thin_row = q * piece + lax.broadcasted_iota(jnp.int32, (piece, rows), 0)
+    thin_upper = thin_row <= lax.broadcasted_iota(jnp.int32, (piece, rows), 1)
+    outs[0] = jnp.where(upper, against(0, 0), against(1, 0))
+    for k in range(1, bands):
+        lower = (lax.bitwise_xor(r, k) < r).astype(jnp.int32)
+        outs[k] = against(lower, k)
+    for k in range(bands):
+        turned = slab[k * rows : (k + 1) * rows, :].T
+        real, imag = turned[:piece], -turned[piece:]
+        if k == 0:
+            extra = jnp.where(thin_upper, real, imag)
+        else:
+            extra = jnp.where(lax.bitwise_xor(r, k) > r, real, imag)
+        outs[k, mine, :] += extra
+
+    def target(piece_index):
+        return jnp.concatenate(
+            [outs[lax.bitwise_xor(r, b)][:, piece_index * piece : (piece_index + 1) * piece] for b in range(bands)],
+            axis=1,
+        )
+
+    for p in range(pieces):
+        offset = lax.bitwise_xor(q, p)
+        value = target(p)
+
+        @pl.when(offset == 0)
+        def _():
+            real = swap_groups(tops[:, :cols], r, piece)
+            imag = swap_groups(tops[:, cols:], r, piece)
+            own_ref[...] = value + jnp.where(r * rows + row_iota <= col_abs, real, imag)
+
+        @pl.when(offset == 2)
+        def _():
+            keep_ref[...] = value
+
+        @pl.when(offset % 2 == 1)
+        def _():
+            send_ref[offset // 2] = value.astype(BF16)
+
+
+def gathered_body(packed, h_real, h_imag, h_cols):
+    here = packed.reshape(packed.shape[1], packed.shape[2])
+    rows, cols = here.shape
+    bands = lax.axis_size("row")
+    piece = rows // lax.axis_size(("col", "sub"))
+    local, count, block = h_real.shape[0], h_real.shape[1], h_real.shape[2]
+    order = bands * rows
+    r = lax.axis_index("row")
+    q = lax.axis_index(("col", "sub"))
+    me_plane = lax.axis_index(("runs", "col"))
+    me_core = lax.axis_index("sub")
+    shares = lax.axis_size(("runs", "col", "sub"))
+    per = 2 * local * count // shares
+    dims = (bands, rows, cols, piece, local, count, block, per)
+
+    smem = pl.BlockSpec(memory_space=pltpu.SMEM)
+    vmem = pl.BlockSpec(memory_space=pltpu.VMEM)
+    start = q * per
+    share = jnp.where(
+        lax.axis_index("runs") == 0,
+        lax.dynamic_slice_in_dim(h_real.reshape(local * count, block, block), start, per, 0),
+        lax.dynamic_slice_in_dim(h_imag.reshape(local * count, block, block), start, per, 0),
+    ).reshape(per * block, block)
+    col_rows = jnp.pad(h_cols.astype(BF16), ((0, 16 - local), (0, block - count)))
+    message = jnp.concatenate([share, col_rows], axis=0)
+    mine = jnp.concatenate(
+        [h.transpose(0, 2, 1, 3).reshape(local, block, count * block) for h in (h_imag, h_real)], axis=1
+    )
+    arrived = [exchange(message, "row", k) for k in range(1, bands)]
+    all_cols = [
+        a[per * block : per * block + local, :count].astype(jnp.int32).reshape(-1) for a in [message] + arrived
+    ]
+    facts = jnp.concatenate([jnp.stack([r, q, me_plane, me_core]).astype(jnp.int32)] + all_cols)
+    theirs = jnp.stack([a[: per * block] for a in arrived])
+    near = jnp.stack([theirs] + [exchange(theirs, ("runs", "col"), k) for k in range(1, shares // 2)])
+    rest = [exchange(here, "row", k) for k in range(1, bands)]
+    far = exchange(near, "sub", 1)
+
+    step = 2 * order * 2 * count * block * 2 * cols
+    h_all, c_side = pl.pallas_call(
+        functools.partial(powers_kernel, dims),
+        out_shape=(
+            jax.ShapeDtypeStruct((bands * local, 2 * block, count * block), BF16),
+            jax.ShapeDtypeStruct((order, 6 * cols), BF16),
+        ),
+        in_specs=[smem] + [vmem] * 3,
+        out_specs=(vmem, vmem),
+        scratch_shapes=[
+            pltpu.VMEM((order, cols), BF16),
+            pltpu.VMEM((order, 2 * cols), BF16),
+            pltpu.VMEM((order, 2 * cols), BF16),
+            pltpu.VMEM((order, 2 * cols), F32),
+        ],
+        compiler_params=pltpu.CompilerParams(vmem_limit_bytes=POWERS_VMEM),
+        cost_estimate=pl.CostEstimate(flops=5 * step // 2, bytes_accessed=2**20, transcendentals=0),
+        name="powers",
+    )(facts, mine, near, far)
+    own, keep, send = pl.pallas_call(
+        functools.partial(main_kernel, dims),
+        out_shape=(
+            jax.ShapeDtypeStruct((rows, cols), F32),
+            jax.ShapeDtypeStruct((rows, cols), F32),
+            jax.ShapeDtypeStruct((2, rows, cols), BF16),
+        ),
+        in_specs=[smem] + [vmem] * (bands + 2),
+        out_specs=(vmem, vmem, vmem),
+        scratch_shapes=[
+            pltpu.VMEM((order, 2 * cols), BF16),
+            pltpu.VMEM((order, 2 * cols), BF16),
+            pltpu.VMEM((order, 2 * cols), BF16),
+            pltpu.VMEM((order, 2 * piece), F32),
+            pltpu.VMEM((rows, 2 * cols), F32),
+            pltpu.VMEM((2, rows, 12 * cols), BF16),
+            pltpu.VMEM((bands, rows, rows), F32),
+        ],
+        compiler_params=pltpu.CompilerParams(vmem_limit_bytes=MAIN_VMEM),
+        cost_estimate=pl.CostEstimate(flops=5 * step, bytes_accessed=2**20, transcendentals=0),
+        name="main",
+    )(facts, here, *rest, h_all, c_side)
+    swapped = exchange(send, "sub", 1)
+    across = exchange((keep + swapped[1].astype(F32)).astype(BF16), "col", 1)
+    total = here.astype(F32) + own + swapped[0].astype(F32) + across.astype(F32)
+    return total[None]
+
+
+def can_gather(mesh, local_packed, local_h):
+    bands = mesh.shape["row"]
+    rows, cols = local_packed[1], local_packed[2]
+    local, count, block = local_h[0], local_h[1], local_h[2]
+    shares = mesh.shape["runs"] * mesh.shape["col"] * mesh.shape["sub"]
+    return (
+        bands & (bands - 1) == 0
+        and mesh.shape["runs"] == mesh.shape["col"] == mesh.shape["sub"] == 2
+        and rows == cols == local * block
+        and (2 * local * count) % shares == 0
+        and local <= 16
+        and count <= block
+        and 80 * bands * rows * bands * rows // 2 <= VMEM_BYTES
+    )
+
+
+def body(mesh, packed, h_real, h_imag, h_cols):
+    if can_gather(mesh, packed.shape, h_real.shape):
+        return gathered_body(packed, h_real, h_imag, h_cols)
+    return banded_body(packed, h_real, h_imag, h_cols)
+
+
 def solution(mesh):
     in_specs = (
         P(("col", "sub"), ("runs", "row"), None),
@@ -101,4 +418,6 @@
         P("row", None),
     )
     out_specs = P(("col", "sub"), ("runs", "row"), None)
-    return jax.shard_map(body, mesh=mesh, in_specs=in_specs, out_specs=out_specs, check_vma=False)
+    return jax.shard_map(
+        functools.partial(body, mesh), mesh=mesh, in_specs=in_specs, out_specs=out_specs, check_vma=False
+    )

time: 148 us -> 48.8 us (0.33)
  waiting for transfers between devices: 61.6 us -> 14.7 us
  blocking collectives: 25.3 us -> 0 us
  between operations: 15.6 us -> 0.11 us
  Pallas kernels: 0 us -> 13 us
  local copies, waits for them, and re-layouts: 13.1 us -> 1.51 us
  starting transfers between devices: 27.9 us -> 16.7 us
    all_to_all x5 -> x0, waiting for transfers between devices: 30 us -> none  [the longest x4 26.3 us: mirror(): lax.all_to_all(turned, 'row', split_axis=1, concat_axis=1, tiled=True)]
    all_to_all x3 -> x0, blocking collectives: 25.3 us -> none  [mirror(): lax.all_to_all(split_rows, ('col', 'sub'), split_axis=1, concat_axis=1, t...]
    all_to_all x5 -> x0, starting transfers between devices: 19.8 us -> none  [the longest x4 15.6 us: mirror(): lax.all_to_all(turned, 'row', split_axis=1, concat_axis=1, tiled=True)]
    ppermute x6 -> x12, waiting for transfers between devices: 31.6 us -> 14.7 us  [exchange(): return lax.ppermute(block, axes, [(i, i ^ offset) for i in range(count)])]
    pallas_call x0 -> x2, Pallas kernels: none -> 13 us  [the longest x1 8.62 us: gathered_body(): pl.pallas_call(functools.partial(main_kernel, dims), out_shape=(jax.Shape...]
    ppermute x6 -> x12, starting transfers between devices: 8.1 us -> 16.7 us  [exchange(): return lax.ppermute(block, axes, [(i, i ^ offset) for i in range(count)])]
    slice x19 -> x0, local copies, waits for them, and re-layouts: 5.07 us -> none  [the longest x9 2.25 us: body(): mirror_part[0]]
    unnamed x37 -> x2, local copies, waits for them, and re-layouts: 2.32 us -> 0.01 us
  transfers between devices with their start and end apart: 11 -> 12, of which waited for: 10 -> 7; matrix products, arithmetic and copies ran while one was open for 1% -> 3% of each run, Pallas kernels for 0% -> 9%
where the time goes in v4:
time: 48.8 us; the launch traced here: 48.6 us
  starting transfers between devices  16.7 us (34%)
  waiting for transfers between devices  14.7 us (30%)
  Pallas kernels  13 us (27%)
  other arithmetic  2.54 us (5%)
  local copies, waits for them, and re-layouts  1.51 us (3%)
    ppermute x12, starting transfers between devices, exchange(): return lax.ppermute(block, axes, [(i, i ^ offset) for i in range(count)])  16.7 us
    ppermute x12, waiting for transfers between devices, exchange(): return lax.ppermute(block, axes, [(i, i ^ offset) for i in range(count)])  14.7 us
    pallas_call x1, Pallas kernels, gathered_body(): pl.pallas_call(functools.partial(main_kernel, dims), out_shape=(jax.Shape...  8.62 us
    pallas_call x1, Pallas kernels, gathered_body(): pl.pallas_call(functools.partial(powers_kernel, dims), out_shape=(jax.Sha...  4.36 us
    reshape x1, local copies, waits for them, and re-layouts, gathered_body(): h.transpose(0, 2, 1, 3).reshape(local, block, count * block)  1.09 us
  transfers between devices with their start and end apart: 12, of which 7 were waited for; matrix products, arithmetic and copies ran while one was open for 3% of the time, Pallas kernels for 9%

profile of v4, /device:TPU:0, one launch (start us, length us, event | category | flops | bytes accessed | tf_op | source)
XLA Modules:
  0.0 48.6 jit_solution(14493059568910261486)
XLA Ops:
  0.0 0.7 %fusion.6 = (s32[2,4]{1,0:T(2,128)S(1)}, bf16[2,4]{1,0:T(2,128)(2,1)S(1)}) fusion(s32[2,4]{1,0:T(2,128)} %param.7), kind=kLoop, calls=%fused_computation.23 | loop fusion | flops 16 | bytes 80 | tf_op jit(solution)/shard_map/reshape | solution.py:336
  0.7 0.9 %dynamic-slice_select_fusion = bf16[2,128,128]{2,1,0:T(8,128)(2,1)S(1)} fusion(bf16[8,128,128]{2,1,0:T(8,128)(2,1)} %bitcast.48, s32[]{:T(128)S(6)} %select_n.13, bf16[8,128,128]{2,1,0:T(8,128)(2,1)} %bitcast.49, pred[]{:T(512)S(6)} %eq.3), kind=kLoop, calls=%fused_computation.18 | loop fusion | flops 32768 | bytes 196613 | tf_op jit(solution)/shard_map/jit(_where)/select_n | solution.py:324
  1.6 5.1 %collective-permute-start.2 = (bf16[272,128]{1,0:T(8,128)(2,1)S(1)}, bf16[272,128]{1,0:T(8,128)(2,1)S(1)}, u32[]{:S(2)}, u32[]{:S(2)}) collective-permute-start(bf16[272,128]{1,0:T(8,128)(2,1)S(1)} %fusion.4), channel_id=1, source_target_pairs={{0,12},{4,8},{8,4},{12,0},{1,13},{5,9},{9,5},{13,1},{2,14},{6,10},... | collective-permute-start | bytes 208904 | tf_op jit(solution)/shard_map/ppermute | solution.py:109
  6.7 0.0 collective-permute-start.1
  6.7 0.6 %collective-permute-start = (bf16[272,128]{1,0:T(8,128)(2,1)S(1)}, bf16[272,128]{1,0:T(8,128)(2,1)S(1)}, u32[]{:S(2)}, u32[]{:S(2)}) collective-permute-start(bf16[272,128]{1,0:T(8,128)(2,1)S(1)} %fusion.4), channel_id=1, source_target_pairs={{0,4},{4,0},{8,12},{12,8},{1,5},{5,1},{9,13},{13,9},{2,6},{6,2},{1... | collective-permute-start | bytes 208904 | tf_op jit(solution)/shard_map/ppermute | solution.py:109
  7.3 1.4 %collective-permute-start.3 = (bf16[256,256]{1,0:T(8,128)(2,1)}, bf16[256,256]{1,0:T(8,128)(2,1)S(1)}, u32[]{:S(2)}, u32[]{:S(2)}) collective-permute-start(bf16[256,256]{1,0:T(8,128)(2,1)} %bitcast.44), channel_id=1, source_target_pairs={{0,4},{4,0},{8,12},{12,8},{1,5},{5,1},{9,13},{13,9},{2,6},{6,2},{1... | collective-permute-start | bytes 393224 | tf_op jit(solution)/shard_map/ppermute | solution.py:109
  8.7 2.9 %collective-permute-start.4 = (bf16[256,256]{1,0:T(8,128)(2,1)}, bf16[256,256]{1,0:T(8,128)(2,1)S(1)}, u32[]{:S(2)}, u32[]{:S(2)}) collective-permute-start(bf16[256,256]{1,0:T(8,128)(2,1)} %bitcast.45), channel_id=1, source_target_pairs={{0,8},{4,12},{8,0},{12,4},{1,9},{5,13},{9,1},{13,5},{2,10},{6,14},... | collective-permute-start | bytes 393224 | tf_op jit(solution)/shard_map/ppermute | solution.py:109
  11.7 0.1 reshape.61
  11.7 0.0 collective-permute-done.2
  11.7 1.6 %collective-permute-done.1 = bf16[272,128]{1,0:T(8,128)(2,1)S(1)} collective-permute-done((bf16[272,128]{1,0:T(8,128)(2,1)S(1)}, bf16[272,128]{1,0:T(8,128)(2,1)S(1)}, u32[]{:S(2)}, u32[]{:S(2)}) %collective-permute-start.1) | collective-permute-done | bytes 69664 | tf_op jit(solution)/shard_map/ppermute | solution.py:109
  13.3 1.1 %collective-permute-done = bf16[272,128]{1,0:T(8,128)(2,1)S(1)} collective-permute-done((bf16[272,128]{1,0:T(8,128)(2,1)S(1)}, bf16[272,128]{1,0:T(8,128)(2,1)S(1)}, u32[]{:S(2)}, u32[]{:S(2)}) %collective-permute-start) | collective-permute-done | bytes 69664 | tf_op jit(solution)/shard_map/ppermute | solution.py:109
  14.4 1.8 %collective-permute-start.6 = (bf16[3,256,128]{2,1,0:T(8,128)(2,1)S(1)}, bf16[3,256,128]{2,1,0:T(8,128)(2,1)S(1)}, u32[]{:S(2)}, u32[]{:S(2)}) collective-permute-start(bf16[3,256,128]{2,1,0:T(8,128)(2,1)S(1)} %get-tuple-element.18), channel_id=1, source_target_pairs={{0,2},{2,0},{16,18},{18,16},{1,3},{3,1},{17,19},{19,17},{4,6},{6,4... | collective-permute-start | bytes 589832 | tf_op jit(solution)/shard_map/ppermute | solution.py:109
  16.3 1.5 %collective-permute-start.7 = (bf16[3,256,128]{2,1,0:T(8,128)(2,1)S(1)}, bf16[3,256,128]{2,1,0:T(8,128)(2,1)S(1)}, u32[]{:S(2)}, u32[]{:S(2)}) collective-permute-start(bf16[3,256,128]{2,1,0:T(8,128)(2,1)S(1)} %get-tuple-element.18), channel_id=1, source_target_pairs={{0,16},{2,18},{16,0},{18,2},{1,17},{3,19},{17,1},{19,3},{4,20},{6,... | collective-permute-start | bytes 589832 | tf_op jit(solution)/shard_map/ppermute | solution.py:109
  17.8 0.2 collective-permute-start.8
  18.0 1.1 %copy_bitcast_fusion = (bf16[2,128,512]{2,1,0:T(8,128)(2,1)S(1)}, bf16[2,128,512]{2,1,0:T(8,128)(2,1)S(1)}) fusion(bf16[2,4,128,128]{3,2,1,0:T(8,128)(2,1)} %param.6, bf16[2,4,128,128]{3,2,1,0:T(8,128)(2,1)} %param.5), kind=kLoop, calls=%fused_computation.2 | loop fusion | bytes 1048576 | tf_op jit(solution)/shard_map/reshape | solution.py:332
  19.1 2.7 %collective-permute-done.6 = bf16[3,256,128]{2,1,0:T(8,128)(2,1)S(1)} collective-permute-done((bf16[3,256,128]{2,1,0:T(8,128)(2,1)S(1)}, bf16[3,256,128]{2,1,0:T(8,128)(2,1)S(1)}, u32[]{:S(2)}, u32[]{:S(2)}) %collective-permute-start.6) | collective-permute-done | bytes 196640 | tf_op jit(solution)/shard_map/ppermute | solution.py:109
  21.8 1.9 %collective-permute-start.5 = (bf16[256,256]{1,0:T(8,128)(2,1)}, bf16[256,256]{1,0:T(8,128)(2,1)S(1)}, u32[]{:S(2)}, u32[]{:S(2)}) collective-permute-start(bf16[256,256]{1,0:T(8,128)(2,1)} %bitcast.46), channel_id=1, source_target_pairs={{0,12},{4,8},{8,4},{12,0},{1,13},{5,9},{9,5},{13,1},{2,14},{6,10},... | collective-permute-start | bytes 393224 | tf_op jit(solution)/shard_map/ppermute | solution.py:109
  23.6 1.5 %collective-permute-done.7 = bf16[3,256,128]{2,1,0:T(8,128)(2,1)S(1)} collective-permute-done((bf16[3,256,128]{2,1,0:T(8,128)(2,1)S(1)}, bf16[3,256,128]{2,1,0:T(8,128)(2,1)S(1)}, u32[]{:S(2)}, u32[]{:S(2)}) %collective-permute-start.7) | collective-permute-done | bytes 196640 | tf_op jit(solution)/shard_map/ppermute | solution.py:109
  25.1 0.0 collective-permute-done.8
  25.1 0.1 pad_maximum_fusion.near_ref
  25.2 0.1 collective-permute-start.9
  25.3 0.1 reshape.63
  25.4 0.1 reshape.65
  25.5 0.1 reshape.67
  25.6 0.1 concatenate.10.facts
  25.7 0.0 copy-start
  25.7 1.9 %collective-permute-done.9.far_ref = bf16[4,3,256,128]{3,2,1,0:T(8,128)(2,1)S(1)} collective-permute-done((bf16[4,3,256,128]{3,2,1,0:T(8,128)(2,1)S(1)}, bf16[4,3,256,128]{3,2,1,0:T(8,128)(2,1)S(1)}, u32[]{:S(2)}, u32[]{:S(2)}) %collective-permute-start.9) | collective-permute-done | bytes 786464 | tf_op jit(solution)/shard_map/ppermute | solution.py:109
  27.6 4.4 %powers.1 = (bf16[8,256,512]{2,1,0:T(8,128)(2,1)S(1)}, bf16[1024,1536]{1,0:T(8,128)(2,1)S(1)}) custom-call(s32[36]{0:T(128)S(1)} %concatenate.10.facts, bf16[2,256,512]{2,1,0:T(8,128)(2,1)S(1)} %pad_maximum_fusion.1.mine_ref, bf16[4,3,256,128]{3,2,1,0:T(8,128)(2,1)S(1)} %pad_maximum_fusion.near_ref, bf16[4,3,256,128]{3,2,1,0:T(8,128)(2,1)S(1)} %collective-permute-done.9.far_ref), custom_call_target="tpu_custom_call" | custom-call | flops 2684354560 | bytes 1048576 | tf_op jit(solution)/shard_map/powers/pallas_call | solution.py:345
  31.9 0.0 collective-permute-done.3.refs_1_
  31.9 0.0 collective-permute-done.4.refs_2_
  31.9 0.0 collective-permute-done.5.refs_3_
  32.0 0.0 copy-done
  32.0 8.6 %main.1 = (f32[256,256]{1,0:T(8,128)S(1)}, f32[256,256]{1,0:T(8,128)S(1)}, bf16[2,256,256]{2,1,0:T(8,128)(2,1)S(1)}) custom-call(s32[36]{0:T(128)S(1)} %concatenate.10.facts, bf16[256,256]{1,0:T(8,128)(2,1)S(1)} %bitcast.47, bf16[256,256]{1,0:T(8,128)(2,1)S(1)} %collective-permute-done.3.refs_1_, bf16[256,256]{1,0:T(8,128)(2,1)S(1)} %collective-permute-done.4.refs_2_, ...), custom_call_target="tpu_custom_call" | custom-call | flops 5368709120 | bytes 1048576 | tf_op jit(solution)/shard_map/main/pallas_call | solution.py:363
  40.6 0.2 collective-permute-start.10
  40.8 1.4 %collective-permute-done.10 = bf16[2,256,256]{2,1,0:T(8,128)(2,1)S(1)} collective-permute-done((bf16[2,256,256]{2,1,0:T(8,128)(2,1)S(1)}, bf16[2,256,256]{2,1,0:T(8,128)(2,1)S(1)}, u32[]{:S(2)}, u32[]{:S(2)}) %collective-permute-start.10) | collective-permute-done | bytes 262176 | tf_op jit(solution)/shard_map/ppermute | solution.py:109
  42.2 1.0 %collective-permute-start.11 = (bf16[256,256]{1,0:T(8,128)(2,1)S(1)}, bf16[256,256]{1,0:T(8,128)(2,1)S(1)}, u32[]{:S(2)}, u32[]{:S(2)}) collective-permute-start(bf16[256,256]{1,0:T(8,128)(2,1)S(1)} %fusion), channel_id=1, source_target_pairs={{0,2},{2,0},{1,3},{3,1},{4,6},{6,4},{5,7},{7,5},{8,10},{10,8},{9,1... | collective-permute-start | bytes 393224 | tf_op jit(solution)/shard_map/ppermute | solution.py:109
  43.2 4.6 %collective-permute-done.11 = bf16[256,256]{1,0:T(8,128)(2,1)S(1)} collective-permute-done((bf16[256,256]{1,0:T(8,128)(2,1)S(1)}, bf16[256,256]{1,0:T(8,128)(2,1)S(1)}, u32[]{:S(2)}, u32[]{:S(2)}) %collective-permute-start.11) | collective-permute-done | bytes 131104 | tf_op jit(solution)/shard_map/ppermute | solution.py:109
  47.8 0.8 %fusion.2 = f32[1,256,256]{2,1,0:T(8,128)} fusion(bf16[256,256]{1,0:T(8,128)(2,1)S(1)} %collective-permute-done.11, f32[256,256]{1,0:T(8,128)S(1)} %get-tuple-element.12, bf16[2,256,256]{2,1,0:T(8,128)(2,1)S(1)} %collective-permute-done.10, bf16[1,256,256]{2,1,0:T(8,128)(2,1)S(1)} %copy-done), kind=kLoop, calls=%fused_computation.8 | loop fusion | flops 393216 | bytes 917504 | tf_op jit(solution)/shard_map/broadcast_in_dim | solution.py:388
  (10 shorter events, 0.1 us)
Async XLA Ops:
  1.6 10.2 %collective-permute-start.2 = (bf16[272,128]{1,0:T(8,128)(2,1)S(1)}, bf16[272,128]{1,0:T(8,128)(2,1)S(1)}, u32[]{:S(2)}, u32[]{:S(2)}) collective-permute-start(bf16[272,128]{1,0:T(8,128)(2,1)S(1)} %fusion.4), channel_id=1, source_target_pairs={{0,12},{4,8},{8,4},{12,0},{1,13},{5,9},{9,5},{13,1},{2,14},{6,10},... | collective-permute-start | bytes 208904 | tf_op jit(solution)/shard_map/ppermute | solution.py:109
  6.7 6.6 %collective-permute-start.1 = (bf16[272,128]{1,0:T(8,128)(2,1)S(1)}, bf16[272,128]{1,0:T(8,128)(2,1)S(1)}, u32[]{:S(2)}, u32[]{:S(2)}) collective-permute-start(bf16[272,128]{1,0:T(8,128)(2,1)S(1)} %fusion.4), channel_id=1, source_target_pairs={{0,8},{4,12},{8,0},{12,4},{1,9},{5,13},{9,1},{13,5},{2,10},{6,14},... | collective-permute-start | bytes 208904 | tf_op jit(solution)/shard_map/ppermute | solution.py:109
  6.7 7.7 %collective-permute-start = (bf16[272,128]{1,0:T(8,128)(2,1)S(1)}, bf16[272,128]{1,0:T(8,128)(2,1)S(1)}, u32[]{:S(2)}, u32[]{:S(2)}) collective-permute-start(bf16[272,128]{1,0:T(8,128)(2,1)S(1)} %fusion.4), channel_id=1, source_target_pairs={{0,4},{4,0},{8,12},{12,8},{1,5},{5,1},{9,13},{13,9},{2,6},{6,2},{1... | collective-permute-start | bytes 208904 | tf_op jit(solution)/shard_map/ppermute | solution.py:109
  7.3 24.6 %collective-permute-start.3 = (bf16[256,256]{1,0:T(8,128)(2,1)}, bf16[256,256]{1,0:T(8,128)(2,1)S(1)}, u32[]{:S(2)}, u32[]{:S(2)}) collective-permute-start(bf16[256,256]{1,0:T(8,128)(2,1)} %bitcast.44), channel_id=1, source_target_pairs={{0,4},{4,0},{8,12},{12,8},{1,5},{5,1},{9,13},{13,9},{2,6},{6,2},{1... | collective-permute-start | bytes 393224 | tf_op jit(solution)/shard_map/ppermute | solution.py:109
  8.7 23.2 %collective-permute-start.4 = (bf16[256,256]{1,0:T(8,128)(2,1)}, bf16[256,256]{1,0:T(8,128)(2,1)S(1)}, u32[]{:S(2)}, u32[]{:S(2)}) collective-permute-start(bf16[256,256]{1,0:T(8,128)(2,1)} %bitcast.45), channel_id=1, source_target_pairs={{0,8},{4,12},{8,0},{12,4},{1,9},{5,13},{9,1},{13,5},{2,10},{6,14},... | collective-permute-start | bytes 393224 | tf_op jit(solution)/shard_map/ppermute | solution.py:109
  14.4 7.3 %collective-permute-start.6 = (bf16[3,256,128]{2,1,0:T(8,128)(2,1)S(1)}, bf16[3,256,128]{2,1,0:T(8,128)(2,1)S(1)}, u32[]{:S(2)}, u32[]{:S(2)}) collective-permute-start(bf16[3,256,128]{2,1,0:T(8,128)(2,1)S(1)} %get-tuple-element.18), channel_id=1, source_target_pairs={{0,2},{2,0},{16,18},{18,16},{1,3},{3,1},{17,19},{19,17},{4,6},{6,4... | collective-permute-start | bytes 589832 | tf_op jit(solution)/shard_map/ppermute | solution.py:109
  16.3 8.8 %collective-permute-start.7 = (bf16[3,256,128]{2,1,0:T(8,128)(2,1)S(1)}, bf16[3,256,128]{2,1,0:T(8,128)(2,1)S(1)}, u32[]{:S(2)}, u32[]{:S(2)}) collective-permute-start(bf16[3,256,128]{2,1,0:T(8,128)(2,1)S(1)} %get-tuple-element.18), channel_id=1, source_target_pairs={{0,16},{2,18},{16,0},{18,2},{1,17},{3,19},{17,1},{19,3},{4,20},{6,... | collective-permute-start | bytes 589832 | tf_op jit(solution)/shard_map/ppermute | solution.py:109
  17.8 7.3 %collective-permute-start.8 = (bf16[3,256,128]{2,1,0:T(8,128)(2,1)S(1)}, bf16[3,256,128]{2,1,0:T(8,128)(2,1)S(1)}, u32[]{:S(2)}, u32[]{:S(2)}) collective-permute-start(bf16[3,256,128]{2,1,0:T(8,128)(2,1)S(1)} %get-tuple-element.18), channel_id=1, source_target_pairs={{0,18},{2,16},{16,2},{18,0},{1,19},{3,17},{17,3},{19,1},{4,22},{6,... | collective-permute-start | bytes 589832 | tf_op jit(solution)/shard_map/ppermute | solution.py:109
  21.8 10.2 %collective-permute-start.5 = (bf16[256,256]{1,0:T(8,128)(2,1)}, bf16[256,256]{1,0:T(8,128)(2,1)S(1)}, u32[]{:S(2)}, u32[]{:S(2)}) collective-permute-start(bf16[256,256]{1,0:T(8,128)(2,1)} %bitcast.46), channel_id=1, source_target_pairs={{0,12},{4,8},{8,4},{12,0},{1,13},{5,9},{9,5},{13,1},{2,14},{6,10},... | collective-permute-start | bytes 393224 | tf_op jit(solution)/shard_map/ppermute | solution.py:109
  25.2 2.4 %collective-permute-start.9 = (bf16[4,3,256,128]{3,2,1,0:T(8,128)(2,1)S(1)}, bf16[4,3,256,128]{3,2,1,0:T(8,128)(2,1)S(1)}, u32[]{:S(2)}, u32[]{:S(2)}) collective-permute-start(bf16[4,3,256,128]{3,2,1,0:T(8,128)(2,1)S(1)} %pad_maximum_fusion.near_ref), channel_id=1, source_target_pairs={{0,1},{1,0},{2,3},{3,2},{4,5},{5,4},{6,7},{7,6},{8,9},{9,8},{10,11... | collective-permute-start | bytes 2359304 | tf_op jit(solution)/shard_map/ppermute | solution.py:109
  25.7 6.3 %copy-start = (bf16[1,256,256]{2,1,0:T(8,128)(2,1)S(1)}, bf16[1,256,256]{2,1,0:T(8,128)(2,1)}, u32[]{:S(2)}) copy-start(bf16[1,256,256]{2,1,0:T(8,128)(2,1)} %param.4) | copy-start | bytes 393220
  40.6 1.6 %collective-permute-start.10 = (bf16[2,256,256]{2,1,0:T(8,128)(2,1)S(1)}, bf16[2,256,256]{2,1,0:T(8,128)(2,1)S(1)}, u32[]{:S(2)}, u32[]{:S(2)}) collective-permute-start(bf16[2,256,256]{2,1,0:T(8,128)(2,1)S(1)} %get-tuple-element.13), channel_id=1, source_target_pairs={{0,1},{1,0},{2,3},{3,2},{4,5},{5,4},{6,7},{7,6},{8,9},{9,8},{10,11... | collective-permute-start | bytes 786440 | tf_op jit(solution)/shard_map/ppermute | solution.py:109
  42.2 5.6 %collective-permute-start.11 = (bf16[256,256]{1,0:T(8,128)(2,1)S(1)}, bf16[256,256]{1,0:T(8,128)(2,1)S(1)}, u32[]{:S(2)}, u32[]{:S(2)}) collective-permute-start(bf16[256,256]{1,0:T(8,128)(2,1)S(1)} %fusion), channel_id=1, source_target_pairs={{0,2},{2,0},{1,3},{3,1},{4,6},{6,4},{5,7},{7,5},{8,10},{10,8},{9,1... | collective-permute-start | bytes 393224 | tf_op jit(solution)/shard_map/ppermute | solution.py:109

commit v5 on v4

--- a/solution.py
+++ b/solution.py
@@ -99,7 +99,8 @@
 
 VMEM_BYTES = 56 * 2**20
 POWERS_VMEM = 20 * 2**20
-MAIN_VMEM = 24 * 2**20
+MAIN_VMEM = 22 * 2**20
+OWN_VMEM = 14 * 2**20
 F32 = jnp.float32
 BF16 = jnp.bfloat16
 
@@ -188,17 +189,62 @@
     return value
 
 
+def products(dims, facts, wanted, c_ref, n_ref, v1_ref, v2_ref, left, slab, outs):
+    bands, rows, cols, piece, local, count, block, per = dims
+    r, q = facts[0], facts[1]
+    nt = (((1,), (1,)), ((), ()))
+    size = len(wanted) * piece
+    spans = [
+        [pl.ds(pl.multiple_of(k * rows + p * piece, piece), piece) for p in wanted] for k in range(bands)
+    ]
+    i_own = lax.broadcasted_iota(jnp.int32, (piece, rows), 1)
+    j_own = lax.broadcasted_iota(jnp.int32, (piece, rows), 0)
+    upper = jnp.concatenate([i_own <= p * piece + j_own for p in wanted], axis=0)
+    mine = lax.broadcasted_iota(jnp.int32, (size, rows), 1) // piece == q
+
+    def against(which, slots):
+        right = jnp.concatenate(
+            [
+                jnp.concatenate([ref[span, :] for ref in (c_ref, n_ref, v1_ref, v2_ref)], axis=1)
+                for k in slots
+                for span in spans[k]
+            ],
+            axis=0,
+        )
+        return lax.dot_general(right, left[which], nt, preferred_element_type=F32)
+
+    for k in range(0, bands, 2):
+        if k == 0:
+            next_side = (lax.bitwise_xor(r, 1) < r).astype(jnp.int32)
+            got = [jnp.where(upper, against(0, (0,)), against(1, (0,))), against(next_side, (1,))]
+        else:
+            side = against((lax.bitwise_xor(r, k) < r).astype(jnp.int32), (k, k + 1))
+            got = [side[:size], side[size:]]
+        for n in (0, 1):
+            thin = jnp.concatenate([slab[span, :] for span in spans[k + n]], axis=0)
+            real = jnp.concatenate([thin[:, :piece]] * (rows // piece), axis=1)
+            imag = jnp.concatenate([-thin[:, piece:]] * (rows // piece), axis=1)
+            above = upper if k + n == 0 else lax.bitwise_xor(r, k + n) > r
+            outs[k + n] = got[n] + jnp.where(mine, jnp.where(above, real, imag), 0.0)
+
+    def target(n):
+        return jnp.concatenate(
+            [outs[lax.bitwise_xor(r, b), n * piece : (n + 1) * piece, :] for b in range(bands)], axis=0
+        ).T
+
+    return target
+
+
 def main_kernel(dims, facts, *refs):
     bands, rows, cols, piece, local, count, block, per = dims
     f_refs = refs[:bands]
-    h_ref, c_ref, own_ref, keep_ref, send_ref, n_ref, v1_ref, v2_ref, slab, tops, left, outs = refs[bands:]
-    pieces = rows // piece
+    h_ref, c_ref, keep_ref, send_ref, n_ref, v1_ref, v2_ref, left, slab, tops, outs = refs[bands:]
     r, q = facts[0], facts[1]
     row_iota = lax.broadcasted_iota(jnp.int32, (rows, cols), 0)
     col_iota = lax.broadcasted_iota(jnp.int32, (rows, cols), 1)
     col_abs = col_iota // piece * rows + q * piece + col_iota % piece
     for k in range(bands):
-        here = f_refs[k][...].astype(F32)
+        here = f_refs[-k % bands][...].astype(F32)
         row_abs = lax.bitwise_xor(r, k) * rows + row_iota
         real = jnp.where(row_abs < col_abs, here, jnp.where(row_abs == col_abs, 0.5 * here, 0.0))
         imag = jnp.where(row_abs > col_abs, here, 0.0)
@@ -254,53 +300,24 @@
             left[which, :, three + m * cols : three + (m + 1) * cols] = second
             left[which, :, 2 * three + 2 * m * cols : 2 * three + (2 * m + 1) * cols] = third
             left[which, :, 2 * three + (2 * m + 1) * cols : 2 * three + (2 * m + 2) * cols] = fourth
-    nt = (((1,), (1,)), ((), ()))
-
-    def against(which, k):
-        span = slice(k * rows, (k + 1) * rows)
-        right = jnp.concatenate([ref[span, :] for ref in (c_ref, n_ref, v1_ref, v2_ref)], axis=1)
-        return lax.dot_general(left[which], right, nt, preferred_element_type=F32)
-
-    upper = row_iota[:, :rows] <= lax.broadcasted_iota(jnp.int32, (rows, rows), 1)
-    mine = pl.ds(pl.multiple_of(q * piece, piece), piece)
-    thin_row = q * piece + lax.broadcasted_iota(jnp.int32, (piece, rows), 0)
-    thin_upper = thin_row <= lax.broadcasted_iota(jnp.int32, (piece, rows), 1)
-    outs[0] = jnp.where(upper, against(0, 0), against(1, 0))
-    for k in range(1, bands):
-        lower = (lax.bitwise_xor(r, k) < r).astype(jnp.int32)
-        outs[k] = against(lower, k)
-    for k in range(bands):
-        turned = slab[k * rows : (k + 1) * rows, :].T
-        real, imag = turned[:piece], -turned[piece:]
-        if k == 0:
-            extra = jnp.where(thin_upper, real, imag)
-        else:
-            extra = jnp.where(lax.bitwise_xor(r, k) > r, real, imag)
-        outs[k, mine, :] += extra
-
-    def target(piece_index):
-        return jnp.concatenate(
-            [outs[lax.bitwise_xor(r, b)][:, piece_index * piece : (piece_index + 1) * piece] for b in range(bands)],
-            axis=1,
-        )
-
-    for p in range(pieces):
-        offset = lax.bitwise_xor(q, p)
-        value = target(p)
-
-        @pl.when(offset == 0)
-        def _():
-            real = swap_groups(tops[:, :cols], r, piece)
-            imag = swap_groups(tops[:, cols:], r, piece)
-            own_ref[...] = value + jnp.where(r * rows + row_iota <= col_abs, real, imag)
-
-        @pl.when(offset == 2)
-        def _():
-            keep_ref[...] = value
-
-        @pl.when(offset % 2 == 1)
-        def _():
-            send_ref[offset // 2] = value.astype(BF16)
+    far = lax.bitwise_xor(q, 2)
+    wanted = (lax.bitwise_xor(far, 1), lax.bitwise_xor(q, 1), far)
+    target = products(dims, facts, wanted, c_ref, n_ref, v1_ref, v2_ref, left, slab, outs)
+    send_ref[0] = target(0).astype(BF16)
+    send_ref[1] = target(1).astype(BF16)
+    keep_ref[...] = target(2)
+
+
+def own_kernel(dims, facts, c_ref, n_ref, v1_ref, v2_ref, left, slab, tops, own_ref, outs):
+    bands, rows, cols, piece, local, count, block, per = dims
+    r, q = facts[0], facts[1]
+    target = products(dims, facts, (q,), c_ref, n_ref, v1_ref, v2_ref, left, slab, outs)
+    col_iota = lax.broadcasted_iota(jnp.int32, (rows, cols), 1)
+    col_abs = col_iota // piece * rows + q * piece + col_iota % piece
+    row_abs = r * rows + lax.broadcasted_iota(jnp.int32, (rows, cols), 0)
+    real = swap_groups(tops[:, :cols], r, piece)
+    imag = swap_groups(tops[:, cols:], r, piece)
+    own_ref[...] = target(0) + jnp.where(row_abs <= col_abs, real, imag)
 
 
 def gathered_body(packed, h_real, h_imag, h_cols):
@@ -338,7 +355,7 @@
     facts = jnp.concatenate([jnp.stack([r, q, me_plane, me_core]).astype(jnp.int32)] + all_cols)
     theirs = jnp.stack([a[: per * block] for a in arrived])
     near = jnp.stack([theirs] + [exchange(theirs, ("runs", "col"), k) for k in range(1, shares // 2)])
-    rest = [exchange(here, "row", k) for k in range(1, bands)]
+    rest = [exchange(here, "row", k) for k in range(bands - 1, 0, -1)]
     far = exchange(near, "sub", 1)
 
     step = 2 * order * 2 * count * block * 2 * cols
@@ -360,31 +377,40 @@
         cost_estimate=pl.CostEstimate(flops=5 * step // 2, bytes_accessed=2**20, transcendentals=0),
         name="powers",
     )(facts, mine, near, far)
-    own, keep, send = pl.pallas_call(
+    block_shape = jax.ShapeDtypeStruct((rows, cols), F32)
+    v_shape = jax.ShapeDtypeStruct((order, 2 * cols), BF16)
+    keep, send, *state = pl.pallas_call(
         functools.partial(main_kernel, dims),
         out_shape=(
-            jax.ShapeDtypeStruct((rows, cols), F32),
-            jax.ShapeDtypeStruct((rows, cols), F32),
+            block_shape,
             jax.ShapeDtypeStruct((2, rows, cols), BF16),
+            v_shape,
+            v_shape,
+            v_shape,
+            jax.ShapeDtypeStruct((2, rows, 12 * cols), BF16),
+            jax.ShapeDtypeStruct((order, 2 * piece), F32),
+            jax.ShapeDtypeStruct((rows, 2 * cols), F32),
         ),
         in_specs=[smem] + [vmem] * (bands + 2),
-        out_specs=(vmem, vmem, vmem),
-        scratch_shapes=[
-            pltpu.VMEM((order, 2 * cols), BF16),
-            pltpu.VMEM((order, 2 * cols), BF16),
-            pltpu.VMEM((order, 2 * cols), BF16),
-            pltpu.VMEM((order, 2 * piece), F32),
-            pltpu.VMEM((rows, 2 * cols), F32),
-            pltpu.VMEM((2, rows, 12 * cols), BF16),
-            pltpu.VMEM((bands, rows, rows), F32),
-        ],
+        out_specs=(vmem,) * 8,
+        scratch_shapes=[pltpu.VMEM((bands, 3 * piece, rows), F32)],
         compiler_params=pltpu.CompilerParams(vmem_limit_bytes=MAIN_VMEM),
-        cost_estimate=pl.CostEstimate(flops=5 * step, bytes_accessed=2**20, transcendentals=0),
+        cost_estimate=pl.CostEstimate(flops=4 * step, bytes_accessed=2**20, transcendentals=0),
         name="main",
     )(facts, here, *rest, h_all, c_side)
     swapped = exchange(send, "sub", 1)
-    across = exchange((keep + swapped[1].astype(F32)).astype(BF16), "col", 1)
-    total = here.astype(F32) + own + swapped[0].astype(F32) + across.astype(F32)
+    across = exchange((keep + swapped[0].astype(F32)).astype(BF16), "col", 1)
+    own = pl.pallas_call(
+        functools.partial(own_kernel, dims),
+        out_shape=block_shape,
+        in_specs=[smem] + [vmem] * 7,
+        out_specs=vmem,
+        scratch_shapes=[pltpu.VMEM((bands, piece, rows), F32)],
+        compiler_params=pltpu.CompilerParams(vmem_limit_bytes=OWN_VMEM),
+        cost_estimate=pl.CostEstimate(flops=step, bytes_accessed=2**20, transcendentals=0),
+        name="own",
+    )(facts, c_side, *state)
+    total = here.astype(F32) + own + swapped[1].astype(F32) + across.astype(F32)
     return total[None]
 
 
@@ -395,6 +421,7 @@
     shares = mesh.shape["runs"] * mesh.shape["col"] * mesh.shape["sub"]
     return (
         bands & (bands - 1) == 0
+        and bands > 1
         and mesh.shape["runs"] == mesh.shape["col"] == mesh.shape["sub"] == 2
         and rows == cols == local * block
         and (2 * local * count) % shares == 0

time: 48.8 us -> 47.2 us (0.967)
  waiting for transfers between devices: 14.7 us -> 11.2 us
  Pallas kernels: 13 us -> 14.4 us
  starting transfers between devices: 16.7 us -> 17.3 us
    ppermute x12, waiting for transfers between devices: 14.7 us -> 11.2 us  [exchange(): return lax.ppermute(block, axes, [(i, i ^ offset) for i in range(count)])]
    pallas_call x1 -> x2, Pallas kernels: 8.62 us -> 10.1 us  [the longest x1 7.33 us: gathered_body(): pl.pallas_call(functools.partial(main_kernel, dims), out_shape=(block_sha...]
    ppermute x12, starting transfers between devices: 16.7 us -> 17.3 us  [exchange(): return lax.ppermute(block, axes, [(i, i ^ offset) for i in range(count)])]
  transfers between devices with their start and end apart: 12 -> 12, of which waited for: 7 -> 7; matrix products, arithmetic and copies ran while one was open for 3% -> 4% of each run, Pallas kernels for 9% -> 15%
where the time goes in v5:
time: 47.2 us; the launch traced here: 47.1 us
  starting transfers between devices  17.3 us (37%)
  Pallas kernels  14.4 us (31%)
  waiting for transfers between devices  11.2 us (24%)
  other arithmetic  2.54 us (5%)
  local copies, waits for them, and re-layouts  1.51 us (3%)
    ppermute x12, starting transfers between devices, exchange(): return lax.ppermute(block, axes, [(i, i ^ offset) for i in range(count)])  17.3 us
    ppermute x12, waiting for transfers between devices, exchange(): return lax.ppermute(block, axes, [(i, i ^ offset) for i in range(count)])  11.2 us
    pallas_call x1, Pallas kernels, gathered_body(): pl.pallas_call(functools.partial(main_kernel, dims), out_shape=(block_sha...  7.33 us
    pallas_call x1, Pallas kernels, gathered_body(): pl.pallas_call(functools.partial(powers_kernel, dims), out_shape=(jax.Sha...  4.36 us
    pallas_call x1, Pallas kernels, gathered_body(): pl.pallas_call(functools.partial(own_kernel, dims), out_shape=block_shape...  2.73 us
    reshape x1, local copies, waits for them, and re-layouts, gathered_body(): h.transpose(0, 2, 1, 3).reshape(local, block, count * block)  1.09 us
  transfers between devices with their start and end apart: 12, of which 7 were waited for; matrix products, arithmetic and copies ran while one was open for 4% of the time, Pallas kernels for 15%

profile of v5, /device:TPU:0, one launch (start us, length us, event | category | flops | bytes accessed | tf_op | source)
XLA Modules:
  0.0 47.1 jit_solution(11306755295213904300)
XLA Ops:
  0.0 0.7 %fusion.6 = (s32[2,4]{1,0:T(2,128)S(1)}, bf16[2,4]{1,0:T(2,128)(2,1)S(1)}) fusion(s32[2,4]{1,0:T(2,128)} %param.7), kind=kLoop, calls=%fused_computation.23 | loop fusion | flops 16 | bytes 80 | tf_op jit(solution)/shard_map/reshape | solution.py:353
  0.7 0.9 %dynamic-slice_select_fusion = bf16[2,128,128]{2,1,0:T(8,128)(2,1)S(1)} fusion(bf16[8,128,128]{2,1,0:T(8,128)(2,1)} %bitcast.48, s32[]{:T(128)S(6)} %select_n.13, bf16[8,128,128]{2,1,0:T(8,128)(2,1)} %bitcast.49, pred[]{:T(512)S(6)} %eq.3), kind=kLoop, calls=%fused_computation.18 | loop fusion | flops 32768 | bytes 196613 | tf_op jit(solution)/shard_map/jit(_where)/select_n | solution.py:341
  1.6 5.1 %collective-permute-start.2 = (bf16[272,128]{1,0:T(8,128)(2,1)S(1)}, bf16[272,128]{1,0:T(8,128)(2,1)S(1)}, u32[]{:S(2)}, u32[]{:S(2)}) collective-permute-start(bf16[272,128]{1,0:T(8,128)(2,1)S(1)} %fusion.4), channel_id=1, source_target_pairs={{0,12},{4,8},{8,4},{12,0},{1,13},{5,9},{9,5},{13,1},{2,14},{6,10},... | collective-permute-start | bytes 208904 | tf_op jit(solution)/shard_map/ppermute | solution.py:110
  6.7 0.0 collective-permute-start.1
  6.7 0.6 %collective-permute-start = (bf16[272,128]{1,0:T(8,128)(2,1)S(1)}, bf16[272,128]{1,0:T(8,128)(2,1)S(1)}, u32[]{:S(2)}, u32[]{:S(2)}) collective-permute-start(bf16[272,128]{1,0:T(8,128)(2,1)S(1)} %fusion.4), channel_id=1, source_target_pairs={{0,4},{4,0},{8,12},{12,8},{1,5},{5,1},{9,13},{13,9},{2,6},{6,2},{1... | collective-permute-start | bytes 208904 | tf_op jit(solution)/shard_map/ppermute | solution.py:110
  7.3 1.4 %collective-permute-start.9 = (bf16[256,256]{1,0:T(8,128)(2,1)}, bf16[256,256]{1,0:T(8,128)(2,1)S(1)}, u32[]{:S(2)}, u32[]{:S(2)}) collective-permute-start(bf16[256,256]{1,0:T(8,128)(2,1)} %bitcast.44), channel_id=1, source_target_pairs={{0,4},{4,0},{8,12},{12,8},{1,5},{5,1},{9,13},{13,9},{2,6},{6,2},{1... | collective-permute-start | bytes 393224 | tf_op jit(solution)/shard_map/ppermute | solution.py:110
  8.7 2.9 %collective-permute-start.8 = (bf16[256,256]{1,0:T(8,128)(2,1)}, bf16[256,256]{1,0:T(8,128)(2,1)S(1)}, u32[]{:S(2)}, u32[]{:S(2)}) collective-permute-start(bf16[256,256]{1,0:T(8,128)(2,1)} %bitcast.45), channel_id=1, source_target_pairs={{0,8},{4,12},{8,0},{12,4},{1,9},{5,13},{9,1},{13,5},{2,10},{6,14},... | collective-permute-start | bytes 393224 | tf_op jit(solution)/shard_map/ppermute | solution.py:110
  11.7 0.1 reshape.61
  11.7 0.0 collective-permute-done.2
  11.7 1.6 %collective-permute-done.1 = bf16[272,128]{1,0:T(8,128)(2,1)S(1)} collective-permute-done((bf16[272,128]{1,0:T(8,128)(2,1)S(1)}, bf16[272,128]{1,0:T(8,128)(2,1)S(1)}, u32[]{:S(2)}, u32[]{:S(2)}) %collective-permute-start.1) | collective-permute-done | bytes 69664 | tf_op jit(solution)/shard_map/ppermute | solution.py:110
  13.3 1.1 %collective-permute-done = bf16[272,128]{1,0:T(8,128)(2,1)S(1)} collective-permute-done((bf16[272,128]{1,0:T(8,128)(2,1)S(1)}, bf16[272,128]{1,0:T(8,128)(2,1)S(1)}, u32[]{:S(2)}, u32[]{:S(2)}) %collective-permute-start) | collective-permute-done | bytes 69664 | tf_op jit(solution)/shard_map/ppermute | solution.py:110
  14.4 1.9 %collective-permute-start.4 = (bf16[3,256,128]{2,1,0:T(8,128)(2,1)S(1)}, bf16[3,256,128]{2,1,0:T(8,128)(2,1)S(1)}, u32[]{:S(2)}, u32[]{:S(2)}) collective-permute-start(bf16[3,256,128]{2,1,0:T(8,128)(2,1)S(1)} %get-tuple-element.28), channel_id=1, source_target_pairs={{0,16},{2,18},{16,0},{18,2},{1,17},{3,19},{17,1},{19,3},{4,20},{6,... | collective-permute-start | bytes 589832 | tf_op jit(solution)/shard_map/ppermute | solution.py:110
  16.3 1.5 %collective-permute-start.3 = (bf16[3,256,128]{2,1,0:T(8,128)(2,1)S(1)}, bf16[3,256,128]{2,1,0:T(8,128)(2,1)S(1)}, u32[]{:S(2)}, u32[]{:S(2)}) collective-permute-start(bf16[3,256,128]{2,1,0:T(8,128)(2,1)S(1)} %get-tuple-element.28), channel_id=1, source_target_pairs={{0,2},{2,0},{16,18},{18,16},{1,3},{3,1},{17,19},{19,17},{4,6},{6,4... | collective-permute-start | bytes 589832 | tf_op jit(solution)/shard_map/ppermute | solution.py:110
  17.8 0.2 collective-permute-start.5
  18.0 1.1 %copy_bitcast_fusion = (bf16[2,128,512]{2,1,0:T(8,128)(2,1)S(1)}, bf16[2,128,512]{2,1,0:T(8,128)(2,1)S(1)}) fusion(bf16[2,4,128,128]{3,2,1,0:T(8,128)(2,1)} %param.6, bf16[2,4,128,128]{3,2,1,0:T(8,128)(2,1)} %param.5), kind=kLoop, calls=%fused_computation.2 | loop fusion | bytes 1048576 | tf_op jit(solution)/shard_map/reshape | solution.py:349
  19.1 3.2 %collective-permute-done.4 = bf16[3,256,128]{2,1,0:T(8,128)(2,1)S(1)} collective-permute-done((bf16[3,256,128]{2,1,0:T(8,128)(2,1)S(1)}, bf16[3,256,128]{2,1,0:T(8,128)(2,1)S(1)}, u32[]{:S(2)}, u32[]{:S(2)}) %collective-permute-start.4) | collective-permute-done | bytes 196640 | tf_op jit(solution)/shard_map/ppermute | solution.py:110
  22.3 1.9 %collective-permute-start.7 = (bf16[256,256]{1,0:T(8,128)(2,1)}, bf16[256,256]{1,0:T(8,128)(2,1)S(1)}, u32[]{:S(2)}, u32[]{:S(2)}) collective-permute-start(bf16[256,256]{1,0:T(8,128)(2,1)} %bitcast.46), channel_id=1, source_target_pairs={{0,12},{4,8},{8,4},{12,0},{1,13},{5,9},{9,5},{13,1},{2,14},{6,10},... | collective-permute-start | bytes 393224 | tf_op jit(solution)/shard_map/ppermute | solution.py:110
  24.1 0.0 collective-permute-done.3
  24.1 0.7 %collective-permute-done.5 = bf16[3,256,128]{2,1,0:T(8,128)(2,1)S(1)} collective-permute-done((bf16[3,256,128]{2,1,0:T(8,128)(2,1)S(1)}, bf16[3,256,128]{2,1,0:T(8,128)(2,1)S(1)}, u32[]{:S(2)}, u32[]{:S(2)}) %collective-permute-start.5) | collective-permute-done | bytes 196640 | tf_op jit(solution)/shard_map/ppermute | solution.py:110
  24.9 0.1 pad_maximum_fusion.near_ref
  25.0 0.1 collective-permute-start.6
  25.1 0.1 reshape.67
  25.2 0.1 reshape.65
  25.3 0.1 reshape.63
  25.4 0.1 concatenate.10.facts
  25.4 0.0 copy-start
  25.4 1.9 %collective-permute-done.6.far_ref = bf16[4,3,256,128]{3,2,1,0:T(8,128)(2,1)S(1)} collective-permute-done((bf16[4,3,256,128]{3,2,1,0:T(8,128)(2,1)S(1)}, bf16[4,3,256,128]{3,2,1,0:T(8,128)(2,1)S(1)}, u32[]{:S(2)}, u32[]{:S(2)}) %collective-permute-start.6) | collective-permute-done | bytes 786464 | tf_op jit(solution)/shard_map/ppermute | solution.py:110
  27.3 4.4 %powers.1 = (bf16[8,256,512]{2,1,0:T(8,128)(2,1)S(1)}, bf16[1024,1536]{1,0:T(8,128)(2,1)S(1)}) custom-call(s32[36]{0:T(128)S(1)} %concatenate.10.facts, bf16[2,256,512]{2,1,0:T(8,128)(2,1)S(1)} %pad_maximum_fusion.1.mine_ref, bf16[4,3,256,128]{3,2,1,0:T(8,128)(2,1)S(1)} %pad_maximum_fusion.near_ref, bf16[4,3,256,128]{3,2,1,0:T(8,128)(2,1)S(1)} %collective-permute-done.6.far_ref), custom_call_target="tpu_custom_call" | custom-call | flops 2684354560 | bytes 1048576 | tf_op jit(solution)/shard_map/powers/pallas_call | solution.py:362
  31.7 0.0 collective-permute-done.9.refs_3_
  31.7 0.0 collective-permute-done.8.refs_2_
  31.7 0.0 collective-permute-done.7.refs_1_
  31.7 0.0 copy-done
  31.7 7.3 %main.1 = (f32[256,256]{1,0:T(8,128)S(1)}, bf16[2,256,256]{2,1,0:T(8,128)(2,1)S(1)}, bf16[1024,512]{1,0:T(8,128)(2,1)S(1)}, bf16[1024,512]{1,0:T(8,128)(2,1)S(1)...) custom-call(s32[36]{0:T(128)S(1)} %concatenate.10.facts, ...), custom_call_target="tpu_custom_call" | custom-call | flops 4294967296 | bytes 1048576 | tf_op jit(solution)/shard_map/main/pallas_call | solution.py:382
  39.1 0.2 collective-permute-start.10
  39.3 1.4 %collective-permute-done.10 = bf16[2,256,256]{2,1,0:T(8,128)(2,1)S(1)} collective-permute-done((bf16[2,256,256]{2,1,0:T(8,128)(2,1)S(1)}, bf16[2,256,256]{2,1,0:T(8,128)(2,1)S(1)}, u32[]{:S(2)}, u32[]{:S(2)}) %collective-permute-start.10) | collective-permute-done | bytes 262176 | tf_op jit(solution)/shard_map/ppermute | solution.py:110
  40.7 1.5 %collective-permute-start.11 = (bf16[256,256]{1,0:T(8,128)(2,1)S(1)}, bf16[256,256]{1,0:T(8,128)(2,1)S(1)}, u32[]{:S(2)}, u32[]{:S(2)}) collective-permute-start(bf16[256,256]{1,0:T(8,128)(2,1)S(1)} %fusion), channel_id=1, source_target_pairs={{0,2},{2,0},{1,3},{3,1},{4,6},{6,4},{5,7},{7,5},{8,10},{10,8},{9,1... | collective-permute-start | bytes 393224 | tf_op jit(solution)/shard_map/ppermute | solution.py:110
  42.2 2.7 %own.1 = f32[256,256]{1,0:T(8,128)S(1)} custom-call(s32[36]{0:T(128)S(1)} %concatenate.10.facts, bf16[1024,1536]{1,0:T(8,128)(2,1)S(1)} %get-tuple-element.15.refs_5_.c_ref, bf16[1024,512]{1,0:T(8,128)(2,1)S(1)} %get-tuple-element.17.n_ref, bf16[1024,512]{1,0:T(8,128)(2,1)S(1)} %get-tuple-element.18.v1_ref, bf16[1024,512]{1,0:T(8,128)(2,1)S(1)} %get-tuple-element.19.v2_ref, ...), custom_call_target="tpu_custom_call" | custom-call | flops 1073741824 | bytes 1048576 | tf_op jit(solution)/shard_map/own/pallas_call | solution.py:403
  44.9 1.4 %collective-permute-done.11 = bf16[256,256]{1,0:T(8,128)(2,1)S(1)} collective-permute-done((bf16[256,256]{1,0:T(8,128)(2,1)S(1)}, bf16[256,256]{1,0:T(8,128)(2,1)S(1)}, u32[]{:S(2)}, u32[]{:S(2)}) %collective-permute-start.11) | collective-permute-done | bytes 131104 | tf_op jit(solution)/shard_map/ppermute | solution.py:110
  46.3 0.8 %fusion.2 = f32[1,256,256]{2,1,0:T(8,128)} fusion(bf16[256,256]{1,0:T(8,128)(2,1)S(1)} %collective-permute-done.11, f32[256,256]{1,0:T(8,128)S(1)} %own.1, bf16[2,256,256]{2,1,0:T(8,128)(2,1)S(1)} %collective-permute-done.10, bf16[1,256,256]{2,1,0:T(8,128)(2,1)S(1)} %copy-done), kind=kLoop, calls=%fused_computation.8 | loop fusion | flops 393216 | bytes 917504 | tf_op jit(solution)/shard_map/broadcast_in_dim | solution.py:414
  (10 shorter events, 0.1 us)
Async XLA Ops:
  1.6 10.2 %collective-permute-start.2 = (bf16[272,128]{1,0:T(8,128)(2,1)S(1)}, bf16[272,128]{1,0:T(8,128)(2,1)S(1)}, u32[]{:S(2)}, u32[]{:S(2)}) collective-permute-start(bf16[272,128]{1,0:T(8,128)(2,1)S(1)} %fusion.4), channel_id=1, source_target_pairs={{0,12},{4,8},{8,4},{12,0},{1,13},{5,9},{9,5},{13,1},{2,14},{6,10},... | collective-permute-start | bytes 208904 | tf_op jit(solution)/shard_map/ppermute | solution.py:110
  6.7 6.6 %collective-permute-start.1 = (bf16[272,128]{1,0:T(8,128)(2,1)S(1)}, bf16[272,128]{1,0:T(8,128)(2,1)S(1)}, u32[]{:S(2)}, u32[]{:S(2)}) collective-permute-start(bf16[272,128]{1,0:T(8,128)(2,1)S(1)} %fusion.4), channel_id=1, source_target_pairs={{0,8},{4,12},{8,0},{12,4},{1,9},{5,13},{9,1},{13,5},{2,10},{6,14},... | collective-permute-start | bytes 208904 | tf_op jit(solution)/shard_map/ppermute | solution.py:110
  6.7 7.7 %collective-permute-start = (bf16[272,128]{1,0:T(8,128)(2,1)S(1)}, bf16[272,128]{1,0:T(8,128)(2,1)S(1)}, u32[]{:S(2)}, u32[]{:S(2)}) collective-permute-start(bf16[272,128]{1,0:T(8,128)(2,1)S(1)} %fusion.4), channel_id=1, source_target_pairs={{0,4},{4,0},{8,12},{12,8},{1,5},{5,1},{9,13},{13,9},{2,6},{6,2},{1... | collective-permute-start | bytes 208904 | tf_op jit(solution)/shard_map/ppermute | solution.py:110
  7.3 24.3 %collective-permute-start.9 = (bf16[256,256]{1,0:T(8,128)(2,1)}, bf16[256,256]{1,0:T(8,128)(2,1)S(1)}, u32[]{:S(2)}, u32[]{:S(2)}) collective-permute-start(bf16[256,256]{1,0:T(8,128)(2,1)} %bitcast.44), channel_id=1, source_target_pairs={{0,4},{4,0},{8,12},{12,8},{1,5},{5,1},{9,13},{13,9},{2,6},{6,2},{1... | collective-permute-start | bytes 393224 | tf_op jit(solution)/shard_map/ppermute | solution.py:110
  8.7 23.0 %collective-permute-start.8 = (bf16[256,256]{1,0:T(8,128)(2,1)}, bf16[256,256]{1,0:T(8,128)(2,1)S(1)}, u32[]{:S(2)}, u32[]{:S(2)}) collective-permute-start(bf16[256,256]{1,0:T(8,128)(2,1)} %bitcast.45), channel_id=1, source_target_pairs={{0,8},{4,12},{8,0},{12,4},{1,9},{5,13},{9,1},{13,5},{2,10},{6,14},... | collective-permute-start | bytes 393224 | tf_op jit(solution)/shard_map/ppermute | solution.py:110
  14.4 7.8 %collective-permute-start.4 = (bf16[3,256,128]{2,1,0:T(8,128)(2,1)S(1)}, bf16[3,256,128]{2,1,0:T(8,128)(2,1)S(1)}, u32[]{:S(2)}, u32[]{:S(2)}) collective-permute-start(bf16[3,256,128]{2,1,0:T(8,128)(2,1)S(1)} %get-tuple-element.28), channel_id=1, source_target_pairs={{0,16},{2,18},{16,0},{18,2},{1,17},{3,19},{17,1},{19,3},{4,20},{6,... | collective-permute-start | bytes 589832 | tf_op jit(solution)/shard_map/ppermute | solution.py:110
  16.3 7.8 %collective-permute-start.3 = (bf16[3,256,128]{2,1,0:T(8,128)(2,1)S(1)}, bf16[3,256,128]{2,1,0:T(8,128)(2,1)S(1)}, u32[]{:S(2)}, u32[]{:S(2)}) collective-permute-start(bf16[3,256,128]{2,1,0:T(8,128)(2,1)S(1)} %get-tuple-element.28), channel_id=1, source_target_pairs={{0,2},{2,0},{16,18},{18,16},{1,3},{3,1},{17,19},{19,17},{4,6},{6,4... | collective-permute-start | bytes 589832 | tf_op jit(solution)/shard_map/ppermute | solution.py:110
  17.8 7.1 %collective-permute-start.5 = (bf16[3,256,128]{2,1,0:T(8,128)(2,1)S(1)}, bf16[3,256,128]{2,1,0:T(8,128)(2,1)S(1)}, u32[]{:S(2)}, u32[]{:S(2)}) collective-permute-start(bf16[3,256,128]{2,1,0:T(8,128)(2,1)S(1)} %get-tuple-element.28), channel_id=1, source_target_pairs={{0,18},{2,16},{16,2},{18,0},{1,19},{3,17},{17,3},{19,1},{4,22},{6,... | collective-permute-start | bytes 589832 | tf_op jit(solution)/shard_map/ppermute | solution.py:110
  22.3 9.4 %collective-permute-start.7 = (bf16[256,256]{1,0:T(8,128)(2,1)}, bf16[256,256]{1,0:T(8,128)(2,1)S(1)}, u32[]{:S(2)}, u32[]{:S(2)}) collective-permute-start(bf16[256,256]{1,0:T(8,128)(2,1)} %bitcast.46), channel_id=1, source_target_pairs={{0,12},{4,8},{8,4},{12,0},{1,13},{5,9},{9,5},{13,1},{2,14},{6,10},... | collective-permute-start | bytes 393224 | tf_op jit(solution)/shard_map/ppermute | solution.py:110
  25.0 2.4 %collective-permute-start.6 = (bf16[4,3,256,128]{3,2,1,0:T(8,128)(2,1)S(1)}, bf16[4,3,256,128]{3,2,1,0:T(8,128)(2,1)S(1)}, u32[]{:S(2)}, u32[]{:S(2)}) collective-permute-start(bf16[4,3,256,128]{3,2,1,0:T(8,128)(2,1)S(1)} %pad_maximum_fusion.near_ref), channel_id=1, source_target_pairs={{0,1},{1,0},{2,3},{3,2},{4,5},{5,4},{6,7},{7,6},{8,9},{9,8},{10,11... | collective-permute-start | bytes 2359304 | tf_op jit(solution)/shard_map/ppermute | solution.py:110
  25.4 6.3 %copy-start = (bf16[1,256,256]{2,1,0:T(8,128)(2,1)S(1)}, bf16[1,256,256]{2,1,0:T(8,128)(2,1)}, u32[]{:S(2)}) copy-start(bf16[1,256,256]{2,1,0:T(8,128)(2,1)} %param.4) | copy-start | bytes 393220
  39.1 1.6 %collective-permute-start.10 = (bf16[2,256,256]{2,1,0:T(8,128)(2,1)S(1)}, bf16[2,256,256]{2,1,0:T(8,128)(2,1)S(1)}, u32[]{:S(2)}, u32[]{:S(2)}) collective-permute-start(bf16[2,256,256]{2,1,0:T(8,128)(2,1)S(1)} %get-tuple-element.23), channel_id=1, source_target_pairs={{0,1},{1,0},{2,3},{3,2},{4,5},{5,4},{6,7},{7,6},{8,9},{9,8},{10,11... | collective-permute-start | bytes 786440 | tf_op jit(solution)/shard_map/ppermute | solution.py:110
  40.7 5.6 %collective-permute-start.11 = (bf16[256,256]{1,0:T(8,128)(2,1)S(1)}, bf16[256,256]{1,0:T(8,128)(2,1)S(1)}, u32[]{:S(2)}, u32[]{:S(2)}) collective-permute-start(bf16[256,256]{1,0:T(8,128)(2,1)S(1)} %fusion), channel_id=1, source_target_pairs={{0,2},{2,0},{1,3},{3,1},{4,6},{6,4},{5,7},{7,5},{8,10},{10,8},{9,1... | collective-permute-start | bytes 393224 | tf_op jit(solution)/shard_map/ppermute | solution.py:110

commit v6 on v5

--- a/solution.py
+++ b/solution.py
@@ -98,6 +98,7 @@
 
 
 VMEM_BYTES = 56 * 2**20
+NEAR_VMEM = 8 * 2**20
 POWERS_VMEM = 20 * 2**20
 MAIN_VMEM = 22 * 2**20
 OWN_VMEM = 14 * 2**20
@@ -110,46 +111,60 @@
     return lax.ppermute(block, axes, [(i, i ^ offset) for i in range(count)])
 
 
-def block_product(dims, facts, h_ref, at, take):
+def block_product(dims, facts, h_refs, at, take):
     bands, rows, cols, piece, local, count, block, per = dims
     starts = []
-    for s in range(count):
-        column = facts[4 + at * count + s]
-        slot = lax.bitwise_xor(column // local, facts[0])
-        starts.append(pl.multiple_of((slot * local + column % local) * block, block))
+    for side in (0, 1):
+        for a in range(per):
+            s = lax.bitwise_xor(facts[3], side) * per + a
+            column = facts[4 + at * count + s]
+            slot = lax.bitwise_xor(column // local, facts[0])
+            starts.append(pl.multiple_of((slot * local + column % local) * block, block))
     right = jnp.concatenate([take(pl.ds(start, block)) for start in starts], axis=0)
-    return jnp.dot(h_ref[at], right, preferred_element_type=F32)
-
-
-def apply_a(dims, facts, h_ref, at, take, width):
+    return jnp.dot(
+        jnp.concatenate([ref[at] for ref in h_refs], axis=1), right, preferred_element_type=F32
+    )
+
+
+def apply_a(dims, facts, h_refs, at, take, width):
     block = dims[6]
-    got = block_product(dims, facts, h_ref, at, take)
+    got = block_product(dims, facts, h_refs, at, take)
     real = got[:block, :width] + got[block:, width:]
     imag = got[:block, width:] - got[block:, :width]
     return 0.5 * jnp.concatenate([real, imag], axis=1)
 
 
-def powers_kernel(dims, facts, mine_ref, near_ref, far_ref, h_ref, c_ref, sel, c1_ref, c2_ref, csum):
-    bands, rows, cols, piece, local, count, block, per = dims
-    r, q, me_plane, me_core = facts[0], facts[1], facts[2], facts[3]
-    h_ref[0:local] = mine_ref[...]
-    for n in range(2 * near_ref.shape[0]):
-        part = (near_ref, far_ref)[n % 2]
-        share = lax.bitwise_xor(me_plane, n // 2) * 2 + lax.bitwise_xor(me_core, n % 2)
-        for at in range(per):
-            flat = share * per + at
-            below = pl.multiple_of((1 - flat // (local * count)) * block, block)
-            b = flat // count % local
-            beside = pl.multiple_of(flat % count * block, block)
-            for k in range(1, bands):
-                h_ref[k * local + b, pl.ds(below, block), pl.ds(beside, block)] = part[
-                    n // 2, k - 1, at * block : (at + 1) * block, :
+def place_side(dims, facts, side, mine_ref, part_ref, h_ref):
+    bands, rows, cols, piece, local, count, block, per = dims
+    core = lax.bitwise_xor(facts[3], side)
+    wide = per * block
+    for b in range(local):
+        h_ref[b] = mine_ref[b, :, pl.ds(pl.multiple_of(core * wide, wide), wide)]
+    for n in range(part_ref.shape[0]):
+        flat = (lax.bitwise_xor(facts[2], n) * 2 + core) * per
+        below = pl.ds(pl.multiple_of((1 - flat // (local * count)) * block, block), block)
+        b = flat // count % local
+        for k in range(1, bands):
+            for at in range(per):
+                h_ref[k * local + b, below, at * block : (at + 1) * block] = part_ref[
+                    n, k - 1, at * block : (at + 1) * block, :
                 ]
+
+
+def near_kernel(dims, facts, mine_ref, near_ref, h_ref, sel_ref):
+    bands, rows, cols, piece, local, count, block, per = dims
+    place_side(dims, facts, 0, mine_ref, near_ref, h_ref)
     row_iota = lax.broadcasted_iota(jnp.int32, (rows, cols), 0)
     col_iota = lax.broadcasted_iota(jnp.int32, (rows, cols), 1)
     for k in range(bands):
-        hit = (col_iota // piece == k) & (row_iota == q * piece + col_iota % piece)
-        sel[k * rows : (k + 1) * rows, :] = jnp.where(hit, 1.0, 0.0).astype(BF16)
+        hit = (col_iota // piece == k) & (row_iota == facts[1] * piece + col_iota % piece)
+        sel_ref[k * rows : (k + 1) * rows, :] = jnp.where(hit, 1.0, 0.0).astype(BF16)
+
+
+def powers_kernel(dims, facts, mine_ref, far_ref, near_h, sel, far_h, c_ref, c1_ref, c2_ref, csum):
+    bands, rows, cols, piece, local, count, block, per = dims
+    place_side(dims, facts, 1, mine_ref, far_ref, far_h)
+    h_refs = (near_h, far_h)
 
     def put_d(span, m, value):
         low = value.astype(BF16)
@@ -158,21 +173,21 @@
 
     for at in range(bands * local):
         span = slice(at * block, (at + 1) * block)
-        got = block_product(dims, facts, h_ref, at, lambda where: sel[where, :])
+        got = block_product(dims, facts, h_refs, at, lambda where: sel[where, :])
         c1 = 0.5 * jnp.concatenate([got[:block], -got[block:]], axis=1)
         c1_ref[span, :] = c1.astype(BF16)
         csum[span, :] = c1
         put_d(span, 2, 0.5 * c1)
     for at in range(bands * local):
         span = slice(at * block, (at + 1) * block)
-        c2 = apply_a(dims, facts, h_ref, at, lambda where: c1_ref[where, :], cols)
+        c2 = apply_a(dims, facts, h_refs, at, lambda where: c1_ref[where, :], cols)
         c2_ref[span, :] = c2.astype(BF16)
         both = csum[span, :] + 0.5 * c2
         csum[span, :] = both
         put_d(span, 1, both)
     for at in range(bands * local):
         span = slice(at * block, (at + 1) * block)
-        c3 = apply_a(dims, facts, h_ref, at, lambda where: c2_ref[where, :], cols)
+        c3 = apply_a(dims, facts, h_refs, at, lambda where: c2_ref[where, :], cols)
         put_d(span, 0, csum[span, :] + c3 * (1.0 / 6.0))
 
 
@@ -238,34 +253,32 @@
 def main_kernel(dims, facts, *refs):
     bands, rows, cols, piece, local, count, block, per = dims
     f_refs = refs[:bands]
-    h_ref, c_ref, keep_ref, send_ref, n_ref, v1_ref, v2_ref, left, slab, tops, outs = refs[bands:]
+    near_h, far_h, c_ref, keep_ref, send_ref, n_ref, v1_ref, v2_ref, left, slab, tops, outs = refs[bands:]
+    h_refs = (near_h, far_h)
     r, q = facts[0], facts[1]
     row_iota = lax.broadcasted_iota(jnp.int32, (rows, cols), 0)
     col_iota = lax.broadcasted_iota(jnp.int32, (rows, cols), 1)
-    col_abs = col_iota // piece * rows + q * piece + col_iota % piece
+    col_abs = lax.bitwise_xor(col_iota // piece, r) * rows + q * piece + col_iota % piece
     for k in range(bands):
-        here = f_refs[-k % bands][...].astype(F32)
+        here = swap_groups(f_refs[-k % bands][...].astype(F32), r, piece)
         row_abs = lax.bitwise_xor(r, k) * rows + row_iota
         real = jnp.where(row_abs < col_abs, here, jnp.where(row_abs == col_abs, 0.5 * here, 0.0))
         imag = jnp.where(row_abs > col_abs, here, 0.0)
-        for half, value in enumerate((real, imag)):
-            n_ref[k * rows : (k + 1) * rows, half * cols : (half + 1) * cols] = swap_groups(
-                value, r, piece
-            ).astype(BF16)
+        n_ref[k * rows : (k + 1) * rows, :] = jnp.concatenate([real, imag], axis=1).astype(BF16)
 
     def thin(value):
         return jnp.concatenate([value[:, :piece], value[:, cols : cols + piece]], axis=1)
 
     for at in range(bands * local):
         span = slice(at * block, (at + 1) * block)
-        v1 = apply_a(dims, facts, h_ref, at, lambda where: n_ref[where, :], cols)
+        v1 = apply_a(dims, facts, h_refs, at, lambda where: n_ref[where, :], cols)
         v1_ref[span, :] = v1.astype(BF16)
         slab[span, :] = thin(v1)
         if at < local:
             tops[span, :] = v1
     for at in range(bands * local):
         span = slice(at * block, (at + 1) * block)
-        v2 = apply_a(dims, facts, h_ref, at, lambda where: v1_ref[where, :], cols)
+        v2 = apply_a(dims, facts, h_refs, at, lambda where: v1_ref[where, :], cols)
         v2_ref[span, :] = v2.astype(BF16)
         slab[span, :] += 0.5 * thin(v2)
         if at < local:
@@ -273,14 +286,14 @@
     for at in range(bands * local):
         span = slice(at * block, (at + 1) * block)
         if at < local:
-            v3 = apply_a(dims, facts, h_ref, at, lambda where: v2_ref[where, :], cols)
+            v3 = apply_a(dims, facts, h_refs, at, lambda where: v2_ref[where, :], cols)
             tops[span, :] += v3 * (1.0 / 6.0)
             slab[span, :] += thin(v3) * (1.0 / 6.0)
         else:
             v3 = apply_a(
                 dims,
                 facts,
-                h_ref,
+                h_refs,
                 at,
                 lambda where: jnp.concatenate(
                     [v2_ref[where, 0:piece], v2_ref[where, cols : cols + piece]],
@@ -337,38 +350,48 @@
 
     smem = pl.BlockSpec(memory_space=pltpu.SMEM)
     vmem = pl.BlockSpec(memory_space=pltpu.VMEM)
-    start = q * per
-    share = jnp.where(
-        lax.axis_index("runs") == 0,
-        lax.dynamic_slice_in_dim(h_real.reshape(local * count, block, block), start, per, 0),
-        lax.dynamic_slice_in_dim(h_imag.reshape(local * count, block, block), start, per, 0),
-    ).reshape(per * block, block)
+    flat_real, flat_imag = [h.reshape(local * count, block, block) for h in (h_real, h_imag)]
+
+    def pick(first, second, at):
+        return jnp.where(
+            lax.axis_index("runs") == 0,
+            lax.dynamic_slice_in_dim(first, at * per, per, 0),
+            lax.dynamic_slice_in_dim(second, at * per, per, 0),
+        ).reshape(per * block, block)
+
+    size = per * block
     col_rows = jnp.pad(h_cols.astype(BF16), ((0, 16 - local), (0, block - count)))
-    message = jnp.concatenate([share, col_rows], axis=0)
+    message = jnp.concatenate([pick(flat_real, flat_imag, q), col_rows], axis=0)
+    diagonal = pick(flat_imag, flat_real, lax.bitwise_xor(q, 2))
     mine = jnp.concatenate(
         [h.transpose(0, 2, 1, 3).reshape(local, block, count * block) for h in (h_imag, h_real)], axis=1
     )
     arrived = [exchange(message, "row", k) for k in range(1, bands)]
-    all_cols = [
-        a[per * block : per * block + local, :count].astype(jnp.int32).reshape(-1) for a in [message] + arrived
-    ]
+    all_cols = [a[size : size + local, :count].astype(jnp.int32).reshape(-1) for a in [message] + arrived]
     facts = jnp.concatenate([jnp.stack([r, q, me_plane, me_core]).astype(jnp.int32)] + all_cols)
-    theirs = jnp.stack([a[: per * block] for a in arrived])
-    near = jnp.stack([theirs] + [exchange(theirs, ("runs", "col"), k) for k in range(1, shares // 2)])
+    theirs = lax.optimization_barrier(jnp.stack([a[:size] for a in arrived]))
+    across_plane = jnp.concatenate([exchange(diagonal, "row", 1)[None], exchange(theirs[1:], ("runs", "col"), 3)], axis=0)
+    near = jnp.stack([theirs] + [exchange(theirs, ("runs", "col"), k) for k in (1, 2)] + [across_plane])
     rest = [exchange(here, "row", k) for k in range(bands - 1, 0, -1)]
     far = exchange(near, "sub", 1)
 
     step = 2 * order * 2 * count * block * 2 * cols
-    h_all, c_side = pl.pallas_call(
+    half_shape = jax.ShapeDtypeStruct((bands * local, 2 * block, per * block), BF16)
+    near_h, sel = pl.pallas_call(
+        functools.partial(near_kernel, dims),
+        out_shape=(half_shape, jax.ShapeDtypeStruct((order, cols), BF16)),
+        in_specs=[smem] + [vmem] * 2,
+        out_specs=(vmem, vmem),
+        compiler_params=pltpu.CompilerParams(vmem_limit_bytes=NEAR_VMEM),
+        cost_estimate=pl.CostEstimate(flops=0, bytes_accessed=2**20, transcendentals=0),
+        name="near",
+    )(facts, mine, near)
+    far_h, c_side = pl.pallas_call(
         functools.partial(powers_kernel, dims),
-        out_shape=(
-            jax.ShapeDtypeStruct((bands * local, 2 * block, count * block), BF16),
-            jax.ShapeDtypeStruct((order, 6 * cols), BF16),
-        ),
-        in_specs=[smem] + [vmem] * 3,
+        out_shape=(half_shape, jax.ShapeDtypeStruct((order, 6 * cols), BF16)),
+        in_specs=[smem] + [vmem] * 4,
         out_specs=(vmem, vmem),
         scratch_shapes=[
-            pltpu.VMEM((order, cols), BF16),
             pltpu.VMEM((order, 2 * cols), BF16),
             pltpu.VMEM((order, 2 * cols), BF16),
             pltpu.VMEM((order, 2 * cols), F32),
@@ -376,7 +399,7 @@
         compiler_params=pltpu.CompilerParams(vmem_limit_bytes=POWERS_VMEM),
         cost_estimate=pl.CostEstimate(flops=5 * step // 2, bytes_accessed=2**20, transcendentals=0),
         name="powers",
-    )(facts, mine, near, far)
+    )(facts, mine, far, near_h, sel)
     block_shape = jax.ShapeDtypeStruct((rows, cols), F32)
     v_shape = jax.ShapeDtypeStruct((order, 2 * cols), BF16)
     keep, send, *state = pl.pallas_call(
@@ -391,13 +414,13 @@
             jax.ShapeDtypeStruct((order, 2 * piece), F32),
             jax.ShapeDtypeStruct((rows, 2 * cols), F32),
         ),
-        in_specs=[smem] + [vmem] * (bands + 2),
+        in_specs=[smem] + [vmem] * (bands + 3),
         out_specs=(vmem,) * 8,
         scratch_shapes=[pltpu.VMEM((bands, 3 * piece, rows), F32)],
         compiler_params=pltpu.CompilerParams(vmem_limit_bytes=MAIN_VMEM),
         cost_estimate=pl.CostEstimate(flops=4 * step, bytes_accessed=2**20, transcendentals=0),
         name="main",
-    )(facts, here, *rest, h_all, c_side)
+    )(facts, here, *rest, near_h, far_h, c_side)
     swapped = exchange(send, "sub", 1)
     across = exchange((keep + swapped[0].astype(F32)).astype(BF16), "col", 1)
     own = pl.pallas_call(
@@ -421,11 +444,12 @@
     shares = mesh.shape["runs"] * mesh.shape["col"] * mesh.shape["sub"]
     return (
         bands & (bands - 1) == 0
-        and bands > 1
+        and bands > 2
         and mesh.shape["runs"] == mesh.shape["col"] == mesh.shape["sub"] == 2
         and rows == cols == local * block
         and (2 * local * count) % shares == 0
         and local <= 16
+        and count * shares == 4 * local * count
         and count <= block
         and 80 * bands * rows * bands * rows // 2 <= VMEM_BYTES
     )

time: 47.2 us -> 47.1 us (level)
  starting transfers between devices: 17.3 us -> 16.4 us
  Pallas kernels: 14.4 us -> 14.9 us
    reshape x5 -> x4, local copies, waits for them, and re-layouts: 1.42 us -> 0.33 us  [gathered_body(): a[size:size + local, :count].astype(jnp.int32).reshape(-1)]
    unnamed x2 -> x5, local copies, waits for them, and re-layouts: 0.01 us -> 0.99 us
    ppermute x12 -> x13, starting transfers between devices: 17.3 us -> 16.4 us  [exchange(): return lax.ppermute(block, axes, [(i, i ^ offset) for i in range(count)])]
    pallas_call x1 -> x2, Pallas kernels: 4.36 us -> 4.94 us  [the longest x1 4.14 us: gathered_body(): pl.pallas_call(functools.partial(powers_kernel, dims), out_shape=(half_sh...]
    ppermute x12 -> x13, waiting for transfers between devices: 11.2 us -> 11.3 us  [exchange(): return lax.ppermute(block, axes, [(i, i ^ offset) for i in range(count)])]
  transfers between devices with their start and end apart: 12 -> 13, of which waited for: 7 -> 6; matrix products, arithmetic and copies ran while one was open for 4% -> 3% of each run, Pallas kernels for 15% -> 16%
where the time goes in v6:
time: 47.1 us; the launch traced here: 46.9 us
  starting transfers between devices  16.4 us (35%)
  Pallas kernels  14.9 us (32%)
  waiting for transfers between devices  11.3 us (24%)
  other arithmetic  2.63 us (6%)
  local copies, waits for them, and re-layouts  1.45 us (3%)
    ppermute x13, starting transfers between devices, exchange(): return lax.ppermute(block, axes, [(i, i ^ offset) for i in range(count)])  16.4 us
    ppermute x13, waiting for transfers between devices, exchange(): return lax.ppermute(block, axes, [(i, i ^ offset) for i in range(count)])  11.3 us
    pallas_call x1, Pallas kernels, gathered_body(): pl.pallas_call(functools.partial(main_kernel, dims), out_shape=(block_sha...  7.2 us
    pallas_call x1, Pallas kernels, gathered_body(): pl.pallas_call(functools.partial(powers_kernel, dims), out_shape=(half_sh...  4.14 us
    pallas_call x1, Pallas kernels, gathered_body(): pl.pallas_call(functools.partial(own_kernel, dims), out_shape=block_shape...  2.73 us
    unnamed x5, local copies, waits for them, and re-layouts  0.99 us
    select_n x1, other arithmetic, pick(): jnp.where(lax.axis_index('runs') == 0, lax.dynamic_slice_in_dim(first, at...  0.95 us
  transfers between devices with their start and end apart: 13, of which 6 were waited for; matrix products, arithmetic and copies ran while one was open for 3% of the time, Pallas kernels for 16%

profile of v6, /device:TPU:0, one launch (start us, length us, event | category | flops | bytes accessed | tf_op | source)
XLA Modules:
  0.0 46.9 jit_solution(6341892219036770802)
XLA Ops:
  0.0 0.0 copy-start.1
  0.0 0.7 %fusion.5 = (s32[2,4]{1,0:T(2,128)S(1)}, bf16[2,4]{1,0:T(2,128)(2,1)S(1)}) fusion(s32[2,4]{1,0:T(2,128)} %param.7), kind=kLoop, calls=%fused_computation.23 | loop fusion | flops 16 | bytes 80 | tf_op jit(solution)/shard_map/reshape | solution.py:370
  0.7 1.0 %dynamic-slice_select_fusion = (bf16[2,128,128]{2,1,0:T(8,128)(2,1)S(1)}, bf16[2,128,128]{2,1,0:T(8,128)(2,1)S(1)}) fusion(bf16[8,128,128]{2,1,0:T(8,128)(2,1)} %bitcast.52, s32[]{:T(128)S(6)} %select_n.23, bf16[8,128,128]{2,1,0:T(8,128)(2,1)} %bitcast.51, pred[]{:T(512)S(6)} %eq.4, s32[]{:T(128)S(6)} %select_n.21), kind=kLoop, calls=%fused_computation.18 | loop fusion | flops 65536 | bytes 393225 | tf_op jit(solution)/shard_map/jit(_where)/select_n | solution.py:356
  1.7 5.1 %collective-permute-start.2 = (bf16[272,128]{1,0:T(8,128)(2,1)S(1)}, bf16[272,128]{1,0:T(8,128)(2,1)S(1)}, u32[]{:S(2)}, u32[]{:S(2)}) collective-permute-start(bf16[272,128]{1,0:T(8,128)(2,1)S(1)} %fusion.4), channel_id=1, source_target_pairs={{0,12},{4,8},{8,4},{12,0},{1,13},{5,9},{9,5},{13,1},{2,14},{6,10},... | collective-permute-start | bytes 208904 | tf_op jit(solution)/shard_map/ppermute | solution.py:111
  6.8 0.0 collective-permute-start.1
  6.8 0.6 %collective-permute-start = (bf16[272,128]{1,0:T(8,128)(2,1)S(1)}, bf16[272,128]{1,0:T(8,128)(2,1)S(1)}, u32[]{:S(2)}, u32[]{:S(2)}) collective-permute-start(bf16[272,128]{1,0:T(8,128)(2,1)S(1)} %fusion.4), channel_id=1, source_target_pairs={{0,4},{4,0},{8,12},{12,8},{1,5},{5,1},{9,13},{13,9},{2,6},{6,2},{1... | collective-permute-start | bytes 208904 | tf_op jit(solution)/shard_map/ppermute | solution.py:111
  7.5 1.4 %collective-permute-start.5 = (bf16[256,128]{1,0:T(8,128)(2,1)S(1)}, bf16[256,128]{1,0:T(8,128)(2,1)S(1)}, u32[]{:S(2)}, u32[]{:S(2)}) collective-permute-start(bf16[256,128]{1,0:T(8,128)(2,1)S(1)} %bitcast.56), channel_id=1, source_target_pairs={{0,4},{4,0},{8,12},{12,8},{1,5},{5,1},{9,13},{13,9},{2,6},{6,2},{1... | collective-permute-start | bytes 196616 | tf_op jit(solution)/shard_map/ppermute | solution.py:111
  8.8 0.7 %collective-permute-start.10 = (bf16[256,256]{1,0:T(8,128)(2,1)}, bf16[256,256]{1,0:T(8,128)(2,1)S(1)}, u32[]{:S(2)}, u32[]{:S(2)}) collective-permute-start(bf16[256,256]{1,0:T(8,128)(2,1)} %bitcast.46), channel_id=1, source_target_pairs={{0,4},{4,0},{8,12},{12,8},{1,5},{5,1},{9,13},{13,9},{2,6},{6,2},{1... | collective-permute-start | bytes 393224 | tf_op jit(solution)/shard_map/ppermute | solution.py:111
  9.5 0.0 collective-permute-done.2
  9.5 3.3 %collective-permute-done.1 = bf16[272,128]{1,0:T(8,128)(2,1)S(1)} collective-permute-done((bf16[272,128]{1,0:T(8,128)(2,1)S(1)}, bf16[272,128]{1,0:T(8,128)(2,1)S(1)}, u32[]{:S(2)}, u32[]{:S(2)}) %collective-permute-start.1) | collective-permute-done | bytes 69664 | tf_op jit(solution)/shard_map/ppermute | solution.py:111
  12.8 0.4 collective-permute-done
  13.3 1.7 %collective-permute-start.4 = (bf16[3,256,128]{2,1,0:T(8,128)(2,1)S(1)}, bf16[3,256,128]{2,1,0:T(8,128)(2,1)S(1)}, u32[]{:S(2)}, u32[]{:S(2)}) collective-permute-start(bf16[3,256,128]{2,1,0:T(8,128)(2,1)S(1)} %pad_maximum_fusion.1), channel_id=1, source_target_pairs={{0,16},{2,18},{16,0},{18,2},{1,17},{3,19},{17,1},{19,3},{4,20},{6,... | collective-permute-start | bytes 589832 | tf_op jit(solution)/shard_map/ppermute | solution.py:111
  15.0 1.5 %collective-permute-start.3 = (bf16[3,256,128]{2,1,0:T(8,128)(2,1)S(1)}, bf16[3,256,128]{2,1,0:T(8,128)(2,1)S(1)}, u32[]{:S(2)}, u32[]{:S(2)}) collective-permute-start(bf16[3,256,128]{2,1,0:T(8,128)(2,1)S(1)} %pad_maximum_fusion.1), channel_id=1, source_target_pairs={{0,2},{2,0},{16,18},{18,16},{1,3},{3,1},{17,19},{19,17},{4,6},{6,4... | collective-permute-start | bytes 589832 | tf_op jit(solution)/shard_map/ppermute | solution.py:111
  16.5 0.3 collective-permute-start.6
  16.8 1.0 %bitcast_dynamic-update-slice_fusion.1 = bf16[2,256,512]{2,1,0:T(8,128)(2,1)S(1)} fusion(bf16[2,4,128,128]{3,2,1,0:T(8,128)(2,1)} %param.6), kind=kLoop, calls=%fused_computation.2 | loop fusion | bytes 524288
  17.8 0.0 collective-permute-done.5
  17.8 1.6 %collective-permute-start.9 = (bf16[256,256]{1,0:T(8,128)(2,1)}, bf16[256,256]{1,0:T(8,128)(2,1)S(1)}, u32[]{:S(2)}, u32[]{:S(2)}) collective-permute-start(bf16[256,256]{1,0:T(8,128)(2,1)} %bitcast.47), channel_id=1, source_target_pairs={{0,8},{4,12},{8,0},{12,4},{1,9},{5,13},{9,1},{13,5},{2,10},{6,14},... | collective-permute-start | bytes 393224 | tf_op jit(solution)/shard_map/ppermute | solution.py:111
  19.5 3.9 %collective-permute-done.6 = bf16[2,256,128]{2,1,0:T(8,128)(2,1)S(1)} collective-permute-done((bf16[2,256,128]{2,1,0:T(8,128)(2,1)S(1)}, bf16[2,256,128]{2,1,0:T(8,128)(2,1)S(1)}, u32[]{:S(2)}, u32[]{:S(2)}) %collective-permute-start.6) | collective-permute-done | bytes 131104 | tf_op jit(solution)/shard_map/ppermute | solution.py:111
  23.3 1.6 %collective-permute-start.8 = (bf16[256,256]{1,0:T(8,128)(2,1)}, bf16[256,256]{1,0:T(8,128)(2,1)S(1)}, u32[]{:S(2)}, u32[]{:S(2)}) collective-permute-start(bf16[256,256]{1,0:T(8,128)(2,1)} %bitcast.48), channel_id=1, source_target_pairs={{0,12},{4,8},{8,4},{12,0},{1,13},{5,9},{9,5},{13,1},{2,14},{6,10},... | collective-permute-start | bytes 393224 | tf_op jit(solution)/shard_map/ppermute | solution.py:111
  25.0 0.0 collective-permute-done.4
  25.0 0.0 collective-permute-done.3
  25.0 0.1 pad_maximum_fusion.near_ref
  25.1 0.1 collective-permute-start.7
  25.2 0.0 copy-done.1
  25.2 0.1 reshape.65
  25.3 0.1 reshape.71
  25.4 0.1 reshape.69
  25.5 0.1 reshape.67
  25.6 0.1 concatenate.13.facts
  25.7 0.8 %near.1 = (bf16[8,256,256]{2,1,0:T(8,128)(2,1)S(1)}, bf16[1024,256]{1,0:T(8,128)(2,1)S(1)}) custom-call(s32[36]{0:T(128)S(1)} %concatenate.13.facts, bf16[2,256,512]{2,1,0:T(8,128)(2,1)S(1)} %bitcast_dynamic-update-slice_fusion.mine_ref, bf16[4,3,256,128]{3,2,1,0:T(8,128)(2,1)S(1)} %pad_maximum_fusion.near_ref), custom_call_target="tpu_custom_call" | custom-call | bytes 1048576 | tf_op jit(solution)/shard_map/near/pallas_call | solution.py:380
  26.5 1.0 %collective-permute-done.7.far_ref = bf16[4,3,256,128]{3,2,1,0:T(8,128)(2,1)S(1)} collective-permute-done((bf16[4,3,256,128]{3,2,1,0:T(8,128)(2,1)S(1)}, bf16[4,3,256,128]{3,2,1,0:T(8,128)(2,1)S(1)}, u32[]{:S(2)}, u32[]{:S(2)}) %collective-permute-start.7) | collective-permute-done | bytes 786464 | tf_op jit(solution)/shard_map/ppermute | solution.py:111
  27.5 0.0 copy-start
  27.5 4.1 %powers.1 = (bf16[8,256,256]{2,1,0:T(8,128)(2,1)S(1)}, bf16[1024,1536]{1,0:T(8,128)(2,1)S(1)}) custom-call(s32[36]{0:T(128)S(1)} %concatenate.13.facts, bf16[2,256,512]{2,1,0:T(8,128)(2,1)S(1)} %bitcast_dynamic-update-slice_fusion.mine_ref, bf16[4,3,256,128]{3,2,1,0:T(8,128)(2,1)S(1)} %collective-permute-done.7.far_ref, ...), custom_call_target="tpu_custom_call" | custom-call | flops 2684354560 | bytes 1048576 | tf_op jit(solution)/shard_map/powers/pallas_call | solution.py:389
  31.6 0.0 collective-permute-done.10.refs_3_
  31.6 0.0 collective-permute-done.9.refs_2_
  31.6 0.0 collective-permute-done.8.refs_1_
  31.6 0.0 copy-done
  31.6 7.2 %main.1 = (f32[256,256]{1,0:T(8,128)S(1)}, bf16[2,256,256]{2,1,0:T(8,128)(2,1)S(1)}, bf16[1024,512]{1,0:T(8,128)(2,1)S(1)}, bf16[1024,512]{1,0:T(8,128)(2,1)S(1)...) custom-call(s32[36]{0:T(128)S(1)} %concatenate.13.facts, ...), custom_call_target="tpu_custom_call" | custom-call | flops 4294967296 | bytes 1048576 | tf_op jit(solution)/shard_map/main/pallas_call | solution.py:405
  38.9 0.2 collective-permute-start.11
  39.1 1.4 %collective-permute-done.11 = bf16[2,256,256]{2,1,0:T(8,128)(2,1)S(1)} collective-permute-done((bf16[2,256,256]{2,1,0:T(8,128)(2,1)S(1)}, bf16[2,256,256]{2,1,0:T(8,128)(2,1)S(1)}, u32[]{:S(2)}, u32[]{:S(2)}) %collective-permute-start.11) | collective-permute-done | bytes 262176 | tf_op jit(solution)/shard_map/ppermute | solution.py:111
  40.5 1.5 %collective-permute-start.12 = (bf16[256,256]{1,0:T(8,128)(2,1)S(1)}, bf16[256,256]{1,0:T(8,128)(2,1)S(1)}, u32[]{:S(2)}, u32[]{:S(2)}) collective-permute-start(bf16[256,256]{1,0:T(8,128)(2,1)S(1)} %fusion), channel_id=1, source_target_pairs={{0,2},{2,0},{1,3},{3,1},{4,6},{6,4},{5,7},{7,5},{8,10},{10,8},{9,1... | collective-permute-start | bytes 393224 | tf_op jit(solution)/shard_map/ppermute | solution.py:111
  42.0 2.7 %own.1 = f32[256,256]{1,0:T(8,128)S(1)} custom-call(s32[36]{0:T(128)S(1)} %concatenate.13.facts, bf16[1024,1536]{1,0:T(8,128)(2,1)S(1)} %get-tuple-element.19.refs_6_.c_ref, bf16[1024,512]{1,0:T(8,128)(2,1)S(1)} %get-tuple-element.21.n_ref, bf16[1024,512]{1,0:T(8,128)(2,1)S(1)} %get-tuple-element.22.v1_ref, bf16[1024,512]{1,0:T(8,128)(2,1)S(1)} %get-tuple-element.23.v2_ref, ...), custom_call_target="tpu_custom_call" | custom-call | flops 1073741824 | bytes 1048576 | tf_op jit(solution)/shard_map/own/pallas_call | solution.py:426
  44.8 1.3 %collective-permute-done.12 = bf16[256,256]{1,0:T(8,128)(2,1)S(1)} collective-permute-done((bf16[256,256]{1,0:T(8,128)(2,1)S(1)}, bf16[256,256]{1,0:T(8,128)(2,1)S(1)}, u32[]{:S(2)}, u32[]{:S(2)}) %collective-permute-start.12) | collective-permute-done | bytes 131104 | tf_op jit(solution)/shard_map/ppermute | solution.py:111
  46.1 0.8 %fusion.2 = f32[1,256,256]{2,1,0:T(8,128)} fusion(bf16[256,256]{1,0:T(8,128)(2,1)S(1)} %collective-permute-done.12, f32[256,256]{1,0:T(8,128)S(1)} %own.1, bf16[2,256,256]{2,1,0:T(8,128)(2,1)S(1)} %collective-permute-done.11, bf16[1,256,256]{2,1,0:T(8,128)(2,1)S(1)} %copy-done), kind=kLoop, calls=%fused_computation.7 | loop fusion | flops 393216 | bytes 917504 | tf_op jit(solution)/shard_map/broadcast_in_dim | solution.py:437
  (12 shorter events, 0.2 us)
Async XLA Ops:
  0.0 25.2 %copy-start.1 = (bf16[2,4,128,128]{3,2,1,0:T(8,128)(2,1)S(1)}, bf16[2,4,128,128]{3,2,1,0:T(8,128)(2,1)}, u32[]{:S(2)}) copy-start(bf16[2,4,128,128]{3,2,1,0:T(8,128)(2,1)} %param.5) | copy-start | bytes 786436
  1.7 7.8 %collective-permute-start.2 = (bf16[272,128]{1,0:T(8,128)(2,1)S(1)}, bf16[272,128]{1,0:T(8,128)(2,1)S(1)}, u32[]{:S(2)}, u32[]{:S(2)}) collective-permute-start(bf16[272,128]{1,0:T(8,128)(2,1)S(1)} %fusion.4), channel_id=1, source_target_pairs={{0,12},{4,8},{8,4},{12,0},{1,13},{5,9},{9,5},{13,1},{2,14},{6,10},... | collective-permute-start | bytes 208904 | tf_op jit(solution)/shard_map/ppermute | solution.py:111
  6.8 6.0 %collective-permute-start.1 = (bf16[272,128]{1,0:T(8,128)(2,1)S(1)}, bf16[272,128]{1,0:T(8,128)(2,1)S(1)}, u32[]{:S(2)}, u32[]{:S(2)}) collective-permute-start(bf16[272,128]{1,0:T(8,128)(2,1)S(1)} %fusion.4), channel_id=1, source_target_pairs={{0,8},{4,12},{8,0},{12,4},{1,9},{5,13},{9,1},{13,5},{2,10},{6,14},... | collective-permute-start | bytes 208904 | tf_op jit(solution)/shard_map/ppermute | solution.py:111
  6.8 6.4 %collective-permute-start = (bf16[272,128]{1,0:T(8,128)(2,1)S(1)}, bf16[272,128]{1,0:T(8,128)(2,1)S(1)}, u32[]{:S(2)}, u32[]{:S(2)}) collective-permute-start(bf16[272,128]{1,0:T(8,128)(2,1)S(1)} %fusion.4), channel_id=1, source_target_pairs={{0,4},{4,0},{8,12},{12,8},{1,5},{5,1},{9,13},{13,9},{2,6},{6,2},{1... | collective-permute-start | bytes 208904 | tf_op jit(solution)/shard_map/ppermute | solution.py:111
  7.5 10.4 %collective-permute-start.5 = (bf16[256,128]{1,0:T(8,128)(2,1)S(1)}, bf16[256,128]{1,0:T(8,128)(2,1)S(1)}, u32[]{:S(2)}, u32[]{:S(2)}) collective-permute-start(bf16[256,128]{1,0:T(8,128)(2,1)S(1)} %bitcast.56), channel_id=1, source_target_pairs={{0,4},{4,0},{8,12},{12,8},{1,5},{5,1},{9,13},{13,9},{2,6},{6,2},{1... | collective-permute-start | bytes 196616 | tf_op jit(solution)/shard_map/ppermute | solution.py:111
  8.8 22.8 %collective-permute-start.10 = (bf16[256,256]{1,0:T(8,128)(2,1)}, bf16[256,256]{1,0:T(8,128)(2,1)S(1)}, u32[]{:S(2)}, u32[]{:S(2)}) collective-permute-start(bf16[256,256]{1,0:T(8,128)(2,1)} %bitcast.46), channel_id=1, source_target_pairs={{0,4},{4,0},{8,12},{12,8},{1,5},{5,1},{9,13},{13,9},{2,6},{6,2},{1... | collective-permute-start | bytes 393224 | tf_op jit(solution)/shard_map/ppermute | solution.py:111
  13.3 11.7 %collective-permute-start.4 = (bf16[3,256,128]{2,1,0:T(8,128)(2,1)S(1)}, bf16[3,256,128]{2,1,0:T(8,128)(2,1)S(1)}, u32[]{:S(2)}, u32[]{:S(2)}) collective-permute-start(bf16[3,256,128]{2,1,0:T(8,128)(2,1)S(1)} %pad_maximum_fusion.1), channel_id=1, source_target_pairs={{0,16},{2,18},{16,0},{18,2},{1,17},{3,19},{17,1},{19,3},{4,20},{6,... | collective-permute-start | bytes 589832 | tf_op jit(solution)/shard_map/ppermute | solution.py:111
  15.0 10.0 %collective-permute-start.3 = (bf16[3,256,128]{2,1,0:T(8,128)(2,1)S(1)}, bf16[3,256,128]{2,1,0:T(8,128)(2,1)S(1)}, u32[]{:S(2)}, u32[]{:S(2)}) collective-permute-start(bf16[3,256,128]{2,1,0:T(8,128)(2,1)S(1)} %pad_maximum_fusion.1), channel_id=1, source_target_pairs={{0,2},{2,0},{16,18},{18,16},{1,3},{3,1},{17,19},{19,17},{4,6},{6,4... | collective-permute-start | bytes 589832 | tf_op jit(solution)/shard_map/ppermute | solution.py:111
  16.5 6.8 %collective-permute-start.6 = (bf16[2,256,128]{2,1,0:T(8,128)(2,1)S(1)}, bf16[2,256,128]{2,1,0:T(8,128)(2,1)S(1)}, u32[]{:S(2)}, u32[]{:S(2)}) collective-permute-start(bf16[2,256,128]{2,1,0:T(8,128)(2,1)S(1)} %slice.43), channel_id=1, source_target_pairs={{0,18},{2,16},{16,2},{18,0},{1,19},{3,17},{17,3},{19,1},{4,22},{6,... | collective-permute-start | bytes 393224 | tf_op jit(solution)/shard_map/ppermute | solution.py:111
  17.8 13.8 %collective-permute-start.9 = (bf16[256,256]{1,0:T(8,128)(2,1)}, bf16[256,256]{1,0:T(8,128)(2,1)S(1)}, u32[]{:S(2)}, u32[]{:S(2)}) collective-permute-start(bf16[256,256]{1,0:T(8,128)(2,1)} %bitcast.47), channel_id=1, source_target_pairs={{0,8},{4,12},{8,0},{12,4},{1,9},{5,13},{9,1},{13,5},{2,10},{6,14},... | collective-permute-start | bytes 393224 | tf_op jit(solution)/shard_map/ppermute | solution.py:111
  23.3 8.3 %collective-permute-start.8 = (bf16[256,256]{1,0:T(8,128)(2,1)}, bf16[256,256]{1,0:T(8,128)(2,1)S(1)}, u32[]{:S(2)}, u32[]{:S(2)}) collective-permute-start(bf16[256,256]{1,0:T(8,128)(2,1)} %bitcast.48), channel_id=1, source_target_pairs={{0,12},{4,8},{8,4},{12,0},{1,13},{5,9},{9,5},{13,1},{2,14},{6,10},... | collective-permute-start | bytes 393224 | tf_op jit(solution)/shard_map/ppermute | solution.py:111
  25.1 2.4 %collective-permute-start.7 = (bf16[4,3,256,128]{3,2,1,0:T(8,128)(2,1)S(1)}, bf16[4,3,256,128]{3,2,1,0:T(8,128)(2,1)S(1)}, u32[]{:S(2)}, u32[]{:S(2)}) collective-permute-start(bf16[4,3,256,128]{3,2,1,0:T(8,128)(2,1)S(1)} %pad_maximum_fusion.near_ref), channel_id=1, source_target_pairs={{0,1},{1,0},{2,3},{3,2},{4,5},{5,4},{6,7},{7,6},{8,9},{9,8},{10,11... | collective-permute-start | bytes 2359304 | tf_op jit(solution)/shard_map/ppermute | solution.py:111
  27.5 4.2 %copy-start = (bf16[1,256,256]{2,1,0:T(8,128)(2,1)S(1)}, bf16[1,256,256]{2,1,0:T(8,128)(2,1)}, u32[]{:S(2)}) copy-start(bf16[1,256,256]{2,1,0:T(8,128)(2,1)} %param.4) | copy-start | bytes 393220
  38.9 1.6 %collective-permute-start.11 = (bf16[2,256,256]{2,1,0:T(8,128)(2,1)S(1)}, bf16[2,256,256]{2,1,0:T(8,128)(2,1)S(1)}, u32[]{:S(2)}, u32[]{:S(2)}) collective-permute-start(bf16[2,256,256]{2,1,0:T(8,128)(2,1)S(1)} %get-tuple-element.27), channel_id=1, source_target_pairs={{0,1},{1,0},{2,3},{3,2},{4,5},{5,4},{6,7},{7,6},{8,9},{9,8},{10,11... | collective-permute-start | bytes 786440 | tf_op jit(solution)/shard_map/ppermute | solution.py:111
  40.5 5.6 %collective-permute-start.12 = (bf16[256,256]{1,0:T(8,128)(2,1)S(1)}, bf16[256,256]{1,0:T(8,128)(2,1)S(1)}, u32[]{:S(2)}, u32[]{:S(2)}) collective-permute-start(bf16[256,256]{1,0:T(8,128)(2,1)S(1)} %fusion), channel_id=1, source_target_pairs={{0,2},{2,0},{1,3},{3,1},{4,6},{6,4},{5,7},{7,5},{8,10},{10,8},{9,1... | collective-permute-start | bytes 393224 | tf_op jit(solution)/shard_map/ppermute | solution.py:111

commit v7 on v6

--- a/solution.py
+++ b/solution.py
@@ -316,8 +316,8 @@
     far = lax.bitwise_xor(q, 2)
     wanted = (lax.bitwise_xor(far, 1), lax.bitwise_xor(q, 1), far)
     target = products(dims, facts, wanted, c_ref, n_ref, v1_ref, v2_ref, left, slab, outs)
-    send_ref[0] = target(0).astype(BF16)
-    send_ref[1] = target(1).astype(BF16)
+    send_ref[0] = target(0)
+    send_ref[1] = target(1)
     keep_ref[...] = target(2)
 
 
@@ -406,7 +406,7 @@
         functools.partial(main_kernel, dims),
         out_shape=(
             block_shape,
-            jax.ShapeDtypeStruct((2, rows, cols), BF16),
+            jax.ShapeDtypeStruct((2, rows, cols), F32),
             v_shape,
             v_shape,
             v_shape,
@@ -422,7 +422,7 @@
         name="main",
     )(facts, here, *rest, near_h, far_h, c_side)
     swapped = exchange(send, "sub", 1)
-    across = exchange((keep + swapped[0].astype(F32)).astype(BF16), "col", 1)
+    across = exchange((keep + swapped[0]).astype(BF16), "col", 1)
     own = pl.pallas_call(
         functools.partial(own_kernel, dims),
         out_shape=block_shape,
@@ -433,7 +433,7 @@
         cost_estimate=pl.CostEstimate(flops=step, bytes_accessed=2**20, transcendentals=0),
         name="own",
     )(facts, c_side, *state)
-    total = here.astype(F32) + own + swapped[1].astype(F32) + across.astype(F32)
+    total = here.astype(F32) + own + swapped[1] + across.astype(F32)
     return total[None]
 
 

time: 47.1 us -> 47.5 us (level)
  no operation moved by 1% of the time
where the time goes in v7:
time: 47.5 us; the launch traced here: 47.3 us
  starting transfers between devices  16.4 us (35%)
  Pallas kernels  14.9 us (31%)
  waiting for transfers between devices  11.7 us (25%)
  other arithmetic  2.63 us (6%)
  local copies, waits for them, and re-layouts  1.45 us (3%)
    ppermute x13, starting transfers between devices, exchange(): return lax.ppermute(block, axes, [(i, i ^ offset) for i in range(count)])  16.4 us
    ppermute x13, waiting for transfers between devices, exchange(): return lax.ppermute(block, axes, [(i, i ^ offset) for i in range(count)])  11.7 us
    pallas_call x1, Pallas kernels, gathered_body(): pl.pallas_call(functools.partial(main_kernel, dims), out_shape=(block_sha...  7.26 us
    pallas_call x1, Pallas kernels, gathered_body(): pl.pallas_call(functools.partial(powers_kernel, dims), out_shape=(half_sh...  4.14 us
    pallas_call x1, Pallas kernels, gathered_body(): pl.pallas_call(functools.partial(own_kernel, dims), out_shape=block_shape...  2.73 us
    unnamed x5, local copies, waits for them, and re-layouts  0.99 us
    select_n x1, other arithmetic, pick(): jnp.where(lax.axis_index('runs') == 0, lax.dynamic_slice_in_dim(first, at...  0.95 us
  transfers between devices with their start and end apart: 13, of which 6 were waited for; matrix products, arithmetic and copies ran while one was open for 3% of the time, Pallas kernels for 16%

profile of v7, /device:TPU:0, one launch (start us, length us, event | category | flops | bytes accessed | tf_op | source)
XLA Modules:
  0.0 47.3 jit_solution(4643037063051253122)
XLA Ops:
  0.0 0.0 copy-start.1
  0.0 0.7 %fusion.7 = (s32[2,4]{1,0:T(2,128)S(1)}, bf16[2,4]{1,0:T(2,128)(2,1)S(1)}) fusion(s32[2,4]{1,0:T(2,128)} %param.7), kind=kLoop, calls=%fused_computation.23 | loop fusion | flops 16 | bytes 80 | tf_op jit(solution)/shard_map/reshape | solution.py:370
  0.7 1.0 %dynamic-slice_select_fusion = (bf16[2,128,128]{2,1,0:T(8,128)(2,1)S(1)}, bf16[2,128,128]{2,1,0:T(8,128)(2,1)S(1)}) fusion(bf16[8,128,128]{2,1,0:T(8,128)(2,1)} %bitcast.56, s32[]{:T(128)S(6)} %select_n.23, bf16[8,128,128]{2,1,0:T(8,128)(2,1)} %bitcast.55, pred[]{:T(512)S(6)} %eq.4, s32[]{:T(128)S(6)} %select_n.21), kind=kLoop, calls=%fused_computation.18 | loop fusion | flops 65536 | bytes 393225 | tf_op jit(solution)/shard_map/jit(_where)/select_n | solution.py:356
  1.7 5.1 %collective-permute-start.2 = (bf16[272,128]{1,0:T(8,128)(2,1)S(1)}, bf16[272,128]{1,0:T(8,128)(2,1)S(1)}, u32[]{:S(2)}, u32[]{:S(2)}) collective-permute-start(bf16[272,128]{1,0:T(8,128)(2,1)S(1)} %fusion.6), channel_id=1, source_target_pairs={{0,12},{4,8},{8,4},{12,0},{1,13},{5,9},{9,5},{13,1},{2,14},{6,10},... | collective-permute-start | bytes 208904 | tf_op jit(solution)/shard_map/ppermute | solution.py:111
  6.8 0.0 collective-permute-start.1
  6.8 0.6 %collective-permute-start = (bf16[272,128]{1,0:T(8,128)(2,1)S(1)}, bf16[272,128]{1,0:T(8,128)(2,1)S(1)}, u32[]{:S(2)}, u32[]{:S(2)}) collective-permute-start(bf16[272,128]{1,0:T(8,128)(2,1)S(1)} %fusion.6), channel_id=1, source_target_pairs={{0,4},{4,0},{8,12},{12,8},{1,5},{5,1},{9,13},{13,9},{2,6},{6,2},{1... | collective-permute-start | bytes 208904 | tf_op jit(solution)/shard_map/ppermute | solution.py:111
  7.5 1.4 %collective-permute-start.5 = (bf16[256,128]{1,0:T(8,128)(2,1)S(1)}, bf16[256,128]{1,0:T(8,128)(2,1)S(1)}, u32[]{:S(2)}, u32[]{:S(2)}) collective-permute-start(bf16[256,128]{1,0:T(8,128)(2,1)S(1)} %bitcast.60), channel_id=1, source_target_pairs={{0,4},{4,0},{8,12},{12,8},{1,5},{5,1},{9,13},{13,9},{2,6},{6,2},{1... | collective-permute-start | bytes 196616 | tf_op jit(solution)/shard_map/ppermute | solution.py:111
  8.8 0.7 %collective-permute-start.10 = (bf16[256,256]{1,0:T(8,128)(2,1)}, bf16[256,256]{1,0:T(8,128)(2,1)S(1)}, u32[]{:S(2)}, u32[]{:S(2)}) collective-permute-start(bf16[256,256]{1,0:T(8,128)(2,1)} %bitcast.50), channel_id=1, source_target_pairs={{0,4},{4,0},{8,12},{12,8},{1,5},{5,1},{9,13},{13,9},{2,6},{6,2},{1... | collective-permute-start | bytes 393224 | tf_op jit(solution)/shard_map/ppermute | solution.py:111
  9.5 0.0 collective-permute-done.2
  9.5 3.3 %collective-permute-done.1 = bf16[272,128]{1,0:T(8,128)(2,1)S(1)} collective-permute-done((bf16[272,128]{1,0:T(8,128)(2,1)S(1)}, bf16[272,128]{1,0:T(8,128)(2,1)S(1)}, u32[]{:S(2)}, u32[]{:S(2)}) %collective-permute-start.1) | collective-permute-done | bytes 69664 | tf_op jit(solution)/shard_map/ppermute | solution.py:111
  12.8 0.4 collective-permute-done
  13.3 1.7 %collective-permute-start.4 = (bf16[3,256,128]{2,1,0:T(8,128)(2,1)S(1)}, bf16[3,256,128]{2,1,0:T(8,128)(2,1)S(1)}, u32[]{:S(2)}, u32[]{:S(2)}) collective-permute-start(bf16[3,256,128]{2,1,0:T(8,128)(2,1)S(1)} %pad_maximum_fusion.1), channel_id=1, source_target_pairs={{0,16},{2,18},{16,0},{18,2},{1,17},{3,19},{17,1},{19,3},{4,20},{6,... | collective-permute-start | bytes 589832 | tf_op jit(solution)/shard_map/ppermute | solution.py:111
  15.0 1.5 %collective-permute-start.3 = (bf16[3,256,128]{2,1,0:T(8,128)(2,1)S(1)}, bf16[3,256,128]{2,1,0:T(8,128)(2,1)S(1)}, u32[]{:S(2)}, u32[]{:S(2)}) collective-permute-start(bf16[3,256,128]{2,1,0:T(8,128)(2,1)S(1)} %pad_maximum_fusion.1), channel_id=1, source_target_pairs={{0,2},{2,0},{16,18},{18,16},{1,3},{3,1},{17,19},{19,17},{4,6},{6,4... | collective-permute-start | bytes 589832 | tf_op jit(solution)/shard_map/ppermute | solution.py:111
  16.5 0.3 collective-permute-start.6
  16.8 1.0 %bitcast_dynamic-update-slice_fusion.1 = bf16[2,256,512]{2,1,0:T(8,128)(2,1)S(1)} fusion(bf16[2,4,128,128]{3,2,1,0:T(8,128)(2,1)} %param.6), kind=kLoop, calls=%fused_computation.2 | loop fusion | bytes 524288
  17.8 0.0 collective-permute-done.5
  17.8 1.6 %collective-permute-start.9 = (bf16[256,256]{1,0:T(8,128)(2,1)}, bf16[256,256]{1,0:T(8,128)(2,1)S(1)}, u32[]{:S(2)}, u32[]{:S(2)}) collective-permute-start(bf16[256,256]{1,0:T(8,128)(2,1)} %bitcast.51), channel_id=1, source_target_pairs={{0,8},{4,12},{8,0},{12,4},{1,9},{5,13},{9,1},{13,5},{2,10},{6,14},... | collective-permute-start | bytes 393224 | tf_op jit(solution)/shard_map/ppermute | solution.py:111
  19.5 3.9 %collective-permute-done.6 = bf16[2,256,128]{2,1,0:T(8,128)(2,1)S(1)} collective-permute-done((bf16[2,256,128]{2,1,0:T(8,128)(2,1)S(1)}, bf16[2,256,128]{2,1,0:T(8,128)(2,1)S(1)}, u32[]{:S(2)}, u32[]{:S(2)}) %collective-permute-start.6) | collective-permute-done | bytes 131104 | tf_op jit(solution)/shard_map/ppermute | solution.py:111
  23.3 1.6 %collective-permute-start.8 = (bf16[256,256]{1,0:T(8,128)(2,1)}, bf16[256,256]{1,0:T(8,128)(2,1)S(1)}, u32[]{:S(2)}, u32[]{:S(2)}) collective-permute-start(bf16[256,256]{1,0:T(8,128)(2,1)} %bitcast.52), channel_id=1, source_target_pairs={{0,12},{4,8},{8,4},{12,0},{1,13},{5,9},{9,5},{13,1},{2,14},{6,10},... | collective-permute-start | bytes 393224 | tf_op jit(solution)/shard_map/ppermute | solution.py:111
  25.0 0.0 collective-permute-done.4
  25.0 0.0 collective-permute-done.3
  25.0 0.1 pad_maximum_fusion.near_ref
  25.1 0.1 collective-permute-start.7
  25.2 0.0 copy-done.1
  25.2 0.1 reshape.61
  25.3 0.1 reshape.67
  25.4 0.1 reshape.65
  25.5 0.1 reshape.63
  25.6 0.1 concatenate.13.facts
  25.7 0.8 %near.1 = (bf16[8,256,256]{2,1,0:T(8,128)(2,1)S(1)}, bf16[1024,256]{1,0:T(8,128)(2,1)S(1)}) custom-call(s32[36]{0:T(128)S(1)} %concatenate.13.facts, bf16[2,256,512]{2,1,0:T(8,128)(2,1)S(1)} %bitcast_dynamic-update-slice_fusion.mine_ref, bf16[4,3,256,128]{3,2,1,0:T(8,128)(2,1)S(1)} %pad_maximum_fusion.near_ref), custom_call_target="tpu_custom_call" | custom-call | bytes 1048576 | tf_op jit(solution)/shard_map/near/pallas_call | solution.py:380
  26.5 1.0 %collective-permute-done.7.far_ref = bf16[4,3,256,128]{3,2,1,0:T(8,128)(2,1)S(1)} collective-permute-done((bf16[4,3,256,128]{3,2,1,0:T(8,128)(2,1)S(1)}, bf16[4,3,256,128]{3,2,1,0:T(8,128)(2,1)S(1)}, u32[]{:S(2)}, u32[]{:S(2)}) %collective-permute-start.7) | collective-permute-done | bytes 786464 | tf_op jit(solution)/shard_map/ppermute | solution.py:111
  27.5 0.0 copy-start
  27.5 4.1 %powers.1 = (bf16[8,256,256]{2,1,0:T(8,128)(2,1)S(1)}, bf16[1024,1536]{1,0:T(8,128)(2,1)S(1)}) custom-call(s32[36]{0:T(128)S(1)} %concatenate.13.facts, bf16[2,256,512]{2,1,0:T(8,128)(2,1)S(1)} %bitcast_dynamic-update-slice_fusion.mine_ref, bf16[4,3,256,128]{3,2,1,0:T(8,128)(2,1)S(1)} %collective-permute-done.7.far_ref, ...), custom_call_target="tpu_custom_call" | custom-call | flops 2684354560 | bytes 1048576 | tf_op jit(solution)/shard_map/powers/pallas_call | solution.py:389
  31.6 0.0 collective-permute-done.10.refs_3_
  31.6 0.0 collective-permute-done.9.refs_2_
  31.6 0.0 collective-permute-done.8.refs_1_
  31.6 0.0 copy-done
  31.6 7.3 %main.1 = (f32[256,256]{1,0:T(8,128)S(1)}, f32[2,256,256]{2,1,0:T(8,128)S(1)}, bf16[1024,512]{1,0:T(8,128)(2,1)S(1)}, bf16[1024,512]{1,0:T(8,128)(2,1)S(1)}, bf1...) custom-call(s32[36]{0:T(128)S(1)} %concatenate.13.facts, ...), custom_call_target="tpu_custom_call" | custom-call | flops 4294967296 | bytes 1048576 | tf_op jit(solution)/shard_map/main/pallas_call | solution.py:405
  38.9 0.2 collective-permute-start.11
  39.1 1.8 %collective-permute-done.11 = f32[2,256,256]{2,1,0:T(8,128)S(1)} collective-permute-done((f32[2,256,256]{2,1,0:T(8,128)S(1)}, f32[2,256,256]{2,1,0:T(8,128)S(1)}, u32[]{:S(2)}, u32[]{:S(2)}) %collective-permute-start.11) | collective-permute-done | bytes 524320 | tf_op jit(solution)/shard_map/ppermute | solution.py:111
  40.9 1.5 %collective-permute-start.12 = (bf16[256,256]{1,0:T(8,128)(2,1)S(1)}, bf16[256,256]{1,0:T(8,128)(2,1)S(1)}, u32[]{:S(2)}, u32[]{:S(2)}) collective-permute-start(bf16[256,256]{1,0:T(8,128)(2,1)S(1)} %fusion.1), channel_id=1, source_target_pairs={{0,2},{2,0},{1,3},{3,1},{4,6},{6,4},{5,7},{7,5},{8,10},{10,8},{9,1... | collective-permute-start | bytes 393224 | tf_op jit(solution)/shard_map/ppermute | solution.py:111
  42.5 2.7 %own.1 = f32[256,256]{1,0:T(8,128)S(1)} custom-call(s32[36]{0:T(128)S(1)} %concatenate.13.facts, bf16[1024,1536]{1,0:T(8,128)(2,1)S(1)} %get-tuple-element.19.refs_6_.c_ref, bf16[1024,512]{1,0:T(8,128)(2,1)S(1)} %get-tuple-element.21.n_ref, bf16[1024,512]{1,0:T(8,128)(2,1)S(1)} %get-tuple-element.22.v1_ref, bf16[1024,512]{1,0:T(8,128)(2,1)S(1)} %get-tuple-element.23.v2_ref, ...), custom_call_target="tpu_custom_call" | custom-call | flops 1073741824 | bytes 1048576 | tf_op jit(solution)/shard_map/own/pallas_call | solution.py:426
  45.2 1.3 %collective-permute-done.12 = bf16[256,256]{1,0:T(8,128)(2,1)S(1)} collective-permute-done((bf16[256,256]{1,0:T(8,128)(2,1)S(1)}, bf16[256,256]{1,0:T(8,128)(2,1)S(1)}, u32[]{:S(2)}, u32[]{:S(2)}) %collective-permute-start.12) | collective-permute-done | bytes 131104 | tf_op jit(solution)/shard_map/ppermute | solution.py:111
  46.5 0.8 %fusion.4 = f32[1,256,256]{2,1,0:T(8,128)} fusion(f32[2,256,256]{2,1,0:T(8,128)S(1)} %collective-permute-done.11, bf16[256,256]{1,0:T(8,128)(2,1)S(1)} %collective-permute-done.12, f32[256,256]{1,0:T(8,128)S(1)} %own.1, bf16[1,256,256]{2,1,0:T(8,128)(2,1)S(1)} %copy-done), kind=kLoop, calls=%fused_computation.9 | loop fusion | flops 327680 | bytes 1048576 | tf_op jit(solution)/shard_map/broadcast_in_dim | solution.py:437
  (12 shorter events, 0.2 us)
Async XLA Ops:
  0.0 25.2 %copy-start.1 = (bf16[2,4,128,128]{3,2,1,0:T(8,128)(2,1)S(1)}, bf16[2,4,128,128]{3,2,1,0:T(8,128)(2,1)}, u32[]{:S(2)}) copy-start(bf16[2,4,128,128]{3,2,1,0:T(8,128)(2,1)} %param.5) | copy-start | bytes 786436
  1.7 7.8 %collective-permute-start.2 = (bf16[272,128]{1,0:T(8,128)(2,1)S(1)}, bf16[272,128]{1,0:T(8,128)(2,1)S(1)}, u32[]{:S(2)}, u32[]{:S(2)}) collective-permute-start(bf16[272,128]{1,0:T(8,128)(2,1)S(1)} %fusion.6), channel_id=1, source_target_pairs={{0,12},{4,8},{8,4},{12,0},{1,13},{5,9},{9,5},{13,1},{2,14},{6,10},... | collective-permute-start | bytes 208904 | tf_op jit(solution)/shard_map/ppermute | solution.py:111
  6.8 6.0 %collective-permute-start.1 = (bf16[272,128]{1,0:T(8,128)(2,1)S(1)}, bf16[272,128]{1,0:T(8,128)(2,1)S(1)}, u32[]{:S(2)}, u32[]{:S(2)}) collective-permute-start(bf16[272,128]{1,0:T(8,128)(2,1)S(1)} %fusion.6), channel_id=1, source_target_pairs={{0,8},{4,12},{8,0},{12,4},{1,9},{5,13},{9,1},{13,5},{2,10},{6,14},... | collective-permute-start | bytes 208904 | tf_op jit(solution)/shard_map/ppermute | solution.py:111
  6.8 6.4 %collective-permute-start = (bf16[272,128]{1,0:T(8,128)(2,1)S(1)}, bf16[272,128]{1,0:T(8,128)(2,1)S(1)}, u32[]{:S(2)}, u32[]{:S(2)}) collective-permute-start(bf16[272,128]{1,0:T(8,128)(2,1)S(1)} %fusion.6), channel_id=1, source_target_pairs={{0,4},{4,0},{8,12},{12,8},{1,5},{5,1},{9,13},{13,9},{2,6},{6,2},{1... | collective-permute-start | bytes 208904 | tf_op jit(solution)/shard_map/ppermute | solution.py:111
  7.5 10.4 %collective-permute-start.5 = (bf16[256,128]{1,0:T(8,128)(2,1)S(1)}, bf16[256,128]{1,0:T(8,128)(2,1)S(1)}, u32[]{:S(2)}, u32[]{:S(2)}) collective-permute-start(bf16[256,128]{1,0:T(8,128)(2,1)S(1)} %bitcast.60), channel_id=1, source_target_pairs={{0,4},{4,0},{8,12},{12,8},{1,5},{5,1},{9,13},{13,9},{2,6},{6,2},{1... | collective-permute-start | bytes 196616 | tf_op jit(solution)/shard_map/ppermute | solution.py:111
  8.8 22.8 %collective-permute-start.10 = (bf16[256,256]{1,0:T(8,128)(2,1)}, bf16[256,256]{1,0:T(8,128)(2,1)S(1)}, u32[]{:S(2)}, u32[]{:S(2)}) collective-permute-start(bf16[256,256]{1,0:T(8,128)(2,1)} %bitcast.50), channel_id=1, source_target_pairs={{0,4},{4,0},{8,12},{12,8},{1,5},{5,1},{9,13},{13,9},{2,6},{6,2},{1... | collective-permute-start | bytes 393224 | tf_op jit(solution)/shard_map/ppermute | solution.py:111
  13.3 11.7 %collective-permute-start.4 = (bf16[3,256,128]{2,1,0:T(8,128)(2,1)S(1)}, bf16[3,256,128]{2,1,0:T(8,128)(2,1)S(1)}, u32[]{:S(2)}, u32[]{:S(2)}) collective-permute-start(bf16[3,256,128]{2,1,0:T(8,128)(2,1)S(1)} %pad_maximum_fusion.1), channel_id=1, source_target_pairs={{0,16},{2,18},{16,0},{18,2},{1,17},{3,19},{17,1},{19,3},{4,20},{6,... | collective-permute-start | bytes 589832 | tf_op jit(solution)/shard_map/ppermute | solution.py:111
  15.0 10.0 %collective-permute-start.3 = (bf16[3,256,128]{2,1,0:T(8,128)(2,1)S(1)}, bf16[3,256,128]{2,1,0:T(8,128)(2,1)S(1)}, u32[]{:S(2)}, u32[]{:S(2)}) collective-permute-start(bf16[3,256,128]{2,1,0:T(8,128)(2,1)S(1)} %pad_maximum_fusion.1), channel_id=1, source_target_pairs={{0,2},{2,0},{16,18},{18,16},{1,3},{3,1},{17,19},{19,17},{4,6},{6,4... | collective-permute-start | bytes 589832 | tf_op jit(solution)/shard_map/ppermute | solution.py:111
  16.5 6.8 %collective-permute-start.6 = (bf16[2,256,128]{2,1,0:T(8,128)(2,1)S(1)}, bf16[2,256,128]{2,1,0:T(8,128)(2,1)S(1)}, u32[]{:S(2)}, u32[]{:S(2)}) collective-permute-start(bf16[2,256,128]{2,1,0:T(8,128)(2,1)S(1)} %slice.43), channel_id=1, source_target_pairs={{0,18},{2,16},{16,2},{18,0},{1,19},{3,17},{17,3},{19,1},{4,22},{6,... | collective-permute-start | bytes 393224 | tf_op jit(solution)/shard_map/ppermute | solution.py:111
  17.8 13.8 %collective-permute-start.9 = (bf16[256,256]{1,0:T(8,128)(2,1)}, bf16[256,256]{1,0:T(8,128)(2,1)S(1)}, u32[]{:S(2)}, u32[]{:S(2)}) collective-permute-start(bf16[256,256]{1,0:T(8,128)(2,1)} %bitcast.51), channel_id=1, source_target_pairs={{0,8},{4,12},{8,0},{12,4},{1,9},{5,13},{9,1},{13,5},{2,10},{6,14},... | collective-permute-start | bytes 393224 | tf_op jit(solution)/shard_map/ppermute | solution.py:111
  23.3 8.3 %collective-permute-start.8 = (bf16[256,256]{1,0:T(8,128)(2,1)}, bf16[256,256]{1,0:T(8,128)(2,1)S(1)}, u32[]{:S(2)}, u32[]{:S(2)}) collective-permute-start(bf16[256,256]{1,0:T(8,128)(2,1)} %bitcast.52), channel_id=1, source_target_pairs={{0,12},{4,8},{8,4},{12,0},{1,13},{5,9},{9,5},{13,1},{2,14},{6,10},... | collective-permute-start | bytes 393224 | tf_op jit(solution)/shard_map/ppermute | solution.py:111
  25.1 2.4 %collective-permute-start.7 = (bf16[4,3,256,128]{3,2,1,0:T(8,128)(2,1)S(1)}, bf16[4,3,256,128]{3,2,1,0:T(8,128)(2,1)S(1)}, u32[]{:S(2)}, u32[]{:S(2)}) collective-permute-start(bf16[4,3,256,128]{3,2,1,0:T(8,128)(2,1)S(1)} %pad_maximum_fusion.near_ref), channel_id=1, source_target_pairs={{0,1},{1,0},{2,3},{3,2},{4,5},{5,4},{6,7},{7,6},{8,9},{9,8},{10,11... | collective-permute-start | bytes 2359304 | tf_op jit(solution)/shard_map/ppermute | solution.py:111
  27.5 4.2 %copy-start = (bf16[1,256,256]{2,1,0:T(8,128)(2,1)S(1)}, bf16[1,256,256]{2,1,0:T(8,128)(2,1)}, u32[]{:S(2)}) copy-start(bf16[1,256,256]{2,1,0:T(8,128)(2,1)} %param.4) | copy-start | bytes 393220
  38.9 2.0 %collective-permute-start.11 = (f32[2,256,256]{2,1,0:T(8,128)S(1)}, f32[2,256,256]{2,1,0:T(8,128)S(1)}, u32[]{:S(2)}, u32[]{:S(2)}) collective-permute-start(f32[2,256,256]{2,1,0:T(8,128)S(1)} %get-tuple-element.27), channel_id=1, source_target_pairs={{0,1},{1,0},{2,3},{3,2},{4,5},{5,4},{6,7},{7,6},{8,9},{9,8},{10,11... | collective-permute-start | bytes 1572872 | tf_op jit(solution)/shard_map/ppermute | solution.py:111
  40.9 5.6 %collective-permute-start.12 = (bf16[256,256]{1,0:T(8,128)(2,1)S(1)}, bf16[256,256]{1,0:T(8,128)(2,1)S(1)}, u32[]{:S(2)}, u32[]{:S(2)}) collective-permute-start(bf16[256,256]{1,0:T(8,128)(2,1)S(1)} %fusion.1), channel_id=1, source_target_pairs={{0,2},{2,0},{1,3},{3,1},{4,6},{6,4},{5,7},{7,5},{8,10},{10,8},{9,1... | collective-permute-start | bytes 393224 | tf_op jit(solution)/shard_map/ppermute | solution.py:111

commit v8 on v6

--- a/solution.py
+++ b/solution.py
@@ -285,23 +285,15 @@
             tops[span, :] += 0.5 * v2
     for at in range(bands * local):
         span = slice(at * block, (at + 1) * block)
-        if at < local:
-            v3 = apply_a(dims, facts, h_refs, at, lambda where: v2_ref[where, :], cols)
-            tops[span, :] += v3 * (1.0 / 6.0)
-            slab[span, :] += thin(v3) * (1.0 / 6.0)
-        else:
-            v3 = apply_a(
-                dims,
-                facts,
-                h_refs,
-                at,
-                lambda where: jnp.concatenate(
-                    [v2_ref[where, 0:piece], v2_ref[where, cols : cols + piece]],
-                    axis=1,
-                ),
-                piece,
-            )
-            slab[span, :] += v3 * (1.0 / 6.0)
+        v3 = apply_a(
+            dims,
+            facts,
+            h_refs,
+            at,
+            lambda where: jnp.concatenate([v2_ref[where, 0:piece], v2_ref[where, cols : cols + piece]], axis=1),
+            piece,
+        )
+        slab[span, :] += v3 * (1.0 / 6.0)
     own = slice(0, rows)
     three = 3 * cols
     for m, t_ref in enumerate((n_ref, v1_ref, v2_ref)):
@@ -321,15 +313,20 @@
     keep_ref[...] = target(2)
 
 
-def own_kernel(dims, facts, c_ref, n_ref, v1_ref, v2_ref, left, slab, tops, own_ref, outs):
+def own_kernel(dims, facts, near_h, far_h, c_ref, n_ref, v1_ref, v2_ref, left, slab, tops, own_ref, outs):
     bands, rows, cols, piece, local, count, block, per = dims
     r, q = facts[0], facts[1]
     target = products(dims, facts, (q,), c_ref, n_ref, v1_ref, v2_ref, left, slab, outs)
     col_iota = lax.broadcasted_iota(jnp.int32, (rows, cols), 1)
     col_abs = col_iota // piece * rows + q * piece + col_iota % piece
     row_abs = r * rows + lax.broadcasted_iota(jnp.int32, (rows, cols), 0)
-    real = swap_groups(tops[:, :cols], r, piece)
-    imag = swap_groups(tops[:, cols:], r, piece)
+    v3 = jnp.concatenate(
+        [apply_a(dims, facts, (near_h, far_h), at, lambda where: v2_ref[where, :], cols) for at in range(local)],
+        axis=0,
+    )
+    direct = tops[...] + v3 * (1.0 / 6.0)
+    real = swap_groups(direct[:, :cols], r, piece)
+    imag = swap_groups(direct[:, cols:], r, piece)
     own_ref[...] = target(0) + jnp.where(row_abs <= col_abs, real, imag)
 
 
@@ -426,13 +423,13 @@
     own = pl.pallas_call(
         functools.partial(own_kernel, dims),
         out_shape=block_shape,
-        in_specs=[smem] + [vmem] * 7,
+        in_specs=[smem] + [vmem] * 9,
         out_specs=vmem,
         scratch_shapes=[pltpu.VMEM((bands, piece, rows), F32)],
         compiler_params=pltpu.CompilerParams(vmem_limit_bytes=OWN_VMEM),
         cost_estimate=pl.CostEstimate(flops=step, bytes_accessed=2**20, transcendentals=0),
         name="own",
-    )(facts, c_side, *state)
+    )(facts, near_h, far_h, c_side, *state)
     total = here.astype(F32) + own + swapped[1].astype(F32) + across.astype(F32)
     return total[None]
 

time: 47.1 us -> 47 us (level)
  transfers between devices with their start and end apart: 13 -> 13, of which waited for: 6 -> 6; matrix products, arithmetic and copies ran while one was open for 3% -> 3% of each run, Pallas kernels for 16% -> 17%
where the time goes in v8:
time: 47 us; the launch traced here: 46.8 us
  starting transfers between devices  16.4 us (35%)
  Pallas kernels  15.1 us (32%)
  waiting for transfers between devices  11 us (23%)
  other arithmetic  2.63 us (6%)
  local copies, waits for them, and re-layouts  1.45 us (3%)
    ppermute x13, starting transfers between devices, exchange(): return lax.ppermute(block, axes, [(i, i ^ offset) for i in range(count)])  16.4 us
    ppermute x13, waiting for transfers between devices, exchange(): return lax.ppermute(block, axes, [(i, i ^ offset) for i in range(count)])  11 us
    pallas_call x1, Pallas kernels, gathered_body(): pl.pallas_call(functools.partial(main_kernel, dims), out_shape=(block_sha...  7.1 us
    pallas_call x1, Pallas kernels, gathered_body(): pl.pallas_call(functools.partial(powers_kernel, dims), out_shape=(half_sh...  4.19 us
    pallas_call x1, Pallas kernels, gathered_body(): pl.pallas_call(functools.partial(own_kernel, dims), out_shape=block_shape...  3.05 us
    unnamed x5, local copies, waits for them, and re-layouts  0.99 us
    select_n x1, other arithmetic, pick(): jnp.where(lax.axis_index('runs') == 0, lax.dynamic_slice_in_dim(first, at...  0.95 us
  transfers between devices with their start and end apart: 13, of which 6 were waited for; matrix products, arithmetic and copies ran while one was open for 3% of the time, Pallas kernels for 17%

profile of v8, /device:TPU:0, one launch (start us, length us, event | category | flops | bytes accessed | tf_op | source)
XLA Modules:
  0.0 46.8 jit_solution(5022916386470092984)
XLA Ops:
  0.0 0.0 copy-start.1
  0.0 0.7 %fusion.5 = (s32[2,4]{1,0:T(2,128)S(1)}, bf16[2,4]{1,0:T(2,128)(2,1)S(1)}) fusion(s32[2,4]{1,0:T(2,128)} %param.7), kind=kLoop, calls=%fused_computation.23 | loop fusion | flops 16 | bytes 80 | tf_op jit(solution)/shard_map/reshape | solution.py:367
  0.7 1.0 %dynamic-slice_select_fusion = (bf16[2,128,128]{2,1,0:T(8,128)(2,1)S(1)}, bf16[2,128,128]{2,1,0:T(8,128)(2,1)S(1)}) fusion(bf16[8,128,128]{2,1,0:T(8,128)(2,1)} %bitcast.52, s32[]{:T(128)S(6)} %select_n.23, bf16[8,128,128]{2,1,0:T(8,128)(2,1)} %bitcast.51, pred[]{:T(512)S(6)} %eq.4, s32[]{:T(128)S(6)} %select_n.21), kind=kLoop, calls=%fused_computation.18 | loop fusion | flops 65536 | bytes 393225 | tf_op jit(solution)/shard_map/jit(_where)/select_n | solution.py:353
  1.7 5.1 %collective-permute-start.2 = (bf16[272,128]{1,0:T(8,128)(2,1)S(1)}, bf16[272,128]{1,0:T(8,128)(2,1)S(1)}, u32[]{:S(2)}, u32[]{:S(2)}) collective-permute-start(bf16[272,128]{1,0:T(8,128)(2,1)S(1)} %fusion.4), channel_id=1, source_target_pairs={{0,12},{4,8},{8,4},{12,0},{1,13},{5,9},{9,5},{13,1},{2,14},{6,10},... | collective-permute-start | bytes 208904 | tf_op jit(solution)/shard_map/ppermute | solution.py:111
  6.8 0.0 collective-permute-start.1
  6.8 0.6 %collective-permute-start = (bf16[272,128]{1,0:T(8,128)(2,1)S(1)}, bf16[272,128]{1,0:T(8,128)(2,1)S(1)}, u32[]{:S(2)}, u32[]{:S(2)}) collective-permute-start(bf16[272,128]{1,0:T(8,128)(2,1)S(1)} %fusion.4), channel_id=1, source_target_pairs={{0,4},{4,0},{8,12},{12,8},{1,5},{5,1},{9,13},{13,9},{2,6},{6,2},{1... | collective-permute-start | bytes 208904 | tf_op jit(solution)/shard_map/ppermute | solution.py:111
  7.5 1.4 %collective-permute-start.5 = (bf16[256,128]{1,0:T(8,128)(2,1)S(1)}, bf16[256,128]{1,0:T(8,128)(2,1)S(1)}, u32[]{:S(2)}, u32[]{:S(2)}) collective-permute-start(bf16[256,128]{1,0:T(8,128)(2,1)S(1)} %bitcast.56), channel_id=1, source_target_pairs={{0,4},{4,0},{8,12},{12,8},{1,5},{5,1},{9,13},{13,9},{2,6},{6,2},{1... | collective-permute-start | bytes 196616 | tf_op jit(solution)/shard_map/ppermute | solution.py:111
  8.8 0.7 %collective-permute-start.10 = (bf16[256,256]{1,0:T(8,128)(2,1)}, bf16[256,256]{1,0:T(8,128)(2,1)S(1)}, u32[]{:S(2)}, u32[]{:S(2)}) collective-permute-start(bf16[256,256]{1,0:T(8,128)(2,1)} %bitcast.46), channel_id=1, source_target_pairs={{0,4},{4,0},{8,12},{12,8},{1,5},{5,1},{9,13},{13,9},{2,6},{6,2},{1... | collective-permute-start | bytes 393224 | tf_op jit(solution)/shard_map/ppermute | solution.py:111
  9.5 0.0 collective-permute-done.2
  9.5 3.3 %collective-permute-done.1 = bf16[272,128]{1,0:T(8,128)(2,1)S(1)} collective-permute-done((bf16[272,128]{1,0:T(8,128)(2,1)S(1)}, bf16[272,128]{1,0:T(8,128)(2,1)S(1)}, u32[]{:S(2)}, u32[]{:S(2)}) %collective-permute-start.1) | collective-permute-done | bytes 69664 | tf_op jit(solution)/shard_map/ppermute | solution.py:111
  12.8 0.4 collective-permute-done
  13.3 1.7 %collective-permute-start.4 = (bf16[3,256,128]{2,1,0:T(8,128)(2,1)S(1)}, bf16[3,256,128]{2,1,0:T(8,128)(2,1)S(1)}, u32[]{:S(2)}, u32[]{:S(2)}) collective-permute-start(bf16[3,256,128]{2,1,0:T(8,128)(2,1)S(1)} %pad_maximum_fusion.1), channel_id=1, source_target_pairs={{0,16},{2,18},{16,0},{18,2},{1,17},{3,19},{17,1},{19,3},{4,20},{6,... | collective-permute-start | bytes 589832 | tf_op jit(solution)/shard_map/ppermute | solution.py:111
  15.0 1.5 %collective-permute-start.3 = (bf16[3,256,128]{2,1,0:T(8,128)(2,1)S(1)}, bf16[3,256,128]{2,1,0:T(8,128)(2,1)S(1)}, u32[]{:S(2)}, u32[]{:S(2)}) collective-permute-start(bf16[3,256,128]{2,1,0:T(8,128)(2,1)S(1)} %pad_maximum_fusion.1), channel_id=1, source_target_pairs={{0,2},{2,0},{16,18},{18,16},{1,3},{3,1},{17,19},{19,17},{4,6},{6,4... | collective-permute-start | bytes 589832 | tf_op jit(solution)/shard_map/ppermute | solution.py:111
  16.5 0.3 collective-permute-start.6
  16.8 1.0 %bitcast_dynamic-update-slice_fusion.1 = bf16[2,256,512]{2,1,0:T(8,128)(2,1)S(1)} fusion(bf16[2,4,128,128]{3,2,1,0:T(8,128)(2,1)} %param.6), kind=kLoop, calls=%fused_computation.2 | loop fusion | bytes 524288
  17.8 0.0 collective-permute-done.5
  17.8 1.6 %collective-permute-start.9 = (bf16[256,256]{1,0:T(8,128)(2,1)}, bf16[256,256]{1,0:T(8,128)(2,1)S(1)}, u32[]{:S(2)}, u32[]{:S(2)}) collective-permute-start(bf16[256,256]{1,0:T(8,128)(2,1)} %bitcast.47), channel_id=1, source_target_pairs={{0,8},{4,12},{8,0},{12,4},{1,9},{5,13},{9,1},{13,5},{2,10},{6,14},... | collective-permute-start | bytes 393224 | tf_op jit(solution)/shard_map/ppermute | solution.py:111
  19.5 3.9 %collective-permute-done.6 = bf16[2,256,128]{2,1,0:T(8,128)(2,1)S(1)} collective-permute-done((bf16[2,256,128]{2,1,0:T(8,128)(2,1)S(1)}, bf16[2,256,128]{2,1,0:T(8,128)(2,1)S(1)}, u32[]{:S(2)}, u32[]{:S(2)}) %collective-permute-start.6) | collective-permute-done | bytes 131104 | tf_op jit(solution)/shard_map/ppermute | solution.py:111
  23.3 1.6 %collective-permute-start.8 = (bf16[256,256]{1,0:T(8,128)(2,1)}, bf16[256,256]{1,0:T(8,128)(2,1)S(1)}, u32[]{:S(2)}, u32[]{:S(2)}) collective-permute-start(bf16[256,256]{1,0:T(8,128)(2,1)} %bitcast.48), channel_id=1, source_target_pairs={{0,12},{4,8},{8,4},{12,0},{1,13},{5,9},{9,5},{13,1},{2,14},{6,10},... | collective-permute-start | bytes 393224 | tf_op jit(solution)/shard_map/ppermute | solution.py:111
  25.0 0.0 collective-permute-done.4
  25.0 0.0 collective-permute-done.3
  25.0 0.1 pad_maximum_fusion.near_ref
  25.1 0.1 collective-permute-start.7
  25.2 0.0 copy-done.1
  25.2 0.1 reshape.65
  25.3 0.1 reshape.71
  25.4 0.1 reshape.69
  25.5 0.1 reshape.67
  25.6 0.1 concatenate.13.facts
  25.7 0.8 %near.1 = (bf16[8,256,256]{2,1,0:T(8,128)(2,1)S(1)}, bf16[1024,256]{1,0:T(8,128)(2,1)S(1)}) custom-call(s32[36]{0:T(128)S(1)} %concatenate.13.facts, bf16[2,256,512]{2,1,0:T(8,128)(2,1)S(1)} %bitcast_dynamic-update-slice_fusion.mine_ref, bf16[4,3,256,128]{3,2,1,0:T(8,128)(2,1)S(1)} %pad_maximum_fusion.near_ref), custom_call_target="tpu_custom_call" | custom-call | bytes 1048576 | tf_op jit(solution)/shard_map/near/pallas_call | solution.py:377
  26.5 1.0 %collective-permute-done.7.far_ref = bf16[4,3,256,128]{3,2,1,0:T(8,128)(2,1)S(1)} collective-permute-done((bf16[4,3,256,128]{3,2,1,0:T(8,128)(2,1)S(1)}, bf16[4,3,256,128]{3,2,1,0:T(8,128)(2,1)S(1)}, u32[]{:S(2)}, u32[]{:S(2)}) %collective-permute-start.7) | collective-permute-done | bytes 786464 | tf_op jit(solution)/shard_map/ppermute | solution.py:111
  27.5 0.0 copy-start
  27.5 4.2 %powers.1 = (bf16[8,256,256]{2,1,0:T(8,128)(2,1)S(1)}, bf16[1024,1536]{1,0:T(8,128)(2,1)S(1)}) custom-call(s32[36]{0:T(128)S(1)} %concatenate.13.facts, bf16[2,256,512]{2,1,0:T(8,128)(2,1)S(1)} %bitcast_dynamic-update-slice_fusion.mine_ref, bf16[4,3,256,128]{3,2,1,0:T(8,128)(2,1)S(1)} %collective-permute-done.7.far_ref, ...), custom_call_target="tpu_custom_call" | custom-call | flops 2684354560 | bytes 1048576 | tf_op jit(solution)/shard_map/powers/pallas_call | solution.py:386
  31.7 0.0 collective-permute-done.10.refs_3_
  31.7 0.0 collective-permute-done.9.refs_2_
  31.7 0.0 collective-permute-done.8.refs_1_
  31.7 0.0 copy-done
  31.7 7.1 %main.1 = (f32[256,256]{1,0:T(8,128)S(1)}, bf16[2,256,256]{2,1,0:T(8,128)(2,1)S(1)}, bf16[1024,512]{1,0:T(8,128)(2,1)S(1)}, bf16[1024,512]{1,0:T(8,128)(2,1)S(1)...) custom-call(s32[36]{0:T(128)S(1)} %concatenate.13.facts, ...), custom_call_target="tpu_custom_call" | custom-call | flops 4294967296 | bytes 1048576 | tf_op jit(solution)/shard_map/main/pallas_call | solution.py:402
  38.8 0.2 collective-permute-start.11
  39.0 1.4 %collective-permute-done.11 = bf16[2,256,256]{2,1,0:T(8,128)(2,1)S(1)} collective-permute-done((bf16[2,256,256]{2,1,0:T(8,128)(2,1)S(1)}, bf16[2,256,256]{2,1,0:T(8,128)(2,1)S(1)}, u32[]{:S(2)}, u32[]{:S(2)}) %collective-permute-start.11) | collective-permute-done | bytes 262176 | tf_op jit(solution)/shard_map/ppermute | solution.py:111
  40.4 1.5 %collective-permute-start.12 = (bf16[256,256]{1,0:T(8,128)(2,1)S(1)}, bf16[256,256]{1,0:T(8,128)(2,1)S(1)}, u32[]{:S(2)}, u32[]{:S(2)}) collective-permute-start(bf16[256,256]{1,0:T(8,128)(2,1)S(1)} %fusion), channel_id=1, source_target_pairs={{0,2},{2,0},{1,3},{3,1},{4,6},{6,4},{5,7},{7,5},{8,10},{10,8},{9,1... | collective-permute-start | bytes 393224 | tf_op jit(solution)/shard_map/ppermute | solution.py:111
  42.0 3.0 %own.1 = f32[256,256]{1,0:T(8,128)S(1)} custom-call(s32[36]{0:T(128)S(1)} %concatenate.13.facts, bf16[8,256,256]{2,1,0:T(8,128)(2,1)S(1)} %get-tuple-element.17.near_h.refs_4_, bf16[8,256,256]{2,1,0:T(8,128)(2,1)S(1)} %get-tuple-element.19.refs_5_.far_h, bf16[1024,1536]{1,0:T(8,128)(2,1)S(1)} %get-tuple-element.20.refs_6_.c_ref, ...), custom_call_target="tpu_custom_call" | custom-call | flops 1073741824 | bytes 1048576 | tf_op jit(solution)/shard_map/own/pallas_call | solution.py:423
  45.0 1.0 %collective-permute-done.12 = bf16[256,256]{1,0:T(8,128)(2,1)S(1)} collective-permute-done((bf16[256,256]{1,0:T(8,128)(2,1)S(1)}, bf16[256,256]{1,0:T(8,128)(2,1)S(1)}, u32[]{:S(2)}, u32[]{:S(2)}) %collective-permute-start.12) | collective-permute-done | bytes 131104 | tf_op jit(solution)/shard_map/ppermute | solution.py:111
  46.0 0.8 %fusion.2 = f32[1,256,256]{2,1,0:T(8,128)} fusion(bf16[256,256]{1,0:T(8,128)(2,1)S(1)} %collective-permute-done.12, f32[256,256]{1,0:T(8,128)S(1)} %own.1, bf16[2,256,256]{2,1,0:T(8,128)(2,1)S(1)} %collective-permute-done.11, bf16[1,256,256]{2,1,0:T(8,128)(2,1)S(1)} %copy-done), kind=kLoop, calls=%fused_computation.7 | loop fusion | flops 393216 | bytes 917504 | tf_op jit(solution)/shard_map/broadcast_in_dim | solution.py:434
  (12 shorter events, 0.2 us)
Async XLA Ops:
  0.0 25.2 %copy-start.1 = (bf16[2,4,128,128]{3,2,1,0:T(8,128)(2,1)S(1)}, bf16[2,4,128,128]{3,2,1,0:T(8,128)(2,1)}, u32[]{:S(2)}) copy-start(bf16[2,4,128,128]{3,2,1,0:T(8,128)(2,1)} %param.5) | copy-start | bytes 786436
  1.7 7.8 %collective-permute-start.2 = (bf16[272,128]{1,0:T(8,128)(2,1)S(1)}, bf16[272,128]{1,0:T(8,128)(2,1)S(1)}, u32[]{:S(2)}, u32[]{:S(2)}) collective-permute-start(bf16[272,128]{1,0:T(8,128)(2,1)S(1)} %fusion.4), channel_id=1, source_target_pairs={{0,12},{4,8},{8,4},{12,0},{1,13},{5,9},{9,5},{13,1},{2,14},{6,10},... | collective-permute-start | bytes 208904 | tf_op jit(solution)/shard_map/ppermute | solution.py:111
  6.8 6.0 %collective-permute-start.1 = (bf16[272,128]{1,0:T(8,128)(2,1)S(1)}, bf16[272,128]{1,0:T(8,128)(2,1)S(1)}, u32[]{:S(2)}, u32[]{:S(2)}) collective-permute-start(bf16[272,128]{1,0:T(8,128)(2,1)S(1)} %fusion.4), channel_id=1, source_target_pairs={{0,8},{4,12},{8,0},{12,4},{1,9},{5,13},{9,1},{13,5},{2,10},{6,14},... | collective-permute-start | bytes 208904 | tf_op jit(solution)/shard_map/ppermute | solution.py:111
  6.8 6.4 %collective-permute-start = (bf16[272,128]{1,0:T(8,128)(2,1)S(1)}, bf16[272,128]{1,0:T(8,128)(2,1)S(1)}, u32[]{:S(2)}, u32[]{:S(2)}) collective-permute-start(bf16[272,128]{1,0:T(8,128)(2,1)S(1)} %fusion.4), channel_id=1, source_target_pairs={{0,4},{4,0},{8,12},{12,8},{1,5},{5,1},{9,13},{13,9},{2,6},{6,2},{1... | collective-permute-start | bytes 208904 | tf_op jit(solution)/shard_map/ppermute | solution.py:111
  7.5 10.4 %collective-permute-start.5 = (bf16[256,128]{1,0:T(8,128)(2,1)S(1)}, bf16[256,128]{1,0:T(8,128)(2,1)S(1)}, u32[]{:S(2)}, u32[]{:S(2)}) collective-permute-start(bf16[256,128]{1,0:T(8,128)(2,1)S(1)} %bitcast.56), channel_id=1, source_target_pairs={{0,4},{4,0},{8,12},{12,8},{1,5},{5,1},{9,13},{13,9},{2,6},{6,2},{1... | collective-permute-start | bytes 196616 | tf_op jit(solution)/shard_map/ppermute | solution.py:111
  8.8 22.8 %collective-permute-start.10 = (bf16[256,256]{1,0:T(8,128)(2,1)}, bf16[256,256]{1,0:T(8,128)(2,1)S(1)}, u32[]{:S(2)}, u32[]{:S(2)}) collective-permute-start(bf16[256,256]{1,0:T(8,128)(2,1)} %bitcast.46), channel_id=1, source_target_pairs={{0,4},{4,0},{8,12},{12,8},{1,5},{5,1},{9,13},{13,9},{2,6},{6,2},{1... | collective-permute-start | bytes 393224 | tf_op jit(solution)/shard_map/ppermute | solution.py:111
  13.3 11.7 %collective-permute-start.4 = (bf16[3,256,128]{2,1,0:T(8,128)(2,1)S(1)}, bf16[3,256,128]{2,1,0:T(8,128)(2,1)S(1)}, u32[]{:S(2)}, u32[]{:S(2)}) collective-permute-start(bf16[3,256,128]{2,1,0:T(8,128)(2,1)S(1)} %pad_maximum_fusion.1), channel_id=1, source_target_pairs={{0,16},{2,18},{16,0},{18,2},{1,17},{3,19},{17,1},{19,3},{4,20},{6,... | collective-permute-start | bytes 589832 | tf_op jit(solution)/shard_map/ppermute | solution.py:111
  15.0 10.0 %collective-permute-start.3 = (bf16[3,256,128]{2,1,0:T(8,128)(2,1)S(1)}, bf16[3,256,128]{2,1,0:T(8,128)(2,1)S(1)}, u32[]{:S(2)}, u32[]{:S(2)}) collective-permute-start(bf16[3,256,128]{2,1,0:T(8,128)(2,1)S(1)} %pad_maximum_fusion.1), channel_id=1, source_target_pairs={{0,2},{2,0},{16,18},{18,16},{1,3},{3,1},{17,19},{19,17},{4,6},{6,4... | collective-permute-start | bytes 589832 | tf_op jit(solution)/shard_map/ppermute | solution.py:111
  16.5 6.8 %collective-permute-start.6 = (bf16[2,256,128]{2,1,0:T(8,128)(2,1)S(1)}, bf16[2,256,128]{2,1,0:T(8,128)(2,1)S(1)}, u32[]{:S(2)}, u32[]{:S(2)}) collective-permute-start(bf16[2,256,128]{2,1,0:T(8,128)(2,1)S(1)} %slice.43), channel_id=1, source_target_pairs={{0,18},{2,16},{16,2},{18,0},{1,19},{3,17},{17,3},{19,1},{4,22},{6,... | collective-permute-start | bytes 393224 | tf_op jit(solution)/shard_map/ppermute | solution.py:111
  17.8 13.8 %collective-permute-start.9 = (bf16[256,256]{1,0:T(8,128)(2,1)}, bf16[256,256]{1,0:T(8,128)(2,1)S(1)}, u32[]{:S(2)}, u32[]{:S(2)}) collective-permute-start(bf16[256,256]{1,0:T(8,128)(2,1)} %bitcast.47), channel_id=1, source_target_pairs={{0,8},{4,12},{8,0},{12,4},{1,9},{5,13},{9,1},{13,5},{2,10},{6,14},... | collective-permute-start | bytes 393224 | tf_op jit(solution)/shard_map/ppermute | solution.py:111
  23.3 8.3 %collective-permute-start.8 = (bf16[256,256]{1,0:T(8,128)(2,1)}, bf16[256,256]{1,0:T(8,128)(2,1)S(1)}, u32[]{:S(2)}, u32[]{:S(2)}) collective-permute-start(bf16[256,256]{1,0:T(8,128)(2,1)} %bitcast.48), channel_id=1, source_target_pairs={{0,12},{4,8},{8,4},{12,0},{1,13},{5,9},{9,5},{13,1},{2,14},{6,10},... | collective-permute-start | bytes 393224 | tf_op jit(solution)/shard_map/ppermute | solution.py:111
  25.1 2.4 %collective-permute-start.7 = (bf16[4,3,256,128]{3,2,1,0:T(8,128)(2,1)S(1)}, bf16[4,3,256,128]{3,2,1,0:T(8,128)(2,1)S(1)}, u32[]{:S(2)}, u32[]{:S(2)}) collective-permute-start(bf16[4,3,256,128]{3,2,1,0:T(8,128)(2,1)S(1)} %pad_maximum_fusion.near_ref), channel_id=1, source_target_pairs={{0,1},{1,0},{2,3},{3,2},{4,5},{5,4},{6,7},{7,6},{8,9},{9,8},{10,11... | collective-permute-start | bytes 2359304 | tf_op jit(solution)/shard_map/ppermute | solution.py:111
  27.5 4.2 %copy-start = (bf16[1,256,256]{2,1,0:T(8,128)(2,1)S(1)}, bf16[1,256,256]{2,1,0:T(8,128)(2,1)}, u32[]{:S(2)}) copy-start(bf16[1,256,256]{2,1,0:T(8,128)(2,1)} %param.4) | copy-start | bytes 393220
  38.8 1.6 %collective-permute-start.11 = (bf16[2,256,256]{2,1,0:T(8,128)(2,1)S(1)}, bf16[2,256,256]{2,1,0:T(8,128)(2,1)S(1)}, u32[]{:S(2)}, u32[]{:S(2)}) collective-permute-start(bf16[2,256,256]{2,1,0:T(8,128)(2,1)S(1)} %get-tuple-element.27), channel_id=1, source_target_pairs={{0,1},{1,0},{2,3},{3,2},{4,5},{5,4},{6,7},{7,6},{8,9},{9,8},{10,11... | collective-permute-start | bytes 786440 | tf_op jit(solution)/shard_map/ppermute | solution.py:111
  40.4 5.6 %collective-permute-start.12 = (bf16[256,256]{1,0:T(8,128)(2,1)S(1)}, bf16[256,256]{1,0:T(8,128)(2,1)S(1)}, u32[]{:S(2)}, u32[]{:S(2)}) collective-permute-start(bf16[256,256]{1,0:T(8,128)(2,1)S(1)} %fusion), channel_id=1, source_target_pairs={{0,2},{2,0},{1,3},{3,1},{4,6},{6,4},{5,7},{7,5},{8,10},{10,8},{9,1... | collective-permute-start | bytes 393224 | tf_op jit(solution)/shard_map/ppermute | solution.py:111

commit v9 on v8

--- a/solution.py
+++ b/solution.py
@@ -134,26 +134,26 @@
     return 0.5 * jnp.concatenate([real, imag], axis=1)
 
 
-def place_side(dims, facts, side, mine_ref, part_ref, h_ref):
+def place_side(dims, facts, side, mine_ref, first_ref, part_ref, h_ref):
     bands, rows, cols, piece, local, count, block, per = dims
     core = lax.bitwise_xor(facts[3], side)
     wide = per * block
     for b in range(local):
         h_ref[b] = mine_ref[b, :, pl.ds(pl.multiple_of(core * wide, wide), wide)]
-    for n in range(part_ref.shape[0]):
+    for n in range(part_ref.shape[0] + 1):
         flat = (lax.bitwise_xor(facts[2], n) * 2 + core) * per
         below = pl.ds(pl.multiple_of((1 - flat // (local * count)) * block, block), block)
         b = flat // count % local
         for k in range(1, bands):
             for at in range(per):
-                h_ref[k * local + b, below, at * block : (at + 1) * block] = part_ref[
-                    n, k - 1, at * block : (at + 1) * block, :
-                ]
-
-
-def near_kernel(dims, facts, mine_ref, near_ref, h_ref, sel_ref):
-    bands, rows, cols, piece, local, count, block, per = dims
-    place_side(dims, facts, 0, mine_ref, near_ref, h_ref)
+                span = slice(at * block, (at + 1) * block)
+                got = first_ref[k - 1, span, :] if n == 0 else part_ref[n - 1, k - 1, span, :]
+                h_ref[k * local + b, below, span] = got
+
+
+def near_kernel(dims, facts, mine_ref, first_ref, near_ref, h_ref, sel_ref):
+    bands, rows, cols, piece, local, count, block, per = dims
+    place_side(dims, facts, 0, mine_ref, first_ref, near_ref, h_ref)
     row_iota = lax.broadcasted_iota(jnp.int32, (rows, cols), 0)
     col_iota = lax.broadcasted_iota(jnp.int32, (rows, cols), 1)
     for k in range(bands):
@@ -161,9 +161,9 @@
         sel_ref[k * rows : (k + 1) * rows, :] = jnp.where(hit, 1.0, 0.0).astype(BF16)
 
 
-def powers_kernel(dims, facts, mine_ref, far_ref, near_h, sel, far_h, c_ref, c1_ref, c2_ref, csum):
-    bands, rows, cols, piece, local, count, block, per = dims
-    place_side(dims, facts, 1, mine_ref, far_ref, far_h)
+def powers_kernel(dims, facts, mine_ref, first_ref, far_ref, near_h, sel, far_h, c_ref, c1_ref, c2_ref, csum):
+    bands, rows, cols, piece, local, count, block, per = dims
+    place_side(dims, facts, 1, mine_ref, first_ref, far_ref, far_h)
     h_refs = (near_h, far_h)
 
     def put_d(span, m, value):
@@ -368,8 +368,9 @@
     facts = jnp.concatenate([jnp.stack([r, q, me_plane, me_core]).astype(jnp.int32)] + all_cols)
     theirs = lax.optimization_barrier(jnp.stack([a[:size] for a in arrived]))
     across_plane = jnp.concatenate([exchange(diagonal, "row", 1)[None], exchange(theirs[1:], ("runs", "col"), 3)], axis=0)
-    near = jnp.stack([theirs] + [exchange(theirs, ("runs", "col"), k) for k in (1, 2)] + [across_plane])
+    near = jnp.stack([exchange(theirs, ("runs", "col"), k) for k in (1, 2)] + [across_plane])
     rest = [exchange(here, "row", k) for k in range(bands - 1, 0, -1)]
+    first = exchange(theirs, "sub", 1)
     far = exchange(near, "sub", 1)
 
     step = 2 * order * 2 * count * block * 2 * cols
@@ -377,16 +378,16 @@
     near_h, sel = pl.pallas_call(
         functools.partial(near_kernel, dims),
         out_shape=(half_shape, jax.ShapeDtypeStruct((order, cols), BF16)),
-        in_specs=[smem] + [vmem] * 2,
+        in_specs=[smem] + [vmem] * 3,
         out_specs=(vmem, vmem),
         compiler_params=pltpu.CompilerParams(vmem_limit_bytes=NEAR_VMEM),
         cost_estimate=pl.CostEstimate(flops=0, bytes_accessed=2**20, transcendentals=0),
         name="near",
-    )(facts, mine, near)
+    )(facts, mine, theirs, near)
     far_h, c_side = pl.pallas_call(
         functools.partial(powers_kernel, dims),
         out_shape=(half_shape, jax.ShapeDtypeStruct((order, 6 * cols), BF16)),
-        in_specs=[smem] + [vmem] * 4,
+        in_specs=[smem] + [vmem] * 5,
         out_specs=(vmem, vmem),
         scratch_shapes=[
             pltpu.VMEM((order, 2 * cols), BF16),
@@ -396,7 +397,7 @@
         compiler_params=pltpu.CompilerParams(vmem_limit_bytes=POWERS_VMEM),
         cost_estimate=pl.CostEstimate(flops=5 * step // 2, bytes_accessed=2**20, transcendentals=0),
         name="powers",
-    )(facts, mine, far, near_h, sel)
+    )(facts, mine, first, far, near_h, sel)
     block_shape = jax.ShapeDtypeStruct((rows, cols), F32)
     v_shape = jax.ShapeDtypeStruct((order, 2 * cols), BF16)
     keep, send, *state = pl.pallas_call(

time: 47 us -> 47.1 us (level)
  waiting for transfers between devices: 11 us -> 9.44 us
  local copies, waits for them, and re-layouts: 1.45 us -> 2.4 us
  starting transfers between devices: 16.4 us -> 17.2 us
    ppermute x13 -> x14, waiting for transfers between devices: 11 us -> 9.44 us  [exchange(): return lax.ppermute(block, axes, [(i, i ^ offset) for i in range(count)])]
    concatenate x1, local copies, waits for them, and re-layouts: 0.03 us -> 0.98 us  [gathered_body(): jnp.concatenate([h.transpose(0, 2, 1, 3).reshape(local, block, count * bl...]
    ppermute x13 -> x14, starting transfers between devices: 16.4 us -> 17.2 us  [exchange(): return lax.ppermute(block, axes, [(i, i ^ offset) for i in range(count)])]
    unnamed x5 -> x3, local copies, waits for them, and re-layouts: 0.99 us -> 0.98 us
  transfers between devices with their start and end apart: 13 -> 14, of which waited for: 6 -> 6; matrix products, arithmetic and copies ran while one was open for 3% -> 5% of each run, Pallas kernels for 17% -> 17%
where the time goes in v9:
time: 47.1 us; the launch traced here: 46.9 us
  starting transfers between devices  17.2 us (37%)
  Pallas kernels  15.1 us (32%)
  waiting for transfers between devices  9.44 us (20%)
  other arithmetic  2.55 us (5%)
  local copies, waits for them, and re-layouts  2.4 us (5%)
    ppermute x14, starting transfers between devices, exchange(): return lax.ppermute(block, axes, [(i, i ^ offset) for i in range(count)])  17.2 us
    ppermute x14, waiting for transfers between devices, exchange(): return lax.ppermute(block, axes, [(i, i ^ offset) for i in range(count)])  9.44 us
    pallas_call x1, Pallas kernels, gathered_body(): pl.pallas_call(functools.partial(main_kernel, dims), out_shape=(block_sha...  7.1 us
    pallas_call x1, Pallas kernels, gathered_body(): pl.pallas_call(functools.partial(powers_kernel, dims), out_shape=(half_sh...  4.18 us
    pallas_call x1, Pallas kernels, gathered_body(): pl.pallas_call(functools.partial(own_kernel, dims), out_shape=block_shape...  3.05 us
    unnamed x3, local copies, waits for them, and re-layouts  0.98 us
    concatenate x1, local copies, waits for them, and re-layouts, gathered_body(): jnp.concatenate([h.transpose(0, 2, 1, 3).reshape(local, block, count * bl...  0.98 us
    select_n x1, other arithmetic, pick(): jnp.where(lax.axis_index('runs') == 0, lax.dynamic_slice_in_dim(first, at...  0.95 us
  transfers between devices with their start and end apart: 14, of which 6 were waited for; matrix products, arithmetic and copies ran while one was open for 5% of the time, Pallas kernels for 17%

profile of v9, /device:TPU:0, one launch (start us, length us, event | category | flops | bytes accessed | tf_op | source)
XLA Modules:
  0.0 46.9 jit_solution(11737969946361634887)
XLA Ops:
  0.0 0.7 %fusion.5 = (s32[2,4]{1,0:T(2,128)S(1)}, bf16[2,4]{1,0:T(2,128)(2,1)S(1)}) fusion(s32[2,4]{1,0:T(2,128)} %param.7), kind=kLoop, calls=%fused_computation.23 | loop fusion | flops 16 | bytes 80 | tf_op jit(solution)/shard_map/reshape | solution.py:367
  0.7 1.0 %dynamic-slice_select_fusion = (bf16[2,128,128]{2,1,0:T(8,128)(2,1)S(1)}, bf16[2,128,128]{2,1,0:T(8,128)(2,1)S(1)}) fusion(bf16[8,128,128]{2,1,0:T(8,128)(2,1)} %bitcast.50, s32[]{:T(128)S(6)} %select_n.23, bf16[8,128,128]{2,1,0:T(8,128)(2,1)} %bitcast.49, pred[]{:T(512)S(6)} %eq.4, s32[]{:T(128)S(6)} %select_n.21), kind=kLoop, calls=%fused_computation.18 | loop fusion | flops 65536 | bytes 393225 | tf_op jit(solution)/shard_map/jit(_where)/select_n | solution.py:353
  1.7 5.1 %collective-permute-start.2 = (bf16[272,128]{1,0:T(8,128)(2,1)S(1)}, bf16[272,128]{1,0:T(8,128)(2,1)S(1)}, u32[]{:S(2)}, u32[]{:S(2)}) collective-permute-start(bf16[272,128]{1,0:T(8,128)(2,1)S(1)} %fusion.4), channel_id=1, source_target_pairs={{0,12},{4,8},{8,4},{12,0},{1,13},{5,9},{9,5},{13,1},{2,14},{6,10},... | collective-permute-start | bytes 208904 | tf_op jit(solution)/shard_map/ppermute | solution.py:111
  6.8 0.0 collective-permute-start.1
  6.8 0.6 %collective-permute-start = (bf16[272,128]{1,0:T(8,128)(2,1)S(1)}, bf16[272,128]{1,0:T(8,128)(2,1)S(1)}, u32[]{:S(2)}, u32[]{:S(2)}) collective-permute-start(bf16[272,128]{1,0:T(8,128)(2,1)S(1)} %fusion.4), channel_id=1, source_target_pairs={{0,4},{4,0},{8,12},{12,8},{1,5},{5,1},{9,13},{13,9},{2,6},{6,2},{1... | collective-permute-start | bytes 208904 | tf_op jit(solution)/shard_map/ppermute | solution.py:111
  7.4 1.4 %collective-permute-start.5 = (bf16[256,128]{1,0:T(8,128)(2,1)S(1)}, bf16[256,128]{1,0:T(8,128)(2,1)S(1)}, u32[]{:S(2)}, u32[]{:S(2)}) collective-permute-start(bf16[256,128]{1,0:T(8,128)(2,1)S(1)} %bitcast.54), channel_id=1, source_target_pairs={{0,4},{4,0},{8,12},{12,8},{1,5},{5,1},{9,13},{13,9},{2,6},{6,2},{1... | collective-permute-start | bytes 196616 | tf_op jit(solution)/shard_map/ppermute | solution.py:111
  8.8 0.7 %collective-permute-start.11 = (bf16[256,256]{1,0:T(8,128)(2,1)}, bf16[256,256]{1,0:T(8,128)(2,1)S(1)}, u32[]{:S(2)}, u32[]{:S(2)}) collective-permute-start(bf16[256,256]{1,0:T(8,128)(2,1)} %bitcast.45), channel_id=1, source_target_pairs={{0,4},{4,0},{8,12},{12,8},{1,5},{5,1},{9,13},{13,9},{2,6},{6,2},{1... | collective-permute-start | bytes 393224 | tf_op jit(solution)/shard_map/ppermute | solution.py:111
  9.5 1.0 %bitcast_dynamic-update-slice_fusion.1 = bf16[2,256,512]{2,1,0:T(8,128)(2,1)S(1)} fusion(bf16[2,4,128,128]{3,2,1,0:T(8,128)(2,1)} %param.6), kind=kLoop, calls=%fused_computation.2 | loop fusion | bytes 524288
  10.4 0.0 collective-permute-done.2
  10.5 2.3 %collective-permute-done.1 = bf16[272,128]{1,0:T(8,128)(2,1)S(1)} collective-permute-done((bf16[272,128]{1,0:T(8,128)(2,1)S(1)}, bf16[272,128]{1,0:T(8,128)(2,1)S(1)}, u32[]{:S(2)}, u32[]{:S(2)}) %collective-permute-start.1) | collective-permute-done | bytes 69664 | tf_op jit(solution)/shard_map/ppermute | solution.py:111
  12.8 0.4 collective-permute-done
  13.2 1.7 %collective-permute-start.4 = (bf16[3,256,128]{2,1,0:T(8,128)(2,1)S(1)}, bf16[3,256,128]{2,1,0:T(8,128)(2,1)S(1)}, u32[]{:S(2)}, u32[]{:S(2)}) collective-permute-start(bf16[3,256,128]{2,1,0:T(8,128)(2,1)S(1)} %pad_maximum_fusion.1.first_ref), channel_id=1, source_target_pairs={{0,16},{2,18},{16,0},{18,2},{1,17},{3,19},{17,1},{19,3},{4,20},{6,... | collective-permute-start | bytes 589832 | tf_op jit(solution)/shard_map/ppermute | solution.py:111
  15.0 1.5 %collective-permute-start.3 = (bf16[3,256,128]{2,1,0:T(8,128)(2,1)S(1)}, bf16[3,256,128]{2,1,0:T(8,128)(2,1)S(1)}, u32[]{:S(2)}, u32[]{:S(2)}) collective-permute-start(bf16[3,256,128]{2,1,0:T(8,128)(2,1)S(1)} %pad_maximum_fusion.1.first_ref), channel_id=1, source_target_pairs={{0,2},{2,0},{16,18},{18,16},{1,3},{3,1},{17,19},{19,17},{4,6},{6,4... | collective-permute-start | bytes 589832 | tf_op jit(solution)/shard_map/ppermute | solution.py:111
  16.5 0.3 collective-permute-start.6
  16.8 1.0 %bitcast_dynamic-update-slice_fusion.mine_ref = bf16[2,256,512]{2,1,0:T(8,128)(2,1)S(1)} fusion(bf16[2,256,512]{2,1,0:T(8,128)(2,1)S(1)} %bitcast_dynamic-update-slice_fusion.1, bf16[2,4,128,128]{3,2,1,0:T(8,128)(2,1)} %param.5), kind=kLoop, calls=%fused_computation.1 | loop fusion | bytes 524288 | tf_op jit(solution)/shard_map/concatenate | solution.py:363
  17.8 0.1 reshape.65
  17.9 0.0 collective-permute-done.5
  17.9 1.6 %collective-permute-start.10 = (bf16[256,256]{1,0:T(8,128)(2,1)}, bf16[256,256]{1,0:T(8,128)(2,1)S(1)}, u32[]{:S(2)}, u32[]{:S(2)}) collective-permute-start(bf16[256,256]{1,0:T(8,128)(2,1)} %bitcast.46), channel_id=1, source_target_pairs={{0,8},{4,12},{8,0},{12,4},{1,9},{5,13},{9,1},{13,5},{2,10},{6,14},... | collective-permute-start | bytes 393224 | tf_op jit(solution)/shard_map/ppermute | solution.py:111
  19.4 3.8 %collective-permute-done.6 = bf16[2,256,128]{2,1,0:T(8,128)(2,1)S(1)} collective-permute-done((bf16[2,256,128]{2,1,0:T(8,128)(2,1)S(1)}, bf16[2,256,128]{2,1,0:T(8,128)(2,1)S(1)}, u32[]{:S(2)}, u32[]{:S(2)}) %collective-permute-start.6) | collective-permute-done | bytes 131104 | tf_op jit(solution)/shard_map/ppermute | solution.py:111
  23.3 1.6 %collective-permute-start.9 = (bf16[256,256]{1,0:T(8,128)(2,1)}, bf16[256,256]{1,0:T(8,128)(2,1)S(1)}, u32[]{:S(2)}, u32[]{:S(2)}) collective-permute-start(bf16[256,256]{1,0:T(8,128)(2,1)} %bitcast.47), channel_id=1, source_target_pairs={{0,12},{4,8},{8,4},{12,0},{1,13},{5,9},{9,5},{13,1},{2,14},{6,10},... | collective-permute-start | bytes 393224 | tf_op jit(solution)/shard_map/ppermute | solution.py:111
  24.9 0.0 collective-permute-done.4
  24.9 0.1 collective-permute-start.7
  25.0 0.0 collective-permute-done.3
  25.0 0.1 pad_maximum_fusion.near_ref
  25.1 0.5 %collective-permute-start.8 = (bf16[3,3,256,128]{3,2,1,0:T(8,128)(2,1)S(1)}, bf16[3,3,256,128]{3,2,1,0:T(8,128)(2,1)S(1)}, u32[]{:S(2)}, u32[]{:S(2)}) collective-permute-start(bf16[3,3,256,128]{3,2,1,0:T(8,128)(2,1)S(1)} %pad_maximum_fusion.near_ref), channel_id=1, source_target_pairs={{0,1},{1,0},{2,3},{3,2},{4,5},{5,4},{6,7},{7,6},{8,9},{9,8},{10,11... | collective-permute-start | bytes 1769480 | tf_op jit(solution)/shard_map/ppermute | solution.py:111
  25.7 0.1 reshape.71
  25.7 0.1 reshape.69
  25.8 0.1 reshape.67
  25.9 0.1 concatenate.13.facts
  26.0 0.8 %near.1 = (bf16[8,256,256]{2,1,0:T(8,128)(2,1)S(1)}, bf16[1024,256]{1,0:T(8,128)(2,1)S(1)}) custom-call(s32[36]{0:T(128)S(1)} %concatenate.13.facts, bf16[2,256,512]{2,1,0:T(8,128)(2,1)S(1)} %bitcast_dynamic-update-slice_fusion.mine_ref, bf16[3,256,128]{2,1,0:T(8,128)(2,1)S(1)} %pad_maximum_fusion.1.first_ref, ...), custom_call_target="tpu_custom_call" | custom-call | bytes 1048576 | tf_op jit(solution)/shard_map/near/pallas_call | solution.py:378
  26.8 0.0 collective-permute-done.7.first_ref
  26.8 0.5 %collective-permute-done.8.far_ref = bf16[3,3,256,128]{3,2,1,0:T(8,128)(2,1)S(1)} collective-permute-done((bf16[3,3,256,128]{3,2,1,0:T(8,128)(2,1)S(1)}, bf16[3,3,256,128]{3,2,1,0:T(8,128)(2,1)S(1)}, u32[]{:S(2)}, u32[]{:S(2)}) %collective-permute-start.8) | collective-permute-done | bytes 589856 | tf_op jit(solution)/shard_map/ppermute | solution.py:111
  27.3 0.0 copy-start
  27.3 4.2 %powers.1 = (bf16[8,256,256]{2,1,0:T(8,128)(2,1)S(1)}, bf16[1024,1536]{1,0:T(8,128)(2,1)S(1)}) custom-call(s32[36]{0:T(128)S(1)} %concatenate.13.facts, bf16[2,256,512]{2,1,0:T(8,128)(2,1)S(1)} %bitcast_dynamic-update-slice_fusion.mine_ref, bf16[3,256,128]{2,1,0:T(8,128)(2,1)S(1)} %collective-permute-done.7.first_ref, ...), custom_call_target="tpu_custom_call" | custom-call | flops 2684354560 | bytes 1048576 | tf_op jit(solution)/shard_map/powers/pallas_call | solution.py:387
  31.5 0.0 collective-permute-done.11.refs_3_
  31.5 0.0 collective-permute-done.10.refs_2_
  31.5 0.0 collective-permute-done.9.refs_1_
  31.5 0.0 copy-done
  31.5 7.1 %main.1 = (f32[256,256]{1,0:T(8,128)S(1)}, bf16[2,256,256]{2,1,0:T(8,128)(2,1)S(1)}, bf16[1024,512]{1,0:T(8,128)(2,1)S(1)}, bf16[1024,512]{1,0:T(8,128)(2,1)S(1)...) custom-call(s32[36]{0:T(128)S(1)} %concatenate.13.facts, ...), custom_call_target="tpu_custom_call" | custom-call | flops 4294967296 | bytes 1048576 | tf_op jit(solution)/shard_map/main/pallas_call | solution.py:403
  38.6 0.4 collective-permute-start.12
  39.1 1.2 %collective-permute-done.12 = bf16[2,256,256]{2,1,0:T(8,128)(2,1)S(1)} collective-permute-done((bf16[2,256,256]{2,1,0:T(8,128)(2,1)S(1)}, bf16[2,256,256]{2,1,0:T(8,128)(2,1)S(1)}, u32[]{:S(2)}, u32[]{:S(2)}) %collective-permute-start.12) | collective-permute-done | bytes 262176 | tf_op jit(solution)/shard_map/ppermute | solution.py:111
  40.3 1.6 %collective-permute-start.13 = (bf16[256,256]{1,0:T(8,128)(2,1)S(1)}, bf16[256,256]{1,0:T(8,128)(2,1)S(1)}, u32[]{:S(2)}, u32[]{:S(2)}) collective-permute-start(bf16[256,256]{1,0:T(8,128)(2,1)S(1)} %fusion), channel_id=1, source_target_pairs={{0,2},{2,0},{1,3},{3,1},{4,6},{6,4},{5,7},{7,5},{8,10},{10,8},{9,1... | collective-permute-start | bytes 393224 | tf_op jit(solution)/shard_map/ppermute | solution.py:111
  41.8 3.0 %own.1 = f32[256,256]{1,0:T(8,128)S(1)} custom-call(s32[36]{0:T(128)S(1)} %concatenate.13.facts, bf16[8,256,256]{2,1,0:T(8,128)(2,1)S(1)} %get-tuple-element.17.near_h.refs_4_, bf16[8,256,256]{2,1,0:T(8,128)(2,1)S(1)} %get-tuple-element.19.refs_5_.far_h, bf16[1024,1536]{1,0:T(8,128)(2,1)S(1)} %get-tuple-element.20.refs_6_.c_ref, ...), custom_call_target="tpu_custom_call" | custom-call | flops 1073741824 | bytes 1048576 | tf_op jit(solution)/shard_map/own/pallas_call | solution.py:424
  44.9 1.2 %collective-permute-done.13 = bf16[256,256]{1,0:T(8,128)(2,1)S(1)} collective-permute-done((bf16[256,256]{1,0:T(8,128)(2,1)S(1)}, bf16[256,256]{1,0:T(8,128)(2,1)S(1)}, u32[]{:S(2)}, u32[]{:S(2)}) %collective-permute-start.13) | collective-permute-done | bytes 131104 | tf_op jit(solution)/shard_map/ppermute | solution.py:111
  46.1 0.8 %fusion.2 = f32[1,256,256]{2,1,0:T(8,128)} fusion(bf16[256,256]{1,0:T(8,128)(2,1)S(1)} %collective-permute-done.13, f32[256,256]{1,0:T(8,128)S(1)} %own.1, bf16[2,256,256]{2,1,0:T(8,128)(2,1)S(1)} %collective-permute-done.12, bf16[1,256,256]{2,1,0:T(8,128)(2,1)S(1)} %copy-done), kind=kLoop, calls=%fused_computation.7 | loop fusion | flops 393216 | bytes 917504 | tf_op jit(solution)/shard_map/broadcast_in_dim | solution.py:435
  (11 shorter events, 0.1 us)
Async XLA Ops:
  1.7 8.8 %collective-permute-start.2 = (bf16[272,128]{1,0:T(8,128)(2,1)S(1)}, bf16[272,128]{1,0:T(8,128)(2,1)S(1)}, u32[]{:S(2)}, u32[]{:S(2)}) collective-permute-start(bf16[272,128]{1,0:T(8,128)(2,1)S(1)} %fusion.4), channel_id=1, source_target_pairs={{0,12},{4,8},{8,4},{12,0},{1,13},{5,9},{9,5},{13,1},{2,14},{6,10},... | collective-permute-start | bytes 208904 | tf_op jit(solution)/shard_map/ppermute | solution.py:111
  6.8 6.0 %collective-permute-start.1 = (bf16[272,128]{1,0:T(8,128)(2,1)S(1)}, bf16[272,128]{1,0:T(8,128)(2,1)S(1)}, u32[]{:S(2)}, u32[]{:S(2)}) collective-permute-start(bf16[272,128]{1,0:T(8,128)(2,1)S(1)} %fusion.4), channel_id=1, source_target_pairs={{0,8},{4,12},{8,0},{12,4},{1,9},{5,13},{9,1},{13,5},{2,10},{6,14},... | collective-permute-start | bytes 208904 | tf_op jit(solution)/shard_map/ppermute | solution.py:111
  6.8 6.4 %collective-permute-start = (bf16[272,128]{1,0:T(8,128)(2,1)S(1)}, bf16[272,128]{1,0:T(8,128)(2,1)S(1)}, u32[]{:S(2)}, u32[]{:S(2)}) collective-permute-start(bf16[272,128]{1,0:T(8,128)(2,1)S(1)} %fusion.4), channel_id=1, source_target_pairs={{0,4},{4,0},{8,12},{12,8},{1,5},{5,1},{9,13},{13,9},{2,6},{6,2},{1... | collective-permute-start | bytes 208904 | tf_op jit(solution)/shard_map/ppermute | solution.py:111
  7.4 10.5 %collective-permute-start.5 = (bf16[256,128]{1,0:T(8,128)(2,1)S(1)}, bf16[256,128]{1,0:T(8,128)(2,1)S(1)}, u32[]{:S(2)}, u32[]{:S(2)}) collective-permute-start(bf16[256,128]{1,0:T(8,128)(2,1)S(1)} %bitcast.54), channel_id=1, source_target_pairs={{0,4},{4,0},{8,12},{12,8},{1,5},{5,1},{9,13},{13,9},{2,6},{6,2},{1... | collective-permute-start | bytes 196616 | tf_op jit(solution)/shard_map/ppermute | solution.py:111
  8.8 22.7 %collective-permute-start.11 = (bf16[256,256]{1,0:T(8,128)(2,1)}, bf16[256,256]{1,0:T(8,128)(2,1)S(1)}, u32[]{:S(2)}, u32[]{:S(2)}) collective-permute-start(bf16[256,256]{1,0:T(8,128)(2,1)} %bitcast.45), channel_id=1, source_target_pairs={{0,4},{4,0},{8,12},{12,8},{1,5},{5,1},{9,13},{13,9},{2,6},{6,2},{1... | collective-permute-start | bytes 393224 | tf_op jit(solution)/shard_map/ppermute | solution.py:111
  13.2 11.7 %collective-permute-start.4 = (bf16[3,256,128]{2,1,0:T(8,128)(2,1)S(1)}, bf16[3,256,128]{2,1,0:T(8,128)(2,1)S(1)}, u32[]{:S(2)}, u32[]{:S(2)}) collective-permute-start(bf16[3,256,128]{2,1,0:T(8,128)(2,1)S(1)} %pad_maximum_fusion.1.first_ref), channel_id=1, source_target_pairs={{0,16},{2,18},{16,0},{18,2},{1,17},{3,19},{17,1},{19,3},{4,20},{6,... | collective-permute-start | bytes 589832 | tf_op jit(solution)/shard_map/ppermute | solution.py:111
  15.0 10.1 %collective-permute-start.3 = (bf16[3,256,128]{2,1,0:T(8,128)(2,1)S(1)}, bf16[3,256,128]{2,1,0:T(8,128)(2,1)S(1)}, u32[]{:S(2)}, u32[]{:S(2)}) collective-permute-start(bf16[3,256,128]{2,1,0:T(8,128)(2,1)S(1)} %pad_maximum_fusion.1.first_ref), channel_id=1, source_target_pairs={{0,2},{2,0},{16,18},{18,16},{1,3},{3,1},{17,19},{19,17},{4,6},{6,4... | collective-permute-start | bytes 589832 | tf_op jit(solution)/shard_map/ppermute | solution.py:111
  16.5 6.8 %collective-permute-start.6 = (bf16[2,256,128]{2,1,0:T(8,128)(2,1)S(1)}, bf16[2,256,128]{2,1,0:T(8,128)(2,1)S(1)}, u32[]{:S(2)}, u32[]{:S(2)}) collective-permute-start(bf16[2,256,128]{2,1,0:T(8,128)(2,1)S(1)} %slice.43), channel_id=1, source_target_pairs={{0,18},{2,16},{16,2},{18,0},{1,19},{3,17},{17,3},{19,1},{4,22},{6,... | collective-permute-start | bytes 393224 | tf_op jit(solution)/shard_map/ppermute | solution.py:111
  17.9 13.6 %collective-permute-start.10 = (bf16[256,256]{1,0:T(8,128)(2,1)}, bf16[256,256]{1,0:T(8,128)(2,1)S(1)}, u32[]{:S(2)}, u32[]{:S(2)}) collective-permute-start(bf16[256,256]{1,0:T(8,128)(2,1)} %bitcast.46), channel_id=1, source_target_pairs={{0,8},{4,12},{8,0},{12,4},{1,9},{5,13},{9,1},{13,5},{2,10},{6,14},... | collective-permute-start | bytes 393224 | tf_op jit(solution)/shard_map/ppermute | solution.py:111
  23.3 8.2 %collective-permute-start.9 = (bf16[256,256]{1,0:T(8,128)(2,1)}, bf16[256,256]{1,0:T(8,128)(2,1)S(1)}, u32[]{:S(2)}, u32[]{:S(2)}) collective-permute-start(bf16[256,256]{1,0:T(8,128)(2,1)} %bitcast.47), channel_id=1, source_target_pairs={{0,12},{4,8},{8,4},{12,0},{1,13},{5,9},{9,5},{13,1},{2,14},{6,10},... | collective-permute-start | bytes 393224 | tf_op jit(solution)/shard_map/ppermute | solution.py:111
  24.9 1.9 %collective-permute-start.7 = (bf16[3,256,128]{2,1,0:T(8,128)(2,1)S(1)}, bf16[3,256,128]{2,1,0:T(8,128)(2,1)S(1)}, u32[]{:S(2)}, u32[]{:S(2)}) collective-permute-start(bf16[3,256,128]{2,1,0:T(8,128)(2,1)S(1)} %pad_maximum_fusion.1.first_ref), channel_id=1, source_target_pairs={{0,1},{1,0},{2,3},{3,2},{4,5},{5,4},{6,7},{7,6},{8,9},{9,8},{10,11... | collective-permute-start | bytes 589832 | tf_op jit(solution)/shard_map/ppermute | solution.py:111
  25.1 2.2 %collective-permute-start.8 = (bf16[3,3,256,128]{3,2,1,0:T(8,128)(2,1)S(1)}, bf16[3,3,256,128]{3,2,1,0:T(8,128)(2,1)S(1)}, u32[]{:S(2)}, u32[]{:S(2)}) collective-permute-start(bf16[3,3,256,128]{3,2,1,0:T(8,128)(2,1)S(1)} %pad_maximum_fusion.near_ref), channel_id=1, source_target_pairs={{0,1},{1,0},{2,3},{3,2},{4,5},{5,4},{6,7},{7,6},{8,9},{9,8},{10,11... | collective-permute-start | bytes 1769480 | tf_op jit(solution)/shard_map/ppermute | solution.py:111
  27.3 4.2 %copy-start = (bf16[1,256,256]{2,1,0:T(8,128)(2,1)S(1)}, bf16[1,256,256]{2,1,0:T(8,128)(2,1)}, u32[]{:S(2)}) copy-start(bf16[1,256,256]{2,1,0:T(8,128)(2,1)} %param.4) | copy-start | bytes 393220
  38.6 1.6 %collective-permute-start.12 = (bf16[2,256,256]{2,1,0:T(8,128)(2,1)S(1)}, bf16[2,256,256]{2,1,0:T(8,128)(2,1)S(1)}, u32[]{:S(2)}, u32[]{:S(2)}) collective-permute-start(bf16[2,256,256]{2,1,0:T(8,128)(2,1)S(1)} %get-tuple-element.27), channel_id=1, source_target_pairs={{0,1},{1,0},{2,3},{3,2},{4,5},{5,4},{6,7},{7,6},{8,9},{9,8},{10,11... | collective-permute-start | bytes 786440 | tf_op jit(solution)/shard_map/ppermute | solution.py:111
  40.3 5.8 %collective-permute-start.13 = (bf16[256,256]{1,0:T(8,128)(2,1)S(1)}, bf16[256,256]{1,0:T(8,128)(2,1)S(1)}, u32[]{:S(2)}, u32[]{:S(2)}) collective-permute-start(bf16[256,256]{1,0:T(8,128)(2,1)S(1)} %fusion), channel_id=1, source_target_pairs={{0,2},{2,0},{1,3},{3,1},{4,6},{6,4},{5,7},{7,5},{8,10},{10,8},{9,1... | collective-permute-start | bytes 393224 | tf_op jit(solution)/shard_map/ppermute | solution.py:111
